TPU v7x, 32 devices: a whole 2x2x4 slice. The times are simulated.
32 devices in a mesh: ax: 8 (over z, y), az: 4 (over x, core).
Axes of the slice: x: 2, y: 2, z: 4, core: 2. Of those that a mesh axis runs over, the one named last changes fastest.
Arguments:
- lamb_vector: bfloat16 [8192, 3, 512], P(('ax', 'az')), may hold values from -6 to 6
- owner: int32 [8192, 1], P(('ax', 'az')), may hold values from 0 to 31; in each aligned block of 256 rows (0 to 255, 256 to 511, ...) at most 24 rows name the same one
- element: int32 [8192], P(('ax', 'az')), may hold values from 0 to 1023
- shape_class: int32 [8192], P(('ax', 'az')), may hold values from 0 to 1
- interp_tables: bfloat16 [2, 512, 125], replicated, may hold values from -0.25 to 0.25
- acoustic_state: float32 [5, 125, 16, 16, 128], P(None, None, 'ax', 'az'), may hold values from -6 to 6
Outputs:
- new_state: float32 [5, 125, 16, 16, 128], P(None, None, 'ax', 'az')
- source: float32 [3, 125, 16, 16, 128], P(None, None, 'ax', 'az')
Inputs may be any that keep to these rules, and one draw needn't show every extreme that they name: `owner`: among one device's 256 flow elements no device is named by more than 24 of them, and some device is named by exactly 24.
All inputs are finite; a program needn't handle non-finite values.
Results may differ from a plain program's by a relative error of at most 0.0013.
Values may be sent and summed in bfloat16 or wider, within the bound.
No kernel may reach another device: no remote copies, remote signals or barrier semaphores. Data moves between devices by JAX's collectives and lax.ppermute only.
A program may use at most 128 MiB of HBM per device.

v0:
```python
import functools
import math

import jax
import jax.numpy as jnp
import numpy as np
from jax import lax
from jax.experimental import pallas as pl
from jax.experimental.pallas import tpu as pltpu
from jax.sharding import PartitionSpec as P

MACH = 0.3
RUSANOV = 1.3
DT = 0.03
LIFT = 10.0
VOLUME = 2.0
STEP_SCALES = (DT, DT / 2.0, DT / 3.0, DT / 4.0)

FIELDS = 5
NODES = 125
ROWS = 8
LANES = 128
VMEM_BYTES = 24 * 1024 * 1024


def derivative_matrix():
    points = np.array([-1.0, -math.sqrt(3.0 / 7.0), 0.0, math.sqrt(3.0 / 7.0), 1.0])
    weights = [1.0 / np.prod([points[j] - points[k] for k in range(5) if k != j]) for j in range(5)]
    matrix = np.zeros((5, 5))
    for i in range(5):
        for j in range(5):
            if i != j:
                matrix[i, j] = weights[j] / weights[i] / (points[i] - points[j])
        matrix[i, i] = -np.sum(matrix[i])
    return matrix


DERIVATIVE = -VOLUME * derivative_matrix()


def differentiate(g, scale):
    d = [[float(scale * v) for v in row] for row in DERIVATIVE]
    even_out, odd_out = g[0] - g[4], g[1] - g[3]
    s_out, s_in = g[0] + g[4], g[1] + g[3]
    results = [None] * 5
    for i in (0, 1):
        same = (d[i][0] - d[i][4]) / 2 * even_out + (d[i][1] - d[i][3]) / 2 * odd_out
        flip = (d[i][0] + d[i][4]) / 2 * s_out + (d[i][1] + d[i][3]) / 2 * s_in + d[i][2] * g[2]
        results[i] = same + flip
        results[4 - i] = same - flip
    results[2] = d[2][0] * even_out + d[2][1] * odd_out
    return results


def flux(q, direction):
    p, u, v, w, rho = q
    pressure = p + MACH * u
    if direction == 0:
        return [MACH * p + u, pressure, None, None, MACH * rho + u]
    if direction == 1:
        return [v, None, pressure, None, v]
    return [w, None, None, pressure, w]


def lifted(q, direction, normal, rusanov_sign):
    result = []
    for value, flow in zip(q, flux(q, direction)):
        term = (LIFT * RUSANOV * rusanov_sign) * value
        if flow is not None:
            term = term + (LIFT * normal) * flow
        result.append(term)
    return result


def coupled(jump, direction, normal, scale):
    p, u, v, w, rho = jump
    rusanov, lift = scale * LIFT * RUSANOV, scale * LIFT * normal
    if direction == 0:
        own = lift * MACH - rusanov
        if abs(own + lift) < 1e-9:
            across = lift * (u - p)
            return [across, -across, -rusanov * v, -rusanov * w, lift * (u - rho)]
        across = lift * u
        return [
            own * p + across,
            lift * p + own * u,
            -rusanov * v,
            -rusanov * w,
            own * rho + across,
        ]
    normal_velocity = (v, w)[direction - 1]
    across = lift * normal_velocity
    along = lift * p + (lift * MACH) * u - rusanov * normal_velocity
    return [
        across - rusanov * p,
        -rusanov * u,
        along if direction == 1 else -rusanov * v,
        along if direction == 2 else -rusanov * w,
        across - rusanov * rho,
    ]


def shifted(q, amount, axis, keep):
    return [jnp.where(keep, pltpu.roll(value, amount, axis), 0.0) for value in q]


def volume_into(state_ref, scale, store):
    row = lax.broadcasted_iota(jnp.int32, (ROWS, LANES), 0)
    lane = lax.broadcasted_iota(jnp.int32, (ROWS, LANES), 1)
    cell = row % 4
    keep = {
        0: (row >= 4, row < 4),
        1: (cell != 0, cell != 3),
        2: (lane != 0, lane != LANES - 1),
    }
    rolls = {0: (4, 4, 0), 1: (1, ROWS - 1, 0), 2: (1, LANES - 1, 1)}

    def load(field, node):
        return state_ref[field * NODES + node]

    def face_terms(direction, low, high):
        up, down, axis = rolls[direction]
        keep_low, keep_high = keep[direction]
        if direction == 0:
            turned = [pltpu.roll(jnp.where(keep_high, b, a), up, axis) for a, b in zip(low, high)]
            below = [jnp.where(keep_low, value, 0.0) for value in turned]
            above = [jnp.where(keep_high, value, 0.0) for value in turned]
        else:
            below = shifted(high, up, axis, keep_low)
            above = shifted(low, down, axis, keep_high)
        jump_low = [a - b for a, b in zip(low, below)]
        jump_high = [a - b for a, b in zip(high, above)]
        return coupled(jump_low, direction, -1.0, scale), coupled(jump_high, direction, 1.0, scale)

    def line(direction, nodes):
        q = [[load(f, n) for n in nodes] for f in range(FIELDS)]
        ends = face_terms(direction, [x[0] for x in q], [x[4] for x in q])
        if direction == 0:
            parts = {
                0: differentiate([MACH * q[0][k] + q[1][k] for k in range(5)], scale),
                1: differentiate([MACH * q[1][k] + q[0][k] for k in range(5)], scale),
                4: differentiate([MACH * q[4][k] + q[1][k] for k in range(5)], scale),
            }
        else:
            along = differentiate(q[direction + 1], scale)
            parts = {
                0: along,
                direction + 1: differentiate([MACH * q[1][k] + q[0][k] for k in range(5)], scale),
                4: along,
            }
        for f in range(FIELDS):
            for k in range(5):
                value = parts[f][k] if f in parts else None
                if k in (0, 4):
                    end = ends[0 if k == 0 else 1][f]
                    value = end if value is None else value + end
                store(direction, f, nodes[k], value, q[f][k])

    @pl.loop(0, 5)
    def _(outer):
        for inner in range(5):
            line(0, [k * 25 + outer * 5 + inner for k in range(5)])

    @pl.loop(0, 5)
    def _(outer):
        for inner in range(5):
            line(1, [outer * 25 + k * 5 + inner for k in range(5)])

    @pl.loop(0, 5)
    def _(outer):
        for inner in range(5):
            line(2, [outer * 25 + inner * 5 + k for k in range(5)])


def volume_first_kernel(scale, state_ref, out_ref):
    volume_into(state_ref, scale, add_to(out_ref))


def add_to(out_ref):
    def store(direction, field, node, value, q):
        at = field * NODES + node
        if direction == 0:
            out_ref[at] = jnp.zeros_like(q) if value is None else value
        elif value is not None:
            out_ref[at] += value

    return store


def volume_kernel(scale, state_ref, sum_in, out_ref, sum_ref):
    add = add_to(out_ref)

    def store(direction, field, node, value, q):
        add(direction, field, node, value, q)
        if direction == 2:
            at = field * NODES + node
            sum_ref[at] = sum_in[at] + q

    volume_into(state_ref, scale, store)


def volume_and_source_kernel(
    scale, state_ref, sum_in, source_ref, out_ref, sum_ref, out_hbm, sem
):
    copy = pltpu.make_async_copy(source_ref, out_hbm, sem.at[0])
    copy.start()
    volume_kernel(scale, state_ref, sum_in, out_ref, sum_ref)
    copy.wait()


def volume_last_kernel(scale, state_ref, sum_in, sum_ref, out_ref):
    add = add_to(out_ref)

    def store(direction, field, node, value, q):
        if direction < 2:
            add(direction, field, node, value, q)
        else:
            at = field * NODES + node
            total = sum_in[at] + q + out_ref[at]
            sum_ref[at] = total if value is None else total + value

    volume_into(state_ref, scale, store)


def on_parity(axis, even, odd):
    parity = lax.axis_index(axis) % 2
    pl.when(parity == 0)(even)
    pl.when(parity == 1)(odd)


def piece(face, row):
    if not isinstance(face, (tuple, list)):
        return face, pl.ds(row, 5)
    first = face[0].shape[0]
    return (face[0], pl.ds(row, 5)) if row < first else (face[1], pl.ds(row - first, 5))


def received(face, start):
    parts = [piece(face, f * 25 + start) for f in range(FIELDS)]
    return [ref[rows].astype(jnp.float32) for ref, rows in parts]


def add_ax(out_ref, face, high, weight):
    sign = -weight if high else weight
    first, rows = (100, slice(4, 8)) if high else (0, slice(0, 4))
    for chunk in range(5):
        terms = lifted(received(face, chunk * 5), 0, sign, weight)
        for f, term in enumerate(terms):
            out_ref[pl.ds(f * NODES + first + chunk * 5, 5), rows, :] += term


def add_far(out_ref, face, weight):
    on_parity(
        "ax",
        lambda: add_ax(out_ref, face, False, weight),
        lambda: add_ax(out_ref, face, True, weight),
    )


def add_near(out_ref, face, weight):
    on_parity(
        "ax",
        lambda: add_ax(out_ref, face, True, weight),
        lambda: add_ax(out_ref, face, False, weight),
    )


def add_az(out_ref, far, near, weight):
    def add(low, high):
        for a in range(5):
            at = a * 25
            for f, term in enumerate(lifted(received(low, a * 5), 1, weight, weight)):
                out_ref[pl.ds(f * NODES + at, 5), 0:1, :] += term[:, 0:1]
                out_ref[pl.ds(f * NODES + at, 5), 4:5, :] += term[:, 1:2]
            for f, term in enumerate(lifted(received(high, a * 5), 1, -weight, weight)):
                out_ref[pl.ds(f * NODES + at + 20, 5), 3:4, :] += term[:, 0:1]
                out_ref[pl.ds(f * NODES + at + 20, 5), 7:8, :] += term[:, 1:2]

    on_parity("az", lambda: add(far, near), lambda: add(near, far))


def pack_ax(state_ref, face, high):
    first, rows = (100, slice(4, 8)) if high else (0, slice(0, 4))
    for f in range(FIELDS):
        for at in range(0, 25, 5):
            ref, to = piece(face, f * 25 + at)
            ref[to] = state_ref[pl.ds(f * NODES + first + at, 5), rows, :].astype(jnp.bfloat16)


def pack_far(state_ref, face):
    on_parity("ax", lambda: pack_ax(state_ref, face, False), lambda: pack_ax(state_ref, face, True))


def pack_near(state_ref, face):
    on_parity("ax", lambda: pack_ax(state_ref, face, True), lambda: pack_ax(state_ref, face, False))


def pack_az(state_ref, far, near):
    def pack(az_low, az_high):
        for f in range(FIELDS):
            for a in range(5):
                at, to = f * NODES + a * 25, pl.ds((f * 5 + a) * 5, 5)
                low = [state_ref[pl.ds(at, 5), k : k + 1, :] for k in (0, 4)]
                high = [state_ref[pl.ds(at + 20, 5), k : k + 1, :] for k in (3, 7)]
                az_low[to] = jnp.concatenate(low, axis=1).astype(jnp.bfloat16)
                az_high[to] = jnp.concatenate(high, axis=1).astype(jnp.bfloat16)

    on_parity("az", lambda: pack(far, near), lambda: pack(near, far))


def load_kernel(state_hbm, state_ref, far, near_a, near_b, az_far, az_near, sems):
    copies = []
    for f in range(FIELDS):
        nodes = pl.ds(f * NODES, NODES)
        copy = pltpu.make_async_copy(state_hbm.at[nodes], state_ref.at[nodes], sems.at[f])
        copy.start()
        copies.append(copy)
    for copy in copies:
        copy.wait()
    pack_faces(state_ref, far, near_a, near_b, az_far, az_near)


def pack_faces(state_ref, far, near_a, near_b, az_far, az_near):
    pack_far(state_ref, far)
    pack_near(state_ref, (near_a, near_b))
    pack_az(state_ref, az_far, az_near)


def finish_first_kernel(
    scale, state_in, source_ref, far, near_a, near_b, az_far, az_near, state_ref, *faces
):
    add_far(state_ref, far, scale)
    add_near(state_ref, (near_a, near_b), scale)
    add_az(state_ref, az_far, az_near, scale)

    for node in range(3 * NODES):
        state_ref[NODES + node] += scale * source_ref[pl.ds(node * ROWS, ROWS), :]

    pack_faces(state_ref, *faces)


def finish_far_kernel(scale, state_in, far, az_far, az_near, state_ref, far_out):
    add_az(state_ref, az_far, az_near, scale)
    add_far(state_ref, far, scale)
    pack_far(state_ref, far_out)


def finish_near_kernel(
    scale, state_in, near_a, near_b, state_ref, near_a_out, near_b_out, az_far_out, az_near_out
):
    add_near(state_ref, (near_a, near_b), scale)
    pack_near(state_ref, (near_a_out, near_b_out))
    pack_az(state_ref, az_far_out, az_near_out)


def last_far_kernel(weight, state_in, far, az_far, az_near, state_ref, out_hbm, sems):
    add_az(state_ref, az_far, az_near, weight)
    add_far(state_ref, far, weight)
    first = 25 * (lax.axis_index("ax") % 2)
    copies = []
    for f in range(FIELDS):
        nodes = pl.ds(f * NODES + first, NODES - 25)
        copy = pltpu.make_async_copy(state_ref.at[nodes], out_hbm.at[nodes], sems.at[f])
        copy.start()
        copies.append(copy)
    for copy in copies:
        copy.wait()


def last_near_kernel(weight, state_in, out_in, near_a, near_b, state_ref, out_hbm, sems):
    add_near(state_ref, (near_a, near_b), weight)
    first = 100 - 100 * (lax.axis_index("ax") % 2)
    copies = []
    for f in range(FIELDS):
        nodes = pl.ds(f * NODES + first, 25)
        copy = pltpu.make_async_copy(state_ref.at[nodes], out_hbm.at[nodes], sems.at[f])
        copy.start()
        copies.append(copy)
    for copy in copies:
        copy.wait()


def contribution_kernel(
    capacity,
    devices,
    lamb_hbm,
    owner_hbm,
    element_hbm,
    class_hbm,
    tables_hbm,
    out_hbm,
    lamb_ref,
    owner_ref,
    rows_ref,
    tables_ref,
    out_ref,
    row_sems,
    tables_sem,
    lamb_sem,
    out_sems,
):
    flow = lamb_ref.shape[1]
    slots = devices * capacity
    row_copies = [
        pltpu.make_async_copy(owner_hbm, owner_ref, row_sems.at[0]),
        pltpu.make_async_copy(element_hbm, rows_ref.at[0], row_sems.at[1]),
        pltpu.make_async_copy(class_hbm, rows_ref.at[1], row_sems.at[2]),
    ]
    lamb_copy = pltpu.make_async_copy(lamb_hbm, lamb_ref, lamb_sem.at[0])
    tables_copy = pltpu.make_async_copy(tables_hbm, tables_ref, tables_sem.at[0])
    for copy in row_copies + [tables_copy, lamb_copy]:
        copy.start()
    for copy in row_copies:
        copy.wait()

    owner_row = owner_ref[...]
    rows = jnp.concatenate(
        [rows_ref[0], rows_ref[1], jnp.zeros((ROWS - 2, flow), jnp.int32)], axis=0
    )
    columns = jnp.transpose(rows.astype(jnp.float32))
    element = columns[:, 0:1]
    second = columns[:, 1:2]

    owned = (lax.broadcasted_iota(jnp.int32, (devices, flow), 0) == owner_row).astype(jnp.float32)
    earlier = lax.broadcasted_iota(jnp.int32, (flow, flow), 0) < lax.broadcasted_iota(
        jnp.int32, (flow, flow), 1
    )
    running = jnp.dot(
        owned.astype(jnp.bfloat16),
        earlier.astype(jnp.bfloat16),
        preferred_element_type=jnp.float32,
    )
    position = jnp.sum(running * owned, axis=0, keepdims=True).astype(jnp.int32)
    slot_row = owner_row * capacity + position
    placing = (lax.broadcasted_iota(jnp.int32, (slots, flow), 0) == slot_row).astype(jnp.bfloat16)

    tables_copy.wait()
    spare = jnp.zeros((LANES - NODES, lamb_ref.shape[2]), jnp.bfloat16)
    tables = jnp.concatenate([tables_ref[:, 0, :], spare, tables_ref[:, 1, :], spare], axis=0)
    lamb_copy.wait()
    both = lax.dot_general(
        lamb_ref[...].reshape(3 * flow, lamb_ref.shape[2]),
        tables,
        (((1,), (1,)), ((), ())),
        preferred_element_type=jnp.float32,
    )
    use_second = jnp.broadcast_to(second, (flow, LANES)) > 0.5
    values = [
        jnp.where(
            use_second, both[c * flow : (c + 1) * flow, LANES:], both[c * flow : (c + 1) * flow, :LANES]
        )
        for c in range(3)
    ]
    largest = jnp.maximum(jnp.maximum(jnp.abs(values[0]), jnp.abs(values[1])), jnp.abs(values[2]))
    largest = jnp.max(largest, axis=1, keepdims=True)
    exponent = jnp.clip(jnp.ceil(jnp.log2(jnp.maximum(largest, 1e-36))), -100.0, 30.0)
    scale = jnp.broadcast_to(jnp.exp2(14.0 - exponent), (flow, LANES))
    column = lax.broadcasted_iota(jnp.int32, (flow, LANES), 1)
    out_copies = []
    for c in range(3):
        whole = jnp.round(values[c] * scale)
        if c == 0:
            whole = jnp.where(column == NODES, exponent, whole)
            whole = jnp.where(column == NODES + 1, element, whole)
        high = jnp.floor(whole * (1.0 / 256.0))
        low = whole - 256.0 * high
        pieces = jnp.concatenate([high, low], axis=1).astype(jnp.bfloat16)
        placed = jnp.dot(placing, pieces, preferred_element_type=jnp.float32)
        placed = placed[:, :LANES] * 256.0 + placed[:, LANES:]
        out_ref[c] = placed.astype(jnp.int32).astype(jnp.int16)
        copy = pltpu.make_async_copy(
            out_ref.at[c], out_hbm.at[:, pl.ds(c * LANES, LANES)], out_sems.at[c]
        )
        copy.start()
        out_copies.append(copy)
    for copy in out_copies:
        copy.wait()


def source_kernel(received_ref, source_ref):
    slots = received_ref.shape[0]
    wide = 2 * LANES
    highs, lows = [], []
    for c in range(3):
        values = received_ref[:, pl.ds(c * LANES, LANES)].astype(jnp.int32).astype(jnp.float32)
        if c == 0:
            element = values[:, NODES + 1 : NODES + 2].astype(jnp.int32)
        values = jnp.transpose(values)
        if c == 0:
            scale = jnp.exp2(values[NODES : NODES + 1, :] - 14.0)
        values = values * scale
        high = values.astype(jnp.bfloat16)
        highs.append(high)
        lows.append((values - high.astype(jnp.float32)).astype(jnp.bfloat16))
    parts = jnp.concatenate(highs + lows, axis=0)
    column = lax.broadcasted_iota(jnp.int32, (slots, wide), 1)
    for group in range(ROWS // 2):
        member = (element == column + group * wide).astype(jnp.bfloat16)
        total = jnp.dot(parts, member, preferred_element_type=jnp.float32)
        total = total[0 : 3 * LANES] + total[3 * LANES :]
        for c in range(3):
            for k in range(2):
                start = c * NODES * ROWS + group * 2 + k
                source_ref[pl.ds(start, NODES, stride=ROWS), :] = total[
                    c * LANES : c * LANES + NODES, k * LANES : (k + 1) * LANES
                ]

STATE = (FIELDS * NODES, ROWS, LANES)
AX_FACE = (FIELDS * 25, 4, LANES)
NEAR_PIECES = ((65, 4, LANES), (60, 4, LANES))
AZ_FACE = (132, 2, LANES)


IN_VMEM = pl.BlockSpec(memory_space=pltpu.VMEM)
IN_HBM = pl.BlockSpec(memory_space=pltpu.HBM)


def in_hbm(x):
    return pltpu.with_memory_space_constraint(x, pltpu.HBM)


def call(kernel, out_shape, in_specs, out_specs=IN_VMEM, aliases=None, scratch=()):
    if not isinstance(out_specs, list):
        out_specs = jax.tree.map(lambda _: out_specs, out_shape)
    return pl.pallas_call(
        kernel,
        out_shape=out_shape,
        in_specs=in_specs if isinstance(in_specs, list) else [IN_VMEM] * in_specs,
        out_specs=out_specs,
        scratch_shapes=scratch,
        input_output_aliases=aliases or {},
        compiler_params=pltpu.CompilerParams(vmem_limit_bytes=VMEM_BYTES),
    )


def swap(far, near):
    count = lax.axis_size("ax")
    pairs = ([], [])
    for i in range(count - 1):
        pairs[i % 2].extend([(i, i + 1), (i + 1, i)])
    return (
        None if far is None else lax.ppermute(far, "ax", pairs[1]),
        None if near is None else [lax.ppermute(part, "ax", pairs[0]) for part in near],
    )


def turn(far, near):
    count = lax.axis_size("az")
    pairs = ([], [])
    for i in range(count):
        pairs[i % 2].extend([(i, (i + 1) % count), ((i + 1) % count, i)])
    return lax.ppermute(far, "az", pairs[1]), lax.ppermute(near, "az", pairs[0])


def body(lamb_vector, owner, element, shape_class, interp_tables, acoustic_state):
    devices = lax.axis_size("ax") * lax.axis_size("az")
    flow, _, points = lamb_vector.shape
    capacity = max(2, 3 * flow // devices)
    slots = devices * capacity
    f32, bf16 = jnp.float32, jnp.bfloat16

    state = acoustic_state.reshape(STATE)
    face_shapes = [jax.ShapeDtypeStruct(s, bf16) for s in (AX_FACE, *NEAR_PIECES, AZ_FACE, AZ_FACE)]
    vmem_state = pltpu.VMEM(STATE, f32)
    source_shape = (3 * NODES * ROWS, LANES)

    buffer = call(
        functools.partial(contribution_kernel, capacity, devices),
        pltpu.HBM((slots, 3 * LANES), jnp.int16),
        [IN_HBM] * 5,
        IN_HBM,
        scratch=[
            pltpu.VMEM((3, flow, points), bf16),
            pltpu.VMEM((1, flow), jnp.int32),
            pltpu.VMEM((2, 1, flow), jnp.int32),
            pltpu.VMEM((NODES, 2, points), bf16),
            pltpu.VMEM((3, slots, LANES), jnp.int16),
            pltpu.SemaphoreType.DMA((3,)),
            pltpu.SemaphoreType.DMA((1,)),
            pltpu.SemaphoreType.DMA((1,)),
            pltpu.SemaphoreType.DMA((3,)),
        ],
    )(
        in_hbm(jnp.transpose(lamb_vector, (1, 0, 2))),
        in_hbm(owner.reshape(1, flow)),
        in_hbm(element.reshape(1, flow)),
        in_hbm(shape_class.reshape(1, flow)),
        in_hbm(jnp.transpose(interp_tables, (2, 0, 1))),
    )
    routed = lax.all_to_all(buffer, ("ax", "az"), split_axis=0, concat_axis=0, tiled=True)

    state, far, *near, az_far, az_near = call(
        load_kernel,
        [vmem_state] + face_shapes,
        [IN_HBM],
        scratch=[pltpu.SemaphoreType.DMA((FIELDS,))],
    )(in_hbm(state))
    far, near = swap(far, near)
    az_far, az_near = turn(az_far, az_near)
    moved = call(functools.partial(volume_first_kernel, STEP_SCALES[0]), vmem_state, 1)(state)
    source = call(source_kernel, pltpu.VMEM(source_shape, f32), 1)(routed)
    rate, far, *near, az_far, az_near = call(
        functools.partial(finish_first_kernel, STEP_SCALES[0]),
        [vmem_state] + face_shapes,
        7,
        aliases={0: 0},
    )(moved, source, far, *near, az_far, az_near)
    far, near = swap(far, near)
    az_far, az_near = turn(az_far, az_near)
    moved, total, source = call(
        functools.partial(volume_and_source_kernel, STEP_SCALES[1]),
        [vmem_state, vmem_state, pltpu.HBM(source_shape, f32)],
        3,
        [IN_VMEM, IN_VMEM, IN_HBM],
        scratch=[pltpu.SemaphoreType.DMA((1,))],
    )(rate, state, source)

    for scale in STEP_SCALES[1:3]:
        rate, far = call(
            functools.partial(finish_far_kernel, scale),
            [vmem_state, face_shapes[0]],
            4,
            aliases={0: 0},
        )(moved, far, az_far, az_near)
        far, _ = swap(far, None)
        rate, *near, az_far, az_near = call(
            functools.partial(finish_near_kernel, scale),
            [vmem_state] + face_shapes[1:],
            3,
            aliases={0: 0},
        )(rate, *near)
        _, near = swap(None, near)
        az_far, az_near = turn(az_far, az_near)
        if scale == STEP_SCALES[1]:
            moved, total = call(
                functools.partial(volume_kernel, STEP_SCALES[2]), [vmem_state, vmem_state], 2
            )(rate, total)

    total = call(
        functools.partial(volume_last_kernel, STEP_SCALES[3]),
        vmem_state,
        2,
        scratch=[pltpu.VMEM(STATE, f32)],
    )(rate, total)
    hbm_state = pltpu.HBM(STATE, f32)
    total, partial = call(
        functools.partial(last_far_kernel, STEP_SCALES[3]),
        [vmem_state, hbm_state],
        4,
        [IN_VMEM, IN_HBM],
        aliases={0: 0},
        scratch=[pltpu.SemaphoreType.DMA((FIELDS,))],
    )(total, far, az_far, az_near)
    _, new_state = call(
        functools.partial(last_near_kernel, STEP_SCALES[3]),
        [vmem_state, hbm_state],
        [IN_VMEM, IN_HBM, IN_VMEM, IN_VMEM],
        [IN_VMEM, IN_HBM],
        aliases={0: 0, 1: 1},
        scratch=[pltpu.SemaphoreType.DMA((FIELDS,))],
    )(total, partial, *near)
    shape = acoustic_state.shape
    return new_state.reshape(shape), source.reshape((3,) + shape[1:])


def solution(mesh):
    in_specs = (
        P(("ax", "az"), None, None),
        P(("ax", "az"), None),
        P(("ax", "az")),
        P(("ax", "az")),
        P(),
        P(None, None, "ax", "az", None),
    )
    out_specs = (P(None, None, "ax", "az", None), P(None, None, "ax", "az", None))
    return jax.shard_map(body, mesh=mesh, in_specs=in_specs, out_specs=out_specs, check_vma=False)
```

profile of v0, /device:TPU:0, one launch (start us, length us, event | category | flops | bytes accessed | tf_op | source)
XLA Modules:
  0.0 61.1 jit_solution(1161339658373961905)
XLA Ops:
  0.6 3.7 %shard_map.79 = s16[768,384]{1,0:T(8,128)(2,1)} custom-call(bf16[3,256,512]{2,1,0:T(8,128)(2,1)} %bitcast.14, s32[1,256]{1,0:T(1,128)} %bitcast.16, s32[1,256]{1,0:T(1,128)} %bitcast.17, s32[1,256]{1,0:T(1,128)} %bitcast.18, bf16[125,2,512]{2,1,0:T(2,128)(2,1)} %bitcast.15), custom_call_target="tpu_custom_call" | custom-call | tf_op jit(solution)/shard_map/pallas_call | solution.py:567
  4.3 7.3 %all-to-all-start = ((s16[32,24,384]{2,1,0:T(8,128)(2,1)}), s16[32,24,384]{2,1,0:T(8,128)(2,1)S(1)}, u32[]{:S(2)}, u32[]{:S(2)}) async-start(s16[32,24,384]{2,1,0:T(8,128)(2,1)} %bitcast.13), calls=%async_computation | async-start | bytes 1179648 | tf_op jit(solution)/shard_map/all_to_all | solution.py:590
  11.7 2.7 %shard_map.77 = (f32[625,8,128]{2,1,0:T(8,128)S(1)}, bf16[125,4,128]{2,1,0:T(4,128)(2,1)}, bf16[65,4,128]{2,1,0:T(4,128)(2,1)}, bf16[60,4,128]{2,1,0:T(4,128)(2,...) custom-call(f32[625,8,128]{2,1,0:T(8,128)} %bitcast.11), custom_call_target="tpu_custom_call" | custom-call | tf_op jit(solution)/shard_map/pallas_call | solution.py:592
  14.4 0.7 %collective-permute-start = (bf16[125,4,128]{2,1,0:T(4,128)(2,1)}, bf16[125,4,128]{2,1,0:T(4,128)(2,1)S(1)}, u32[]{:S(2)}, u32[]{:S(2)}) collective-permute-start(bf16[125,4,128]{2,1,0:T(4,128)(2,1)} %get-tuple-element.37), channel_id=1, source_target_pairs={{4,8},{8,4},{12,16},{16,12},{20,24},{24,20},{5,9},{9,5},{13,17},{1... | collective-permute-start | bytes 384008 | tf_op jit(solution)/shard_map/ppermute | solution.py:542
  15.1 1.6 %collective-permute-start.3 = (bf16[132,2,128]{2,1,0:T(2,128)(2,1)}, bf16[132,2,128]{2,1,0:T(2,128)(2,1)S(1)}, u32[]{:S(2)}, u32[]{:S(2)}) collective-permute-start(bf16[132,2,128]{2,1,0:T(2,128)(2,1)} %get-tuple-element.40), channel_id=1, source_target_pairs={{1,2},{2,1},{3,0},{0,3},{5,6},{6,5},{7,4},{4,7},{9,10},{10,9},{11,... | collective-permute-start | bytes 202760 | tf_op jit(solution)/shard_map/ppermute | solution.py:552
  16.7 0.4 collective-permute-start.4
  17.0 4.2 %collective-permute-start.1 = (bf16[65,4,128]{2,1,0:T(4,128)(2,1)}, bf16[65,4,128]{2,1,0:T(4,128)(2,1)S(1)}, u32[]{:S(2)}, u32[]{:S(2)}) collective-permute-start(bf16[65,4,128]{2,1,0:T(4,128)(2,1)} %get-tuple-element.38), channel_id=1, source_target_pairs={{0,4},{4,0},{8,12},{12,8},{16,20},{20,16},{24,28},{28,24},{1,5},{5... | collective-permute-start | bytes 199688 | tf_op jit(solution)/shard_map/ppermute | solution.py:543
  21.2 0.0 collective-permute-start.2
  21.2 1.7 %shard_map.78.state_in = f32[625,8,128]{2,1,0:T(8,128)S(1)} custom-call(f32[625,8,128]{2,1,0:T(8,128)S(1)} %get-tuple-element.36.state_ref.sum_in), custom_call_target="tpu_custom_call" | custom-call | tf_op jit(solution)/shard_map/pallas_call | solution.py:600
  22.9 0.0 copy-start
  23.0 1.5 %copy-done = f32[625,8,128]{2,1,0:T(8,128)} copy-done((f32[625,8,128]{2,1,0:T(8,128)}, f32[625,8,128]{2,1,0:T(8,128)S(1)}, u32[]{:S(2)}) %copy-start) | copy-done | bytes 2560024
  24.4 4.1 %all-to-all-done = s16[32,24,384]{2,1,0:T(8,128)(2,1)S(1)} async-done(((s16[32,24,384]{2,1,0:T(8,128)(2,1)}), s16[32,24,384]{2,1,0:T(8,128)(2,1)S(1)}, u32[]{:S(2)}, u32[]{:S(2)}) %all-to-all-start) | async-done | bytes 589856 | tf_op jit(solution)/shard_map/all_to_all | solution.py:590
  28.5 1.7 %shard_map.80.source_ref = f32[3000,128]{1,0:T(8,128)S(1)} custom-call(s16[768,384]{1,0:T(8,128)(2,1)S(1)} %bitcast.10), custom_call_target="tpu_custom_call" | custom-call | tf_op jit(solution)/shard_map/pallas_call | solution.py:601
  30.2 0.0 copy-start.1
  30.3 0.0 collective-permute-done.2.near_b
  30.3 0.0 collective-permute-done.3.az_far
  30.3 0.0 collective-permute-done.4.az_near
  30.3 1.2 %shard_map.81 = (f32[625,8,128]{2,1,0:T(8,128)S(1)}, bf16[125,4,128]{2,1,0:T(4,128)(2,1)S(1)}, bf16[65,4,128]{2,1,0:T(4,128)(2,1)S(1)}, bf16[60,4,128]{2,1,0:T(4...) custom-call(f32[625,8,128]{2,1,0:T(8,128)S(1)} %shard_map.78.state_i, ...), custom_call_target="tpu_custom_call", output_to_operand_aliasing={{0}: (0, {})} | custom-call | tf_op jit(solution)/shard_map/pallas_call | solution.py:602
  31.5 0.7 %collective-permute-start.5 = (bf16[125,4,128]{2,1,0:T(4,128)(2,1)S(1)}, bf16[125,4,128]{2,1,0:T(4,128)(2,1)S(1)}, u32[]{:S(2)}, u32[]{:S(2)}) collective-permute-start(bf16[125,4,128]{2,1,0:T(4,128)(2,1)S(1)} %get-tuple-element.44), channel_id=1, source_target_pairs={{4,8},{8,4},{12,16},{16,12},{20,24},{24,20},{5,9},{9,5},{13,17},{1... | collective-permute-start | bytes 384008 | tf_op jit(solution)/shard_map/ppermute | solution.py:542
  32.1 1.0 %collective-permute-start.6 = (bf16[132,2,128]{2,1,0:T(2,128)(2,1)S(1)}, bf16[132,2,128]{2,1,0:T(2,128)(2,1)S(1)}, u32[]{:S(2)}, u32[]{:S(2)}) collective-permute-start(bf16[132,2,128]{2,1,0:T(2,128)(2,1)S(1)} %get-tuple-element.45), channel_id=1, source_target_pairs={{1,2},{2,1},{3,0},{0,3},{5,6},{6,5},{7,4},{4,7},{9,10},{10,9},{11,... | collective-permute-start | bytes 202760 | tf_op jit(solution)/shard_map/ppermute | solution.py:552
  33.2 0.6 %collective-permute-start.7 = (bf16[132,2,128]{2,1,0:T(2,128)(2,1)S(1)}, bf16[132,2,128]{2,1,0:T(2,128)(2,1)S(1)}, u32[]{:S(2)}, u32[]{:S(2)}) collective-permute-start(bf16[132,2,128]{2,1,0:T(2,128)(2,1)S(1)} %get-tuple-element.46), channel_id=1, source_target_pairs={{0,1},{1,0},{2,3},{3,2},{4,5},{5,4},{6,7},{7,6},{8,9},{9,8},{10,11... | collective-permute-start | bytes 202760 | tf_op jit(solution)/shard_map/ppermute | solution.py:552
  33.8 3.1 %collective-permute-start.8 = (bf16[65,4,128]{2,1,0:T(4,128)(2,1)S(1)}, bf16[65,4,128]{2,1,0:T(4,128)(2,1)S(1)}, u32[]{:S(2)}, u32[]{:S(2)}) collective-permute-start(bf16[65,4,128]{2,1,0:T(4,128)(2,1)S(1)} %get-tuple-element.48), channel_id=1, source_target_pairs={{0,4},{4,0},{8,12},{12,8},{16,20},{20,16},{24,28},{28,24},{1,5},{5... | collective-permute-start | bytes 199688 | tf_op jit(solution)/shard_map/ppermute | solution.py:543
  36.9 0.0 collective-permute-start.9
  36.9 1.9 %shard_map.82 = (f32[625,8,128]{2,1,0:T(8,128)S(1)}, f32[625,8,128]{2,1,0:T(8,128)S(1)}, f32[3000,128]{1,0:T(8,128)}) custom-call(f32[625,8,128]{2,1,0:T(8,128)S(1)} %get-tuple-element.42.state_ref, f32[625,8,128]{2,1,0:T(8,128)S(1)} %copy-done.1, f32[3000,128]{1,0:T(8,128)S(1)} %shard_map.80.source_ref), custom_call_target="tpu_custom_call" | custom-call | tf_op jit(solution)/shard_map/pallas_call | solution.py:610
  38.8 0.0 collective-permute-done.5.far
  38.8 0.5 shard_map.83
  39.3 0.7 %collective-permute-start.10 = (bf16[125,4,128]{2,1,0:T(4,128)(2,1)S(1)}, bf16[125,4,128]{2,1,0:T(4,128)(2,1)S(1)}, u32[]{:S(2)}, u32[]{:S(2)}) collective-permute-start(bf16[125,4,128]{2,1,0:T(4,128)(2,1)S(1)} %get-tuple-element.53), channel_id=1, source_target_pairs={{4,8},{8,4},{12,16},{16,12},{20,24},{24,20},{5,9},{9,5},{13,17},{1... | collective-permute-start | bytes 384008 | tf_op jit(solution)/shard_map/ppermute | solution.py:542
  40.0 1.1 %collective-permute-done.9.near_b = bf16[60,4,128]{2,1,0:T(4,128)(2,1)S(1)} collective-permute-done((bf16[60,4,128]{2,1,0:T(4,128)(2,1)S(1)}, bf16[60,4,128]{2,1,0:T(4,128)(2,1)S(1)}, u32[]{:S(2)}, u32[]{:S(2)}) %collective-permute-start.9) | collective-permute-done | bytes 61472 | tf_op jit(solution)/shard_map/ppermute | solution.py:543
  41.1 0.0 collective-permute-done.8.near_a
  41.1 0.4 shard_map.84
  41.5 0.8 %collective-permute-start.11 = (bf16[132,2,128]{2,1,0:T(2,128)(2,1)S(1)}, bf16[132,2,128]{2,1,0:T(2,128)(2,1)S(1)}, u32[]{:S(2)}, u32[]{:S(2)}) collective-permute-start(bf16[132,2,128]{2,1,0:T(2,128)(2,1)S(1)} %get-tuple-element.54), channel_id=1, source_target_pairs={{1,2},{2,1},{3,0},{0,3},{5,6},{6,5},{7,4},{4,7},{9,10},{10,9},{11,... | collective-permute-start | bytes 202760 | tf_op jit(solution)/shard_map/ppermute | solution.py:552
  42.3 0.8 %collective-permute-start.12 = (bf16[132,2,128]{2,1,0:T(2,128)(2,1)S(1)}, bf16[132,2,128]{2,1,0:T(2,128)(2,1)S(1)}, u32[]{:S(2)}, u32[]{:S(2)}) collective-permute-start(bf16[132,2,128]{2,1,0:T(2,128)(2,1)S(1)} %get-tuple-element.55), channel_id=1, source_target_pairs={{0,1},{1,0},{2,3},{3,2},{4,5},{5,4},{6,7},{7,6},{8,9},{9,8},{10,11... | collective-permute-start | bytes 202760 | tf_op jit(solution)/shard_map/ppermute | solution.py:552
  43.0 3.7 %collective-permute-start.13 = (bf16[65,4,128]{2,1,0:T(4,128)(2,1)S(1)}, bf16[65,4,128]{2,1,0:T(4,128)(2,1)S(1)}, u32[]{:S(2)}, u32[]{:S(2)}) collective-permute-start(bf16[65,4,128]{2,1,0:T(4,128)(2,1)S(1)} %get-tuple-element.57), channel_id=1, source_target_pairs={{0,4},{4,0},{8,12},{12,8},{16,20},{20,16},{24,28},{28,24},{1,5},{5... | collective-permute-start | bytes 199688 | tf_op jit(solution)/shard_map/ppermute | solution.py:543
  46.7 0.0 collective-permute-start.14
  46.7 1.9 %shard_map.85 = (f32[625,8,128]{2,1,0:T(8,128)S(1)}, f32[625,8,128]{2,1,0:T(8,128)S(1)}) custom-call(f32[625,8,128]{2,1,0:T(8,128)S(1)} %get-tuple-element.50.state_ref, f32[625,8,128]{2,1,0:T(8,128)S(1)} %get-tuple-element.51.sum_in), custom_call_target="tpu_custom_call" | custom-call | tf_op jit(solution)/shard_map/pallas_call | solution.py:635
  48.6 0.0 collective-permute-done.11.az_far
  48.7 0.5 shard_map.86
  49.2 0.7 %collective-permute-start.15 = (bf16[125,4,128]{2,1,0:T(4,128)(2,1)S(1)}, bf16[125,4,128]{2,1,0:T(4,128)(2,1)S(1)}, u32[]{:S(2)}, u32[]{:S(2)}) collective-permute-start(bf16[125,4,128]{2,1,0:T(4,128)(2,1)S(1)} %get-tuple-element.61), channel_id=1, source_target_pairs={{4,8},{8,4},{12,16},{16,12},{20,24},{24,20},{5,9},{9,5},{13,17},{1... | collective-permute-start | bytes 384008 | tf_op jit(solution)/shard_map/ppermute | solution.py:542
  49.9 1.0 %collective-permute-done.14.near_b = bf16[60,4,128]{2,1,0:T(4,128)(2,1)S(1)} collective-permute-done((bf16[60,4,128]{2,1,0:T(4,128)(2,1)S(1)}, bf16[60,4,128]{2,1,0:T(4,128)(2,1)S(1)}, u32[]{:S(2)}, u32[]{:S(2)}) %collective-permute-start.14) | collective-permute-done | bytes 61472 | tf_op jit(solution)/shard_map/ppermute | solution.py:543
  50.9 0.4 shard_map.87
  51.3 0.1 collective-permute-start.16
  51.4 1.4 %collective-permute-start.17 = (bf16[132,2,128]{2,1,0:T(2,128)(2,1)S(1)}, bf16[132,2,128]{2,1,0:T(2,128)(2,1)S(1)}, u32[]{:S(2)}, u32[]{:S(2)}) collective-permute-start(bf16[132,2,128]{2,1,0:T(2,128)(2,1)S(1)} %get-tuple-element.63), channel_id=1, source_target_pairs={{0,1},{1,0},{2,3},{3,2},{4,5},{5,4},{6,7},{7,6},{8,9},{9,8},{10,11... | collective-permute-start | bytes 202760 | tf_op jit(solution)/shard_map/ppermute | solution.py:552
  52.7 3.2 %collective-permute-start.18 = (bf16[65,4,128]{2,1,0:T(4,128)(2,1)S(1)}, bf16[65,4,128]{2,1,0:T(4,128)(2,1)S(1)}, u32[]{:S(2)}, u32[]{:S(2)}) collective-permute-start(bf16[65,4,128]{2,1,0:T(4,128)(2,1)S(1)} %get-tuple-element.66), channel_id=1, source_target_pairs={{0,4},{4,0},{8,12},{12,8},{16,20},{20,16},{24,28},{28,24},{1,5},{5... | collective-permute-start | bytes 199688 | tf_op jit(solution)/shard_map/ppermute | solution.py:543
  55.9 0.0 collective-permute-start.19
  56.0 2.0 %shard_map.88.state_in = f32[625,8,128]{2,1,0:T(8,128)S(1)} custom-call(f32[625,8,128]{2,1,0:T(8,128)S(1)} %get-tuple-element.59.state_ref, f32[625,8,128]{2,1,0:T(8,128)S(1)} %get-tuple-element.60.sum_in), custom_call_target="tpu_custom_call" | custom-call | tf_op jit(solution)/shard_map/pallas_call | solution.py:639
  58.0 1.8 %shard_map.89 = (f32[625,8,128]{2,1,0:T(8,128)S(1)}, f32[625,8,128]{2,1,0:T(8,128)}) custom-call(f32[625,8,128]{2,1,0:T(8,128)S(1)} %shard_map.88.state_in, bf16[125,4,128]{2,1,0:T(4,128)(2,1)S(1)} %collective-permute-done.15.far, bf16[132,2,128]{2,1,0:T(2,128)(2,1)S(1)} %collective-permute-done.16.az_far, ...), custom_call_target="tpu_custom_call", output_to_operand_aliasing={{0}: (0, {})} | custom-call | tf_op jit(solution)/shard_map/pallas_call | solution.py:646
  59.8 0.4 collective-permute-done.19.near_b
  60.1 0.9 %shard_map.90 = (f32[625,8,128]{2,1,0:T(8,128)S(1)}, f32[625,8,128]{2,1,0:T(8,128)}) custom-call(f32[625,8,128]{2,1,0:T(8,128)S(1)} %get-tuple-element.64.state_in, f32[625,8,128]{2,1,0:T(8,128)} %get-tuple-element.65.out_in, bf16[65,4,128]{2,1,0:T(4,128)(2,1)S(1)} %collective-permute-done.18.near_a, ...), custom_call_target="tpu_custom_call", output_to_operand_aliasing={{0}: (0, {}), {1}: (1, {})} | custom-call | tf_op jit(solution)/shard_map/pallas_call | solution.py:654
  (12 shorter events, 0.0 us)
Async XLA Ops:
  4.3 24.2 %all-to-all-start = ((s16[32,24,384]{2,1,0:T(8,128)(2,1)}), s16[32,24,384]{2,1,0:T(8,128)(2,1)S(1)}, u32[]{:S(2)}, u32[]{:S(2)}) async-start(s16[32,24,384]{2,1,0:T(8,128)(2,1)} %bitcast.13), calls=%async_computation | async-start | bytes 1179648 | tf_op jit(solution)/shard_map/all_to_all | solution.py:590
  14.4 15.9 %collective-permute-start = (bf16[125,4,128]{2,1,0:T(4,128)(2,1)}, bf16[125,4,128]{2,1,0:T(4,128)(2,1)S(1)}, u32[]{:S(2)}, u32[]{:S(2)}) collective-permute-start(bf16[125,4,128]{2,1,0:T(4,128)(2,1)} %get-tuple-element.37), channel_id=1, source_target_pairs={{4,8},{8,4},{12,16},{16,12},{20,24},{24,20},{5,9},{9,5},{13,17},{1... | collective-permute-start | bytes 384008 | tf_op jit(solution)/shard_map/ppermute | solution.py:542
  15.1 15.2 %collective-permute-start.3 = (bf16[132,2,128]{2,1,0:T(2,128)(2,1)}, bf16[132,2,128]{2,1,0:T(2,128)(2,1)S(1)}, u32[]{:S(2)}, u32[]{:S(2)}) collective-permute-start(bf16[132,2,128]{2,1,0:T(2,128)(2,1)} %get-tuple-element.40), channel_id=1, source_target_pairs={{1,2},{2,1},{3,0},{0,3},{5,6},{6,5},{7,4},{4,7},{9,10},{10,9},{11,... | collective-permute-start | bytes 202760 | tf_op jit(solution)/shard_map/ppermute | solution.py:552
  16.7 13.6 %collective-permute-start.4 = (bf16[132,2,128]{2,1,0:T(2,128)(2,1)}, bf16[132,2,128]{2,1,0:T(2,128)(2,1)S(1)}, u32[]{:S(2)}, u32[]{:S(2)}) collective-permute-start(bf16[132,2,128]{2,1,0:T(2,128)(2,1)} %get-tuple-element.41), channel_id=1, source_target_pairs={{0,1},{1,0},{2,3},{3,2},{4,5},{5,4},{6,7},{7,6},{8,9},{9,8},{10,11... | collective-permute-start | bytes 202760 | tf_op jit(solution)/shard_map/ppermute | solution.py:552
  17.0 13.2 %collective-permute-start.1 = (bf16[65,4,128]{2,1,0:T(4,128)(2,1)}, bf16[65,4,128]{2,1,0:T(4,128)(2,1)S(1)}, u32[]{:S(2)}, u32[]{:S(2)}) collective-permute-start(bf16[65,4,128]{2,1,0:T(4,128)(2,1)} %get-tuple-element.38), channel_id=1, source_target_pairs={{0,4},{4,0},{8,12},{12,8},{16,20},{20,16},{24,28},{28,24},{1,5},{5... | collective-permute-start | bytes 199688 | tf_op jit(solution)/shard_map/ppermute | solution.py:543
  21.2 9.1 %collective-permute-start.2 = (bf16[60,4,128]{2,1,0:T(4,128)(2,1)}, bf16[60,4,128]{2,1,0:T(4,128)(2,1)S(1)}, u32[]{:S(2)}, u32[]{:S(2)}) collective-permute-start(bf16[60,4,128]{2,1,0:T(4,128)(2,1)} %get-tuple-element.39), channel_id=1, source_target_pairs={{0,4},{4,0},{8,12},{12,8},{16,20},{20,16},{24,28},{28,24},{1,5},{5... | collective-permute-start | bytes 184328 | tf_op jit(solution)/shard_map/ppermute | solution.py:543
  22.9 1.5 %copy-start = (f32[625,8,128]{2,1,0:T(8,128)}, f32[625,8,128]{2,1,0:T(8,128)S(1)}, u32[]{:S(2)}) copy-start(f32[625,8,128]{2,1,0:T(8,128)S(1)} %get-tuple-element.36.state_ref.sum_in) | copy-start | bytes 7680004
  30.2 6.7 %copy-start.1 = (f32[625,8,128]{2,1,0:T(8,128)S(1)}, f32[625,8,128]{2,1,0:T(8,128)}, u32[]{:S(2)}) copy-start(f32[625,8,128]{2,1,0:T(8,128)} %copy-done) | copy-start | bytes 7680004
  31.5 7.3 %collective-permute-start.5 = (bf16[125,4,128]{2,1,0:T(4,128)(2,1)S(1)}, bf16[125,4,128]{2,1,0:T(4,128)(2,1)S(1)}, u32[]{:S(2)}, u32[]{:S(2)}) collective-permute-start(bf16[125,4,128]{2,1,0:T(4,128)(2,1)S(1)} %get-tuple-element.44), channel_id=1, source_target_pairs={{4,8},{8,4},{12,16},{16,12},{20,24},{24,20},{5,9},{9,5},{13,17},{1... | collective-permute-start | bytes 384008 | tf_op jit(solution)/shard_map/ppermute | solution.py:542
  32.1 6.6 %collective-permute-start.6 = (bf16[132,2,128]{2,1,0:T(2,128)(2,1)S(1)}, bf16[132,2,128]{2,1,0:T(2,128)(2,1)S(1)}, u32[]{:S(2)}, u32[]{:S(2)}) collective-permute-start(bf16[132,2,128]{2,1,0:T(2,128)(2,1)S(1)} %get-tuple-element.45), channel_id=1, source_target_pairs={{1,2},{2,1},{3,0},{0,3},{5,6},{6,5},{7,4},{4,7},{9,10},{10,9},{11,... | collective-permute-start | bytes 202760 | tf_op jit(solution)/shard_map/ppermute | solution.py:552
  33.2 5.6 %collective-permute-start.7 = (bf16[132,2,128]{2,1,0:T(2,128)(2,1)S(1)}, bf16[132,2,128]{2,1,0:T(2,128)(2,1)S(1)}, u32[]{:S(2)}, u32[]{:S(2)}) collective-permute-start(bf16[132,2,128]{2,1,0:T(2,128)(2,1)S(1)} %get-tuple-element.46), channel_id=1, source_target_pairs={{0,1},{1,0},{2,3},{3,2},{4,5},{5,4},{6,7},{7,6},{8,9},{9,8},{10,11... | collective-permute-start | bytes 202760 | tf_op jit(solution)/shard_map/ppermute | solution.py:552
  33.8 7.3 %collective-permute-start.8 = (bf16[65,4,128]{2,1,0:T(4,128)(2,1)S(1)}, bf16[65,4,128]{2,1,0:T(4,128)(2,1)S(1)}, u32[]{:S(2)}, u32[]{:S(2)}) collective-permute-start(bf16[65,4,128]{2,1,0:T(4,128)(2,1)S(1)} %get-tuple-element.48), channel_id=1, source_target_pairs={{0,4},{4,0},{8,12},{12,8},{16,20},{20,16},{24,28},{28,24},{1,5},{5... | collective-permute-start | bytes 199688 | tf_op jit(solution)/shard_map/ppermute | solution.py:543
  36.9 4.2 %collective-permute-start.9 = (bf16[60,4,128]{2,1,0:T(4,128)(2,1)S(1)}, bf16[60,4,128]{2,1,0:T(4,128)(2,1)S(1)}, u32[]{:S(2)}, u32[]{:S(2)}) collective-permute-start(bf16[60,4,128]{2,1,0:T(4,128)(2,1)S(1)} %get-tuple-element.49), channel_id=1, source_target_pairs={{0,4},{4,0},{8,12},{12,8},{16,20},{20,16},{24,28},{28,24},{1,5},{5... | collective-permute-start | bytes 184328 | tf_op jit(solution)/shard_map/ppermute | solution.py:543
  39.3 9.3 %collective-permute-start.10 = (bf16[125,4,128]{2,1,0:T(4,128)(2,1)S(1)}, bf16[125,4,128]{2,1,0:T(4,128)(2,1)S(1)}, u32[]{:S(2)}, u32[]{:S(2)}) collective-permute-start(bf16[125,4,128]{2,1,0:T(4,128)(2,1)S(1)} %get-tuple-element.53), channel_id=1, source_target_pairs={{4,8},{8,4},{12,16},{16,12},{20,24},{24,20},{5,9},{9,5},{13,17},{1... | collective-permute-start | bytes 384008 | tf_op jit(solution)/shard_map/ppermute | solution.py:542
  41.5 7.2 %collective-permute-start.11 = (bf16[132,2,128]{2,1,0:T(2,128)(2,1)S(1)}, bf16[132,2,128]{2,1,0:T(2,128)(2,1)S(1)}, u32[]{:S(2)}, u32[]{:S(2)}) collective-permute-start(bf16[132,2,128]{2,1,0:T(2,128)(2,1)S(1)} %get-tuple-element.54), channel_id=1, source_target_pairs={{1,2},{2,1},{3,0},{0,3},{5,6},{6,5},{7,4},{4,7},{9,10},{10,9},{11,... | collective-permute-start | bytes 202760 | tf_op jit(solution)/shard_map/ppermute | solution.py:552
  42.3 6.4 %collective-permute-start.12 = (bf16[132,2,128]{2,1,0:T(2,128)(2,1)S(1)}, bf16[132,2,128]{2,1,0:T(2,128)(2,1)S(1)}, u32[]{:S(2)}, u32[]{:S(2)}) collective-permute-start(bf16[132,2,128]{2,1,0:T(2,128)(2,1)S(1)} %get-tuple-element.55), channel_id=1, source_target_pairs={{0,1},{1,0},{2,3},{3,2},{4,5},{5,4},{6,7},{7,6},{8,9},{9,8},{10,11... | collective-permute-start | bytes 202760 | tf_op jit(solution)/shard_map/ppermute | solution.py:552
  43.0 7.9 %collective-permute-start.13 = (bf16[65,4,128]{2,1,0:T(4,128)(2,1)S(1)}, bf16[65,4,128]{2,1,0:T(4,128)(2,1)S(1)}, u32[]{:S(2)}, u32[]{:S(2)}) collective-permute-start(bf16[65,4,128]{2,1,0:T(4,128)(2,1)S(1)} %get-tuple-element.57), channel_id=1, source_target_pairs={{0,4},{4,0},{8,12},{12,8},{16,20},{20,16},{24,28},{28,24},{1,5},{5... | collective-permute-start | bytes 199688 | tf_op jit(solution)/shard_map/ppermute | solution.py:543
  46.7 4.2 %collective-permute-start.14 = (bf16[60,4,128]{2,1,0:T(4,128)(2,1)S(1)}, bf16[60,4,128]{2,1,0:T(4,128)(2,1)S(1)}, u32[]{:S(2)}, u32[]{:S(2)}) collective-permute-start(bf16[60,4,128]{2,1,0:T(4,128)(2,1)S(1)} %get-tuple-element.58), channel_id=1, source_target_pairs={{0,4},{4,0},{8,12},{12,8},{16,20},{20,16},{24,28},{28,24},{1,5},{5... | collective-permute-start | bytes 184328 | tf_op jit(solution)/shard_map/ppermute | solution.py:543
  49.2 8.7 %collective-permute-start.15 = (bf16[125,4,128]{2,1,0:T(4,128)(2,1)S(1)}, bf16[125,4,128]{2,1,0:T(4,128)(2,1)S(1)}, u32[]{:S(2)}, u32[]{:S(2)}) collective-permute-start(bf16[125,4,128]{2,1,0:T(4,128)(2,1)S(1)} %get-tuple-element.61), channel_id=1, source_target_pairs={{4,8},{8,4},{12,16},{16,12},{20,24},{24,20},{5,9},{9,5},{13,17},{1... | collective-permute-start | bytes 384008 | tf_op jit(solution)/shard_map/ppermute | solution.py:542
  51.3 6.6 %collective-permute-start.16 = (bf16[132,2,128]{2,1,0:T(2,128)(2,1)S(1)}, bf16[132,2,128]{2,1,0:T(2,128)(2,1)S(1)}, u32[]{:S(2)}, u32[]{:S(2)}) collective-permute-start(bf16[132,2,128]{2,1,0:T(2,128)(2,1)S(1)} %get-tuple-element.62), channel_id=1, source_target_pairs={{1,2},{2,1},{3,0},{0,3},{5,6},{6,5},{7,4},{4,7},{9,10},{10,9},{11,... | collective-permute-start | bytes 202760 | tf_op jit(solution)/shard_map/ppermute | solution.py:552
  51.4 6.6 %collective-permute-start.17 = (bf16[132,2,128]{2,1,0:T(2,128)(2,1)S(1)}, bf16[132,2,128]{2,1,0:T(2,128)(2,1)S(1)}, u32[]{:S(2)}, u32[]{:S(2)}) collective-permute-start(bf16[132,2,128]{2,1,0:T(2,128)(2,1)S(1)} %get-tuple-element.63), channel_id=1, source_target_pairs={{0,1},{1,0},{2,3},{3,2},{4,5},{5,4},{6,7},{7,6},{8,9},{9,8},{10,11... | collective-permute-start | bytes 202760 | tf_op jit(solution)/shard_map/ppermute | solution.py:552
  52.7 7.4 %collective-permute-start.18 = (bf16[65,4,128]{2,1,0:T(4,128)(2,1)S(1)}, bf16[65,4,128]{2,1,0:T(4,128)(2,1)S(1)}, u32[]{:S(2)}, u32[]{:S(2)}) collective-permute-start(bf16[65,4,128]{2,1,0:T(4,128)(2,1)S(1)} %get-tuple-element.66), channel_id=1, source_target_pairs={{0,4},{4,0},{8,12},{12,8},{16,20},{20,16},{24,28},{28,24},{1,5},{5... | collective-permute-start | bytes 199688 | tf_op jit(solution)/shard_map/ppermute | solution.py:543
  55.9 4.2 %collective-permute-start.19 = (bf16[60,4,128]{2,1,0:T(4,128)(2,1)S(1)}, bf16[60,4,128]{2,1,0:T(4,128)(2,1)S(1)}, u32[]{:S(2)}, u32[]{:S(2)}) collective-permute-start(bf16[60,4,128]{2,1,0:T(4,128)(2,1)S(1)} %get-tuple-element.67), channel_id=1, source_target_pairs={{0,4},{4,0},{8,12},{12,8},{16,20},{20,16},{24,28},{28,24},{1,5},{5... | collective-permute-start | bytes 184328 | tf_op jit(solution)/shard_map/ppermute | solution.py:543
where the time goes:
time: 61.4 us; the launch traced here: 61.1 us
  starting transfers between devices  30.8 us (50%)
  Pallas kernels  21.3 us (35%)
  waiting for transfers between devices  6.62 us (11%)
  local copies, waits for them, and re-layouts  1.47 us (2%)
  between operations  0.9 us (1%)
    ppermute x8, starting transfers between devices, swap(): lax.ppermute(part, 'ax', pairs[0])  14.2 us
    all_to_all x1, starting transfers between devices, body(): lax.all_to_all(buffer, ('ax', 'az'), split_axis=0, concat_axis=0, tiled=T...  7.3 us
    all_to_all x1, waiting for transfers between devices, body(): lax.all_to_all(buffer, ('ax', 'az'), split_axis=0, concat_axis=0, tiled=T...  4.11 us
    pallas_call x1, Pallas kernels, body(): call(functools.partial(contribution_kernel, capacity, devices), pltpu.HBM...  3.7 us
    ppermute x4, starting transfers between devices, turn(): lax.ppermute(far, 'az', pairs[1])  3.49 us
    ppermute x4, starting transfers between devices, turn(): lax.ppermute(near, 'az', pairs[0])  3.12 us
    pallas_call x1, Pallas kernels, body(): call(load_kernel, [vmem_state] + face_shapes, [IN_HBM], scratch=[pltpu.Se...  2.75 us
    ppermute x4, starting transfers between devices, swap(): lax.ppermute(far, 'ax', pairs[1])  2.68 us
  transfers between devices with their start and end apart: 21, of which 4 were waited for; matrix products, arithmetic and copies ran while one was open for 0% of the time, Pallas kernels for 25%

commit v1 on v0

--- a/solution.py
+++ b/solution.py
@@ -53,13 +53,18 @@
 
 
 def flux(q, direction):
-    p, u, v, w, rho = q
-    pressure = p + MACH * u
+    g, u, v, w, e = q
     if direction == 0:
-        return [MACH * p + u, pressure, None, None, MACH * rho + u]
+        return [(2.0 * MACH) * g + (1.0 - MACH**2) * u, g, None, None, MACH * e]
     if direction == 1:
-        return [v, None, pressure, None, v]
-    return [w, None, None, pressure, w]
+        return [v, None, g, None, None]
+    return [w, None, None, g, None]
+
+
+def original(q):
+    g, u, v, w, e = q
+    p = g - MACH * u
+    return [p, u, v, w, e + p]
 
 
 def lifted(q, direction, normal, rusanov_sign):
@@ -73,30 +78,24 @@
 
 
 def coupled(jump, direction, normal, scale):
-    p, u, v, w, rho = jump
+    g, u, v, w, e = jump
     rusanov, lift = scale * LIFT * RUSANOV, scale * LIFT * normal
     if direction == 0:
-        own = lift * MACH - rusanov
-        if abs(own + lift) < 1e-9:
-            across = lift * (u - p)
-            return [across, -across, -rusanov * v, -rusanov * w, lift * (u - rho)]
-        across = lift * u
         return [
-            own * p + across,
-            lift * p + own * u,
+            (2.0 * MACH * lift - rusanov) * g + ((1.0 - MACH**2) * lift) * u,
+            lift * g - rusanov * u,
             -rusanov * v,
             -rusanov * w,
-            own * rho + across,
+            (MACH * lift - rusanov) * e,
         ]
     normal_velocity = (v, w)[direction - 1]
-    across = lift * normal_velocity
-    along = lift * p + (lift * MACH) * u - rusanov * normal_velocity
+    along = lift * g - rusanov * normal_velocity
     return [
-        across - rusanov * p,
+        lift * normal_velocity - rusanov * g,
         -rusanov * u,
         along if direction == 1 else -rusanov * v,
         along if direction == 2 else -rusanov * w,
-        across - rusanov * rho,
+        -rusanov * e,
     ]
 
 
@@ -135,26 +134,26 @@
     def line(direction, nodes):
         q = [[load(f, n) for n in nodes] for f in range(FIELDS)]
         ends = face_terms(direction, [x[0] for x in q], [x[4] for x in q])
+        g, u, e = q[0], q[1], q[4]
         if direction == 0:
+            mixed = [(2.0 * MACH) * g[k] + (1.0 - MACH**2) * u[k] for k in range(5)]
             parts = {
-                0: differentiate([MACH * q[0][k] + q[1][k] for k in range(5)], scale),
-                1: differentiate([MACH * q[1][k] + q[0][k] for k in range(5)], scale),
-                4: differentiate([MACH * q[4][k] + q[1][k] for k in range(5)], scale),
+                0: differentiate(mixed, scale),
+                1: differentiate(g, scale),
+                4: differentiate(e, scale * MACH),
             }
         else:
-            along = differentiate(q[direction + 1], scale)
             parts = {
-                0: along,
-                direction + 1: differentiate([MACH * q[1][k] + q[0][k] for k in range(5)], scale),
-                4: along,
+                0: differentiate(q[direction + 1], scale),
+                direction + 1: differentiate(g, scale),
             }
+        values = []
         for f in range(FIELDS):
-            for k in range(5):
-                value = parts[f][k] if f in parts else None
-                if k in (0, 4):
-                    end = ends[0 if k == 0 else 1][f]
-                    value = end if value is None else value + end
-                store(direction, f, nodes[k], value, q[f][k])
+            row = list(parts[f]) if f in parts else [None] * 5
+            for k, end in ((0, ends[0][f]), (4, ends[1][f])):
+                row[k] = end if row[k] is None else row[k] + end
+            values.append(row)
+        store(direction, nodes, values, q)
 
     @pl.loop(0, 5)
     def _(outer):
@@ -177,12 +176,14 @@
 
 
 def add_to(out_ref):
-    def store(direction, field, node, value, q):
-        at = field * NODES + node
-        if direction == 0:
-            out_ref[at] = jnp.zeros_like(q) if value is None else value
-        elif value is not None:
-            out_ref[at] += value
+    def store(direction, nodes, values, q):
+        for f in range(FIELDS):
+            for node, value in zip(nodes, values[f]):
+                at = f * NODES + node
+                if direction == 0:
+                    out_ref[at] = jnp.zeros_like(q[0][0]) if value is None else value
+                elif value is not None:
+                    out_ref[at] += value
 
     return store
 
@@ -190,11 +191,13 @@
 def volume_kernel(scale, state_ref, sum_in, out_ref, sum_ref):
     add = add_to(out_ref)
 
-    def store(direction, field, node, value, q):
-        add(direction, field, node, value, q)
+    def store(direction, nodes, values, q):
+        add(direction, nodes, values, q)
         if direction == 2:
-            at = field * NODES + node
-            sum_ref[at] = sum_in[at] + q
+            for f in range(FIELDS):
+                for node, value in zip(nodes, q[f]):
+                    at = f * NODES + node
+                    sum_ref[at] = sum_in[at] + value
 
     volume_into(state_ref, scale, store)
 
@@ -211,13 +214,18 @@
 def volume_last_kernel(scale, state_ref, sum_in, sum_ref, out_ref):
     add = add_to(out_ref)
 
-    def store(direction, field, node, value, q):
+    def store(direction, nodes, values, q):
         if direction < 2:
-            add(direction, field, node, value, q)
-        else:
-            at = field * NODES + node
-            total = sum_in[at] + q + out_ref[at]
-            sum_ref[at] = total if value is None else total + value
+            add(direction, nodes, values, q)
+            return
+        for k, node in enumerate(nodes):
+            totals = []
+            for f in range(FIELDS):
+                at = f * NODES + node
+                total = sum_in[at] + q[f][k] + out_ref[at]
+                totals.append(total if values[f][k] is None else total + values[f][k])
+            for f, total in enumerate(original(totals)):
+                sum_ref[f * NODES + node] = total
 
     volume_into(state_ref, scale, store)
 
@@ -228,53 +236,47 @@
     pl.when(parity == 1)(odd)
 
 
-def piece(face, row):
-    if not isinstance(face, (tuple, list)):
-        return face, pl.ds(row, 5)
-    first = face[0].shape[0]
-    return (face[0], pl.ds(row, 5)) if row < first else (face[1], pl.ds(row - first, 5))
-
-
-def received(face, start):
-    parts = [piece(face, f * 25 + start) for f in range(FIELDS)]
-    return [ref[rows].astype(jnp.float32) for ref, rows in parts]
-
-
-def add_ax(out_ref, face, high, weight):
+def received(ref, start):
+    return [ref[pl.ds(f * 25 + start, 5)].astype(jnp.float32) for f in range(FIELDS)]
+
+
+def add_ax(out_ref, face, high, weight, final):
     sign = -weight if high else weight
     first, rows = (100, slice(4, 8)) if high else (0, slice(0, 4))
     for chunk in range(5):
         terms = lifted(received(face, chunk * 5), 0, sign, weight)
+        terms = original(terms) if final else terms
         for f, term in enumerate(terms):
             out_ref[pl.ds(f * NODES + first + chunk * 5, 5), rows, :] += term
 
 
-def add_far(out_ref, face, weight):
+def add_far(out_ref, face, weight, final=False):
     on_parity(
         "ax",
-        lambda: add_ax(out_ref, face, False, weight),
-        lambda: add_ax(out_ref, face, True, weight),
-    )
-
-
-def add_near(out_ref, face, weight):
+        lambda: add_ax(out_ref, face, False, weight, final),
+        lambda: add_ax(out_ref, face, True, weight, final),
+    )
+
+
+def add_near(out_ref, face, weight, final=False):
     on_parity(
         "ax",
-        lambda: add_ax(out_ref, face, True, weight),
-        lambda: add_ax(out_ref, face, False, weight),
-    )
-
-
-def add_az(out_ref, far, near, weight):
+        lambda: add_ax(out_ref, face, True, weight, final),
+        lambda: add_ax(out_ref, face, False, weight, final),
+    )
+
+
+def add_az(out_ref, far, near, weight, final=False):
+    def add_side(face, at, rows, chunk, sign):
+        terms = lifted(received(face, chunk), 1, sign, weight)
+        for f, term in enumerate(original(terms) if final else terms):
+            for k, row in enumerate(rows):
+                out_ref[pl.ds(f * NODES + at, 5), row : row + 1, :] += term[:, k : k + 1]
+
     def add(low, high):
         for a in range(5):
-            at = a * 25
-            for f, term in enumerate(lifted(received(low, a * 5), 1, weight, weight)):
-                out_ref[pl.ds(f * NODES + at, 5), 0:1, :] += term[:, 0:1]
-                out_ref[pl.ds(f * NODES + at, 5), 4:5, :] += term[:, 1:2]
-            for f, term in enumerate(lifted(received(high, a * 5), 1, -weight, weight)):
-                out_ref[pl.ds(f * NODES + at + 20, 5), 3:4, :] += term[:, 0:1]
-                out_ref[pl.ds(f * NODES + at + 20, 5), 7:8, :] += term[:, 1:2]
+            add_side(low, a * 25, (0, 4), a * 5, weight)
+            add_side(high, a * 25 + 20, (3, 7), a * 5, -weight)
 
     on_parity("az", lambda: add(far, near), lambda: add(near, far))
 
@@ -282,9 +284,9 @@
 def pack_ax(state_ref, face, high):
     first, rows = (100, slice(4, 8)) if high else (0, slice(0, 4))
     for f in range(FIELDS):
-        for at in range(0, 25, 5):
-            ref, to = piece(face, f * 25 + at)
-            ref[to] = state_ref[pl.ds(f * NODES + first + at, 5), rows, :].astype(jnp.bfloat16)
+        face[pl.ds(f * 25, 25)] = state_ref[pl.ds(f * NODES + first, 25), rows, :].astype(
+            jnp.bfloat16
+        )
 
 
 def pack_far(state_ref, face):
@@ -308,7 +310,7 @@
     on_parity("az", lambda: pack(far, near), lambda: pack(near, far))
 
 
-def load_kernel(state_hbm, state_ref, far, near_a, near_b, az_far, az_near, sems):
+def load_kernel(state_hbm, state_ref, far, near, az_far, az_near, sems):
     copies = []
     for f in range(FIELDS):
         nodes = pl.ds(f * NODES, NODES)
@@ -317,24 +319,36 @@
         copies.append(copy)
     for copy in copies:
         copy.wait()
-    pack_faces(state_ref, far, near_a, near_b, az_far, az_near)
-
-
-def pack_faces(state_ref, far, near_a, near_b, az_far, az_near):
+
+    @pl.loop(0, NODES // 5)
+    def _(chunk):
+        for k in range(5):
+            node = chunk * 5 + k
+            p = state_ref[node]
+            state_ref[node] = p + MACH * state_ref[NODES + node]
+            state_ref[4 * NODES + node] -= p
+
+    pack_faces(state_ref, far, near, az_far, az_near)
+
+
+def pack_faces(state_ref, far, near, az_far, az_near):
     pack_far(state_ref, far)
-    pack_near(state_ref, (near_a, near_b))
+    pack_near(state_ref, near)
     pack_az(state_ref, az_far, az_near)
 
 
 def finish_first_kernel(
-    scale, state_in, source_ref, far, near_a, near_b, az_far, az_near, state_ref, *faces
+    scale, state_in, source_ref, far, near, az_far, az_near, state_ref, *faces
 ):
     add_far(state_ref, far, scale)
-    add_near(state_ref, (near_a, near_b), scale)
+    add_near(state_ref, near, scale)
     add_az(state_ref, az_far, az_near, scale)
 
     for node in range(3 * NODES):
-        state_ref[NODES + node] += scale * source_ref[pl.ds(node * ROWS, ROWS), :]
+        value = scale * source_ref[pl.ds(node * ROWS, ROWS), :]
+        state_ref[NODES + node] += value
+        if node < NODES:
+            state_ref[node] += MACH * value
 
     pack_faces(state_ref, *faces)
 
@@ -345,17 +359,15 @@
     pack_far(state_ref, far_out)
 
 
-def finish_near_kernel(
-    scale, state_in, near_a, near_b, state_ref, near_a_out, near_b_out, az_far_out, az_near_out
-):
-    add_near(state_ref, (near_a, near_b), scale)
-    pack_near(state_ref, (near_a_out, near_b_out))
+def finish_near_kernel(scale, state_in, near, state_ref, near_out, az_far_out, az_near_out):
+    add_near(state_ref, near, scale)
+    pack_near(state_ref, near_out)
     pack_az(state_ref, az_far_out, az_near_out)
 
 
 def last_far_kernel(weight, state_in, far, az_far, az_near, state_ref, out_hbm, sems):
-    add_az(state_ref, az_far, az_near, weight)
-    add_far(state_ref, far, weight)
+    add_az(state_ref, az_far, az_near, weight, final=True)
+    add_far(state_ref, far, weight, final=True)
     first = 25 * (lax.axis_index("ax") % 2)
     copies = []
     for f in range(FIELDS):
@@ -367,8 +379,8 @@
         copy.wait()
 
 
-def last_near_kernel(weight, state_in, out_in, near_a, near_b, state_ref, out_hbm, sems):
-    add_near(state_ref, (near_a, near_b), weight)
+def last_near_kernel(weight, state_in, out_in, near, state_ref, out_hbm, sems):
+    add_near(state_ref, near, weight, final=True)
     first = 100 - 100 * (lax.axis_index("ax") % 2)
     copies = []
     for f in range(FIELDS):
@@ -507,10 +519,10 @@
 
 STATE = (FIELDS * NODES, ROWS, LANES)
 AX_FACE = (FIELDS * 25, 4, LANES)
-NEAR_PIECES = ((65, 4, LANES), (60, 4, LANES))
-AZ_FACE = (132, 2, LANES)
-
-
+AZ_FACE = (FIELDS * 25, 2, LANES)
+
+
+LONG = pl.CostEstimate(flops=10**11, bytes_accessed=10**9, transcendentals=0)
 IN_VMEM = pl.BlockSpec(memory_space=pltpu.VMEM)
 IN_HBM = pl.BlockSpec(memory_space=pltpu.HBM)
 
@@ -519,7 +531,7 @@
     return pltpu.with_memory_space_constraint(x, pltpu.HBM)
 
 
-def call(kernel, out_shape, in_specs, out_specs=IN_VMEM, aliases=None, scratch=()):
+def call(kernel, out_shape, in_specs, out_specs=IN_VMEM, aliases=None, scratch=(), cost=None):
     if not isinstance(out_specs, list):
         out_specs = jax.tree.map(lambda _: out_specs, out_shape)
     return pl.pallas_call(
@@ -529,6 +541,7 @@
         out_specs=out_specs,
         scratch_shapes=scratch,
         input_output_aliases=aliases or {},
+        cost_estimate=cost,
         compiler_params=pltpu.CompilerParams(vmem_limit_bytes=VMEM_BYTES),
     )
 
@@ -540,7 +553,7 @@
         pairs[i % 2].extend([(i, i + 1), (i + 1, i)])
     return (
         None if far is None else lax.ppermute(far, "ax", pairs[1]),
-        None if near is None else [lax.ppermute(part, "ax", pairs[0]) for part in near],
+        None if near is None else lax.ppermute(near, "ax", pairs[0]),
     )
 
 
@@ -560,7 +573,7 @@
     f32, bf16 = jnp.float32, jnp.bfloat16
 
     state = acoustic_state.reshape(STATE)
-    face_shapes = [jax.ShapeDtypeStruct(s, bf16) for s in (AX_FACE, *NEAR_PIECES, AZ_FACE, AZ_FACE)]
+    face_shapes = [jax.ShapeDtypeStruct(s, bf16) for s in (AX_FACE, AX_FACE, AZ_FACE, AZ_FACE)]
     vmem_state = pltpu.VMEM(STATE, f32)
     source_shape = (3 * NODES * ROWS, LANES)
 
@@ -589,7 +602,7 @@
     )
     routed = lax.all_to_all(buffer, ("ax", "az"), split_axis=0, concat_axis=0, tiled=True)
 
-    state, far, *near, az_far, az_near = call(
+    state, far, near, az_far, az_near = call(
         load_kernel,
         [vmem_state] + face_shapes,
         [IN_HBM],
@@ -599,12 +612,12 @@
     az_far, az_near = turn(az_far, az_near)
     moved = call(functools.partial(volume_first_kernel, STEP_SCALES[0]), vmem_state, 1)(state)
     source = call(source_kernel, pltpu.VMEM(source_shape, f32), 1)(routed)
-    rate, far, *near, az_far, az_near = call(
+    rate, far, near, az_far, az_near = call(
         functools.partial(finish_first_kernel, STEP_SCALES[0]),
         [vmem_state] + face_shapes,
-        7,
+        6,
         aliases={0: 0},
-    )(moved, source, far, *near, az_far, az_near)
+    )(moved, source, far, near, az_far, az_near)
     far, near = swap(far, near)
     az_far, az_near = turn(az_far, az_near)
     moved, total, source = call(
@@ -621,14 +634,15 @@
             [vmem_state, face_shapes[0]],
             4,
             aliases={0: 0},
+            cost=LONG,
         )(moved, far, az_far, az_near)
         far, _ = swap(far, None)
-        rate, *near, az_far, az_near = call(
+        rate, near, az_far, az_near = call(
             functools.partial(finish_near_kernel, scale),
             [vmem_state] + face_shapes[1:],
-            3,
+            2,
             aliases={0: 0},
-        )(rate, *near)
+        )(rate, near)
         _, near = swap(None, near)
         az_far, az_near = turn(az_far, az_near)
         if scale == STEP_SCALES[1]:
@@ -649,16 +663,17 @@
         4,
         [IN_VMEM, IN_HBM],
         aliases={0: 0},
+        cost=LONG,
         scratch=[pltpu.SemaphoreType.DMA((FIELDS,))],
     )(total, far, az_far, az_near)
     _, new_state = call(
         functools.partial(last_near_kernel, STEP_SCALES[3]),
         [vmem_state, hbm_state],
-        [IN_VMEM, IN_HBM, IN_VMEM, IN_VMEM],
+        [IN_VMEM, IN_HBM, IN_VMEM],
         [IN_VMEM, IN_HBM],
         aliases={0: 0, 1: 1},
         scratch=[pltpu.SemaphoreType.DMA((FIELDS,))],
-    )(total, partial, *near)
+    )(total, partial, near)
     shape = acoustic_state.shape
     return new_state.reshape(shape), source.reshape((3,) + shape[1:])
 

time: 61.4 us -> 60 us (0.977)
  starting transfers between devices: 30.8 us -> 29.3 us
    ppermute x4, starting transfers between devices: 3.49 us -> 2.47 us  [turn(): lax.ppermute(far, 'az', pairs[1])]
    ppermute x8 -> x4, starting transfers between devices: 14.2 us -> 13.2 us  [swap(): lax.ppermute(near, 'ax', pairs[0])]
    ppermute x8 -> x4, waiting for transfers between devices: 2.48 us -> 2.98 us  [swap(): lax.ppermute(near, 'ax', pairs[0])]
  transfers between devices with their start and end apart: 21 -> 17, of which waited for: 4 -> 3; matrix products, arithmetic and copies ran while one was open for 0% -> 0% of each run, Pallas kernels for 25% -> 25%
where the time goes in v1:
time: 60 us; the launch traced here: 59.7 us
  starting transfers between devices  29.3 us (49%)
  Pallas kernels  21 us (35%)
  waiting for transfers between devices  7.08 us (12%)
  local copies, waits for them, and re-layouts  1.47 us (2%)
  between operations  0.88 us (1%)
    ppermute x4, starting transfers between devices, swap(): lax.ppermute(near, 'ax', pairs[0])  13.2 us
    all_to_all x1, starting transfers between devices, body(): lax.all_to_all(buffer, ('ax', 'az'), split_axis=0, concat_axis=0, tiled=T...  7.3 us
    all_to_all x1, waiting for transfers between devices, body(): lax.all_to_all(buffer, ('ax', 'az'), split_axis=0, concat_axis=0, tiled=T...  4.06 us
    pallas_call x1, Pallas kernels, body(): call(functools.partial(contribution_kernel, capacity, devices), pltpu.HBM...  3.7 us
    ppermute x4, starting transfers between devices, turn(): lax.ppermute(near, 'az', pairs[0])  3.64 us
    ppermute x4, waiting for transfers between devices, swap(): lax.ppermute(near, 'ax', pairs[0])  2.98 us
    pallas_call x1, Pallas kernels, body(): call(load_kernel, [vmem_state] + face_shapes, [IN_HBM], scratch=[pltpu.Se...  2.95 us
    ppermute x4, starting transfers between devices, swap(): lax.ppermute(far, 'ax', pairs[1])  2.68 us
  transfers between devices with their start and end apart: 17, of which 3 were waited for; matrix products, arithmetic and copies ran while one was open for 0% of the time, Pallas kernels for 25%

profile of v1, /device:TPU:0, one launch (start us, length us, event | category | flops | bytes accessed | tf_op | source)
XLA Modules:
  0.0 59.7 jit_solution(6542141779360570481)
XLA Ops:
  0.6 3.7 %shard_map.79 = s16[768,384]{1,0:T(8,128)(2,1)} custom-call(bf16[3,256,512]{2,1,0:T(8,128)(2,1)} %bitcast.14, s32[1,256]{1,0:T(1,128)} %bitcast.16, s32[1,256]{1,0:T(1,128)} %bitcast.17, s32[1,256]{1,0:T(1,128)} %bitcast.18, bf16[125,2,512]{2,1,0:T(2,128)(2,1)} %bitcast.15), custom_call_target="tpu_custom_call" | custom-call | tf_op jit(solution)/shard_map/pallas_call | solution.py:580
  4.3 7.3 %all-to-all-start = ((s16[32,24,384]{2,1,0:T(8,128)(2,1)}), s16[32,24,384]{2,1,0:T(8,128)(2,1)S(1)}, u32[]{:S(2)}, u32[]{:S(2)}) async-start(s16[32,24,384]{2,1,0:T(8,128)(2,1)} %bitcast.13), calls=%async_computation | async-start | bytes 1179648 | tf_op jit(solution)/shard_map/all_to_all | solution.py:603
  11.7 2.9 %shard_map.77 = (f32[625,8,128]{2,1,0:T(8,128)S(1)}, bf16[125,4,128]{2,1,0:T(4,128)(2,1)}, bf16[125,4,128]{2,1,0:T(4,128)(2,1)}, bf16[125,2,128]{2,1,0:T(2,128)(2,1)}, bf16[125,2,128]{2,1,0:T(2,128)(2,1)}) custom-call(f32[625,8,128]{2,1,0:T(8,128)} %bitcast.11), custom_call_target="tpu_custom_call" | custom-call | tf_op jit(solution)/shard_map/pallas_call | solution.py:605
  14.6 0.7 %collective-permute-start = (bf16[125,4,128]{2,1,0:T(4,128)(2,1)}, bf16[125,4,128]{2,1,0:T(4,128)(2,1)S(1)}, u32[]{:S(2)}, u32[]{:S(2)}) collective-permute-start(bf16[125,4,128]{2,1,0:T(4,128)(2,1)} %get-tuple-element.33), channel_id=1, source_target_pairs={{4,8},{8,4},{12,16},{16,12},{20,24},{24,20},{5,9},{9,5},{13,17},{1... | collective-permute-start | bytes 384008 | tf_op jit(solution)/shard_map/ppermute | solution.py:555
  15.3 4.5 %collective-permute-start.1 = (bf16[125,4,128]{2,1,0:T(4,128)(2,1)}, bf16[125,4,128]{2,1,0:T(4,128)(2,1)S(1)}, u32[]{:S(2)}, u32[]{:S(2)}) collective-permute-start(bf16[125,4,128]{2,1,0:T(4,128)(2,1)} %get-tuple-element.34), channel_id=1, source_target_pairs={{0,4},{4,0},{8,12},{12,8},{16,20},{20,16},{24,28},{28,24},{1,5},{5... | collective-permute-start | bytes 384008 | tf_op jit(solution)/shard_map/ppermute | solution.py:556
  19.8 0.7 %collective-permute-start.2 = (bf16[125,2,128]{2,1,0:T(2,128)(2,1)}, bf16[125,2,128]{2,1,0:T(2,128)(2,1)S(1)}, u32[]{:S(2)}, u32[]{:S(2)}) collective-permute-start(bf16[125,2,128]{2,1,0:T(2,128)(2,1)} %get-tuple-element.35), channel_id=1, source_target_pairs={{1,2},{2,1},{3,0},{0,3},{5,6},{6,5},{7,4},{4,7},{9,10},{10,9},{11,... | collective-permute-start | bytes 192008 | tf_op jit(solution)/shard_map/ppermute | solution.py:565
  20.5 0.9 %collective-permute-start.3 = (bf16[125,2,128]{2,1,0:T(2,128)(2,1)}, bf16[125,2,128]{2,1,0:T(2,128)(2,1)S(1)}, u32[]{:S(2)}, u32[]{:S(2)}) collective-permute-start(bf16[125,2,128]{2,1,0:T(2,128)(2,1)} %get-tuple-element.36), channel_id=1, source_target_pairs={{0,1},{1,0},{2,3},{3,2},{4,5},{5,4},{6,7},{7,6},{8,9},{9,8},{10,11... | collective-permute-start | bytes 192008 | tf_op jit(solution)/shard_map/ppermute | solution.py:565
  21.4 1.6 %shard_map.78.state_in = f32[625,8,128]{2,1,0:T(8,128)S(1)} custom-call(f32[625,8,128]{2,1,0:T(8,128)S(1)} %get-tuple-element.32.state_ref.sum_in), custom_call_target="tpu_custom_call" | custom-call | tf_op jit(solution)/shard_map/pallas_call | solution.py:613
  23.0 0.0 copy-start
  23.0 1.5 %copy-done = f32[625,8,128]{2,1,0:T(8,128)} copy-done((f32[625,8,128]{2,1,0:T(8,128)}, f32[625,8,128]{2,1,0:T(8,128)S(1)}, u32[]{:S(2)}) %copy-start) | copy-done | bytes 2560024
  24.5 4.1 %all-to-all-done = s16[32,24,384]{2,1,0:T(8,128)(2,1)S(1)} async-done(((s16[32,24,384]{2,1,0:T(8,128)(2,1)}), s16[32,24,384]{2,1,0:T(8,128)(2,1)S(1)}, u32[]{:S(2)}, u32[]{:S(2)}) %all-to-all-start) | async-done | bytes 589856 | tf_op jit(solution)/shard_map/all_to_all | solution.py:603
  28.5 1.7 %shard_map.80.source_ref = f32[3000,128]{1,0:T(8,128)S(1)} custom-call(s16[768,384]{1,0:T(8,128)(2,1)S(1)} %bitcast.10), custom_call_target="tpu_custom_call" | custom-call | tf_op jit(solution)/shard_map/pallas_call | solution.py:614
  30.2 0.0 copy-start.1
  30.3 0.0 collective-permute-done.2.az_far
  30.3 0.0 collective-permute-done.3.az_near
  30.3 0.0 collective-permute-done.far
  30.3 0.0 collective-permute-done.1.near
  30.3 1.1 %shard_map.81 = (f32[625,8,128]{2,1,0:T(8,128)S(1)}, bf16[125,4,128]{2,1,0:T(4,128)(2,1)S(1)}, bf16[125,4,128]{2,1,0:T(4,128)(2,1)S(1)}, bf16[125,2,128]{2,1,0:T(2,128)(2,1)S(1)}, bf16[125,2,128]{2,1,0:T(2,128)(2,1)S(1)}) custom-call(f32[625,8,128]{2,1,0:T(8,128)S(1)} %shard_map.78.state_in, ...), custom_call_target="tpu_custom_call", output_to_operand_aliasing={{0}: (0, {})} | custom-call | tf_op jit(solution)/shard_map/pallas_call | solution.py:615
  31.5 0.7 %collective-permute-start.4 = (bf16[125,4,128]{2,1,0:T(4,128)(2,1)S(1)}, bf16[125,4,128]{2,1,0:T(4,128)(2,1)S(1)}, u32[]{:S(2)}, u32[]{:S(2)}) collective-permute-start(bf16[125,4,128]{2,1,0:T(4,128)(2,1)S(1)} %get-tuple-element.39), channel_id=1, source_target_pairs={{4,8},{8,4},{12,16},{16,12},{20,24},{24,20},{5,9},{9,5},{13,17},{1... | collective-permute-start | bytes 384008 | tf_op jit(solution)/shard_map/ppermute | solution.py:555
  32.1 1.0 %collective-permute-start.5 = (bf16[125,2,128]{2,1,0:T(2,128)(2,1)S(1)}, bf16[125,2,128]{2,1,0:T(2,128)(2,1)S(1)}, u32[]{:S(2)}, u32[]{:S(2)}) collective-permute-start(bf16[125,2,128]{2,1,0:T(2,128)(2,1)S(1)} %get-tuple-element.40), channel_id=1, source_target_pairs={{1,2},{2,1},{3,0},{0,3},{5,6},{6,5},{7,4},{4,7},{9,10},{10,9},{11,... | collective-permute-start | bytes 192008 | tf_op jit(solution)/shard_map/ppermute | solution.py:565
  33.1 0.6 %collective-permute-start.6 = (bf16[125,2,128]{2,1,0:T(2,128)(2,1)S(1)}, bf16[125,2,128]{2,1,0:T(2,128)(2,1)S(1)}, u32[]{:S(2)}, u32[]{:S(2)}) collective-permute-start(bf16[125,2,128]{2,1,0:T(2,128)(2,1)S(1)} %get-tuple-element.41), channel_id=1, source_target_pairs={{0,1},{1,0},{2,3},{3,2},{4,5},{5,4},{6,7},{7,6},{8,9},{9,8},{10,11... | collective-permute-start | bytes 192008 | tf_op jit(solution)/shard_map/ppermute | solution.py:565
  33.8 1.7 %shard_map.82 = (f32[625,8,128]{2,1,0:T(8,128)S(1)}, f32[625,8,128]{2,1,0:T(8,128)S(1)}, f32[3000,128]{1,0:T(8,128)}) custom-call(f32[625,8,128]{2,1,0:T(8,128)S(1)} %get-tuple-element.37.state_ref, f32[625,8,128]{2,1,0:T(8,128)S(1)} %copy-done.1, f32[3000,128]{1,0:T(8,128)S(1)} %shard_map.80.source_ref), custom_call_target="tpu_custom_call" | custom-call | tf_op jit(solution)/shard_map/pallas_call | solution.py:623
  35.5 3.1 %collective-permute-start.7 = (bf16[125,4,128]{2,1,0:T(4,128)(2,1)S(1)}, bf16[125,4,128]{2,1,0:T(4,128)(2,1)S(1)}, u32[]{:S(2)}, u32[]{:S(2)}) collective-permute-start(bf16[125,4,128]{2,1,0:T(4,128)(2,1)S(1)} %get-tuple-element.43), channel_id=1, source_target_pairs={{0,4},{4,0},{8,12},{12,8},{16,20},{20,16},{24,28},{28,24},{1,5},{5... | collective-permute-start | bytes 384008 | tf_op jit(solution)/shard_map/ppermute | solution.py:556
  38.6 0.0 collective-permute-done.5.az_far
  38.6 0.0 collective-permute-done.6.az_near
  38.6 0.0 collective-permute-done.4.far
  38.6 0.5 shard_map.83
  39.2 0.7 %collective-permute-start.8 = (bf16[125,4,128]{2,1,0:T(4,128)(2,1)S(1)}, bf16[125,4,128]{2,1,0:T(4,128)(2,1)S(1)}, u32[]{:S(2)}, u32[]{:S(2)}) collective-permute-start(bf16[125,4,128]{2,1,0:T(4,128)(2,1)S(1)} %get-tuple-element.47), channel_id=1, source_target_pairs={{4,8},{8,4},{12,16},{16,12},{20,24},{24,20},{5,9},{9,5},{13,17},{1... | collective-permute-start | bytes 384008 | tf_op jit(solution)/shard_map/ppermute | solution.py:555
  39.8 2.4 %collective-permute-done.7.near = bf16[125,4,128]{2,1,0:T(4,128)(2,1)S(1)} collective-permute-done((bf16[125,4,128]{2,1,0:T(4,128)(2,1)S(1)}, bf16[125,4,128]{2,1,0:T(4,128)(2,1)S(1)}, u32[]{:S(2)}, u32[]{:S(2)}) %collective-permute-start.7) | collective-permute-done | bytes 128032 | tf_op jit(solution)/shard_map/ppermute | solution.py:556
  42.2 0.4 shard_map.84
  42.6 0.5 collective-permute-start.9
  43.1 1.0 %collective-permute-start.10 = (bf16[125,2,128]{2,1,0:T(2,128)(2,1)S(1)}, bf16[125,2,128]{2,1,0:T(2,128)(2,1)S(1)}, u32[]{:S(2)}, u32[]{:S(2)}) collective-permute-start(bf16[125,2,128]{2,1,0:T(2,128)(2,1)S(1)} %get-tuple-element.49), channel_id=1, source_target_pairs={{0,1},{1,0},{2,3},{3,2},{4,5},{5,4},{6,7},{7,6},{8,9},{9,8},{10,11... | collective-permute-start | bytes 192008 | tf_op jit(solution)/shard_map/ppermute | solution.py:565
  44.2 2.0 %collective-permute-start.11 = (bf16[125,4,128]{2,1,0:T(4,128)(2,1)S(1)}, bf16[125,4,128]{2,1,0:T(4,128)(2,1)S(1)}, u32[]{:S(2)}, u32[]{:S(2)}) collective-permute-start(bf16[125,4,128]{2,1,0:T(4,128)(2,1)S(1)} %get-tuple-element.51), channel_id=1, source_target_pairs={{0,4},{4,0},{8,12},{12,8},{16,20},{20,16},{24,28},{28,24},{1,5},{5... | collective-permute-start | bytes 384008 | tf_op jit(solution)/shard_map/ppermute | solution.py:556
  46.2 1.8 %shard_map.85 = (f32[625,8,128]{2,1,0:T(8,128)S(1)}, f32[625,8,128]{2,1,0:T(8,128)S(1)}) custom-call(f32[625,8,128]{2,1,0:T(8,128)S(1)} %get-tuple-element.44.state_ref, f32[625,8,128]{2,1,0:T(8,128)S(1)} %get-tuple-element.45.sum_in), custom_call_target="tpu_custom_call" | custom-call | tf_op jit(solution)/shard_map/pallas_call | solution.py:649
  47.9 0.0 collective-permute-done.9.az_far
  48.0 0.5 shard_map.86
  48.5 0.7 %collective-permute-start.12 = (bf16[125,4,128]{2,1,0:T(4,128)(2,1)S(1)}, bf16[125,4,128]{2,1,0:T(4,128)(2,1)S(1)}, u32[]{:S(2)}, u32[]{:S(2)}) collective-permute-start(bf16[125,4,128]{2,1,0:T(4,128)(2,1)S(1)} %get-tuple-element.54), channel_id=1, source_target_pairs={{4,8},{8,4},{12,16},{16,12},{20,24},{24,20},{5,9},{9,5},{13,17},{1... | collective-permute-start | bytes 384008 | tf_op jit(solution)/shard_map/ppermute | solution.py:555
  49.2 0.6 collective-permute-done.11.near
  49.8 0.4 shard_map.87
  50.1 0.3 collective-permute-start.13
  50.4 1.0 %collective-permute-start.14 = (bf16[125,2,128]{2,1,0:T(2,128)(2,1)S(1)}, bf16[125,2,128]{2,1,0:T(2,128)(2,1)S(1)}, u32[]{:S(2)}, u32[]{:S(2)}) collective-permute-start(bf16[125,2,128]{2,1,0:T(2,128)(2,1)S(1)} %get-tuple-element.56), channel_id=1, source_target_pairs={{0,1},{1,0},{2,3},{3,2},{4,5},{5,4},{6,7},{7,6},{8,9},{9,8},{10,11... | collective-permute-start | bytes 192008 | tf_op jit(solution)/shard_map/ppermute | solution.py:565
  51.4 3.5 %collective-permute-start.15 = (bf16[125,4,128]{2,1,0:T(4,128)(2,1)S(1)}, bf16[125,4,128]{2,1,0:T(4,128)(2,1)S(1)}, u32[]{:S(2)}, u32[]{:S(2)}) collective-permute-start(bf16[125,4,128]{2,1,0:T(4,128)(2,1)S(1)} %get-tuple-element.59), channel_id=1, source_target_pairs={{0,4},{4,0},{8,12},{12,8},{16,20},{20,16},{24,28},{28,24},{1,5},{5... | collective-permute-start | bytes 384008 | tf_op jit(solution)/shard_map/ppermute | solution.py:556
  55.0 1.9 %shard_map.88.state_in = f32[625,8,128]{2,1,0:T(8,128)S(1)} custom-call(f32[625,8,128]{2,1,0:T(8,128)S(1)} %get-tuple-element.52.state_ref, f32[625,8,128]{2,1,0:T(8,128)S(1)} %get-tuple-element.53.sum_in), custom_call_target="tpu_custom_call" | custom-call | tf_op jit(solution)/shard_map/pallas_call | solution.py:653
  56.9 0.0 collective-permute-done.13.az_far
  56.9 0.0 collective-permute-done.12.far
  56.9 1.8 %shard_map.89 = (f32[625,8,128]{2,1,0:T(8,128)S(1)}, f32[625,8,128]{2,1,0:T(8,128)}) custom-call(f32[625,8,128]{2,1,0:T(8,128)S(1)} %shard_map.88.state_in, bf16[125,4,128]{2,1,0:T(4,128)(2,1)S(1)} %collective-permute-done.12.far, bf16[125,2,128]{2,1,0:T(2,128)(2,1)S(1)} %collective-permute-done.13.az_far, ...), custom_call_target="tpu_custom_call", output_to_operand_aliasing={{0}: (0, {})} | custom-call | flops 99999997952 | bytes 1000000000 | tf_op jit(solution)/shard_map/pallas_call | solution.py:660
  58.8 0.0 collective-permute-done.15.near
  58.8 1.0 %shard_map.90 = (f32[625,8,128]{2,1,0:T(8,128)S(1)}, f32[625,8,128]{2,1,0:T(8,128)}) custom-call(f32[625,8,128]{2,1,0:T(8,128)S(1)} %get-tuple-element.57.state_in, f32[625,8,128]{2,1,0:T(8,128)} %get-tuple-element.58.out_in, bf16[125,4,128]{2,1,0:T(4,128)(2,1)S(1)} %collective-permute-done.15.near), custom_call_target="tpu_custom_call", output_to_operand_aliasing={{0}: (0, {}), {1}: (1, {})} | custom-call | tf_op jit(solution)/shard_map/pallas_call | solution.py:669
  (4 shorter events, 0.0 us)
Async XLA Ops:
  4.3 24.2 %all-to-all-start = ((s16[32,24,384]{2,1,0:T(8,128)(2,1)}), s16[32,24,384]{2,1,0:T(8,128)(2,1)S(1)}, u32[]{:S(2)}, u32[]{:S(2)}) async-start(s16[32,24,384]{2,1,0:T(8,128)(2,1)} %bitcast.13), calls=%async_computation | async-start | bytes 1179648 | tf_op jit(solution)/shard_map/all_to_all | solution.py:603
  14.6 15.7 %collective-permute-start = (bf16[125,4,128]{2,1,0:T(4,128)(2,1)}, bf16[125,4,128]{2,1,0:T(4,128)(2,1)S(1)}, u32[]{:S(2)}, u32[]{:S(2)}) collective-permute-start(bf16[125,4,128]{2,1,0:T(4,128)(2,1)} %get-tuple-element.33), channel_id=1, source_target_pairs={{4,8},{8,4},{12,16},{16,12},{20,24},{24,20},{5,9},{9,5},{13,17},{1... | collective-permute-start | bytes 384008 | tf_op jit(solution)/shard_map/ppermute | solution.py:555
  15.3 15.0 %collective-permute-start.1 = (bf16[125,4,128]{2,1,0:T(4,128)(2,1)}, bf16[125,4,128]{2,1,0:T(4,128)(2,1)S(1)}, u32[]{:S(2)}, u32[]{:S(2)}) collective-permute-start(bf16[125,4,128]{2,1,0:T(4,128)(2,1)} %get-tuple-element.34), channel_id=1, source_target_pairs={{0,4},{4,0},{8,12},{12,8},{16,20},{20,16},{24,28},{28,24},{1,5},{5... | collective-permute-start | bytes 384008 | tf_op jit(solution)/shard_map/ppermute | solution.py:556
  19.8 10.4 %collective-permute-start.2 = (bf16[125,2,128]{2,1,0:T(2,128)(2,1)}, bf16[125,2,128]{2,1,0:T(2,128)(2,1)S(1)}, u32[]{:S(2)}, u32[]{:S(2)}) collective-permute-start(bf16[125,2,128]{2,1,0:T(2,128)(2,1)} %get-tuple-element.35), channel_id=1, source_target_pairs={{1,2},{2,1},{3,0},{0,3},{5,6},{6,5},{7,4},{4,7},{9,10},{10,9},{11,... | collective-permute-start | bytes 192008 | tf_op jit(solution)/shard_map/ppermute | solution.py:565
  20.5 9.8 %collective-permute-start.3 = (bf16[125,2,128]{2,1,0:T(2,128)(2,1)}, bf16[125,2,128]{2,1,0:T(2,128)(2,1)S(1)}, u32[]{:S(2)}, u32[]{:S(2)}) collective-permute-start(bf16[125,2,128]{2,1,0:T(2,128)(2,1)} %get-tuple-element.36), channel_id=1, source_target_pairs={{0,1},{1,0},{2,3},{3,2},{4,5},{5,4},{6,7},{7,6},{8,9},{9,8},{10,11... | collective-permute-start | bytes 192008 | tf_op jit(solution)/shard_map/ppermute | solution.py:565
  23.0 1.5 %copy-start = (f32[625,8,128]{2,1,0:T(8,128)}, f32[625,8,128]{2,1,0:T(8,128)S(1)}, u32[]{:S(2)}) copy-start(f32[625,8,128]{2,1,0:T(8,128)S(1)} %get-tuple-element.32.state_ref.sum_in) | copy-start | bytes 7680004
  30.2 3.5 %copy-start.1 = (f32[625,8,128]{2,1,0:T(8,128)S(1)}, f32[625,8,128]{2,1,0:T(8,128)}, u32[]{:S(2)}) copy-start(f32[625,8,128]{2,1,0:T(8,128)} %copy-done) | copy-start | bytes 7680004
  31.5 7.2 %collective-permute-start.4 = (bf16[125,4,128]{2,1,0:T(4,128)(2,1)S(1)}, bf16[125,4,128]{2,1,0:T(4,128)(2,1)S(1)}, u32[]{:S(2)}, u32[]{:S(2)}) collective-permute-start(bf16[125,4,128]{2,1,0:T(4,128)(2,1)S(1)} %get-tuple-element.39), channel_id=1, source_target_pairs={{4,8},{8,4},{12,16},{16,12},{20,24},{24,20},{5,9},{9,5},{13,17},{1... | collective-permute-start | bytes 384008 | tf_op jit(solution)/shard_map/ppermute | solution.py:555
  32.1 6.5 %collective-permute-start.5 = (bf16[125,2,128]{2,1,0:T(2,128)(2,1)S(1)}, bf16[125,2,128]{2,1,0:T(2,128)(2,1)S(1)}, u32[]{:S(2)}, u32[]{:S(2)}) collective-permute-start(bf16[125,2,128]{2,1,0:T(2,128)(2,1)S(1)} %get-tuple-element.40), channel_id=1, source_target_pairs={{1,2},{2,1},{3,0},{0,3},{5,6},{6,5},{7,4},{4,7},{9,10},{10,9},{11,... | collective-permute-start | bytes 192008 | tf_op jit(solution)/shard_map/ppermute | solution.py:565
  33.1 5.5 %collective-permute-start.6 = (bf16[125,2,128]{2,1,0:T(2,128)(2,1)S(1)}, bf16[125,2,128]{2,1,0:T(2,128)(2,1)S(1)}, u32[]{:S(2)}, u32[]{:S(2)}) collective-permute-start(bf16[125,2,128]{2,1,0:T(2,128)(2,1)S(1)} %get-tuple-element.41), channel_id=1, source_target_pairs={{0,1},{1,0},{2,3},{3,2},{4,5},{5,4},{6,7},{7,6},{8,9},{9,8},{10,11... | collective-permute-start | bytes 192008 | tf_op jit(solution)/shard_map/ppermute | solution.py:565
  35.5 6.7 %collective-permute-start.7 = (bf16[125,4,128]{2,1,0:T(4,128)(2,1)S(1)}, bf16[125,4,128]{2,1,0:T(4,128)(2,1)S(1)}, u32[]{:S(2)}, u32[]{:S(2)}) collective-permute-start(bf16[125,4,128]{2,1,0:T(4,128)(2,1)S(1)} %get-tuple-element.43), channel_id=1, source_target_pairs={{0,4},{4,0},{8,12},{12,8},{16,20},{20,16},{24,28},{28,24},{1,5},{5... | collective-permute-start | bytes 384008 | tf_op jit(solution)/shard_map/ppermute | solution.py:556
  39.2 8.8 %collective-permute-start.8 = (bf16[125,4,128]{2,1,0:T(4,128)(2,1)S(1)}, bf16[125,4,128]{2,1,0:T(4,128)(2,1)S(1)}, u32[]{:S(2)}, u32[]{:S(2)}) collective-permute-start(bf16[125,4,128]{2,1,0:T(4,128)(2,1)S(1)} %get-tuple-element.47), channel_id=1, source_target_pairs={{4,8},{8,4},{12,16},{16,12},{20,24},{24,20},{5,9},{9,5},{13,17},{1... | collective-permute-start | bytes 384008 | tf_op jit(solution)/shard_map/ppermute | solution.py:555
  42.6 5.4 %collective-permute-start.9 = (bf16[125,2,128]{2,1,0:T(2,128)(2,1)S(1)}, bf16[125,2,128]{2,1,0:T(2,128)(2,1)S(1)}, u32[]{:S(2)}, u32[]{:S(2)}) collective-permute-start(bf16[125,2,128]{2,1,0:T(2,128)(2,1)S(1)} %get-tuple-element.48), channel_id=1, source_target_pairs={{1,2},{2,1},{3,0},{0,3},{5,6},{6,5},{7,4},{4,7},{9,10},{10,9},{11,... | collective-permute-start | bytes 192008 | tf_op jit(solution)/shard_map/ppermute | solution.py:565
  43.1 4.8 %collective-permute-start.10 = (bf16[125,2,128]{2,1,0:T(2,128)(2,1)S(1)}, bf16[125,2,128]{2,1,0:T(2,128)(2,1)S(1)}, u32[]{:S(2)}, u32[]{:S(2)}) collective-permute-start(bf16[125,2,128]{2,1,0:T(2,128)(2,1)S(1)} %get-tuple-element.49), channel_id=1, source_target_pairs={{0,1},{1,0},{2,3},{3,2},{4,5},{5,4},{6,7},{7,6},{8,9},{9,8},{10,11... | collective-permute-start | bytes 192008 | tf_op jit(solution)/shard_map/ppermute | solution.py:565
  44.2 5.6 %collective-permute-start.11 = (bf16[125,4,128]{2,1,0:T(4,128)(2,1)S(1)}, bf16[125,4,128]{2,1,0:T(4,128)(2,1)S(1)}, u32[]{:S(2)}, u32[]{:S(2)}) collective-permute-start(bf16[125,4,128]{2,1,0:T(4,128)(2,1)S(1)} %get-tuple-element.51), channel_id=1, source_target_pairs={{0,4},{4,0},{8,12},{12,8},{16,20},{20,16},{24,28},{28,24},{1,5},{5... | collective-permute-start | bytes 384008 | tf_op jit(solution)/shard_map/ppermute | solution.py:556
  48.5 8.4 %collective-permute-start.12 = (bf16[125,4,128]{2,1,0:T(4,128)(2,1)S(1)}, bf16[125,4,128]{2,1,0:T(4,128)(2,1)S(1)}, u32[]{:S(2)}, u32[]{:S(2)}) collective-permute-start(bf16[125,4,128]{2,1,0:T(4,128)(2,1)S(1)} %get-tuple-element.54), channel_id=1, source_target_pairs={{4,8},{8,4},{12,16},{16,12},{20,24},{24,20},{5,9},{9,5},{13,17},{1... | collective-permute-start | bytes 384008 | tf_op jit(solution)/shard_map/ppermute | solution.py:555
  50.1 6.8 %collective-permute-start.13 = (bf16[125,2,128]{2,1,0:T(2,128)(2,1)S(1)}, bf16[125,2,128]{2,1,0:T(2,128)(2,1)S(1)}, u32[]{:S(2)}, u32[]{:S(2)}) collective-permute-start(bf16[125,2,128]{2,1,0:T(2,128)(2,1)S(1)} %get-tuple-element.55), channel_id=1, source_target_pairs={{1,2},{2,1},{3,0},{0,3},{5,6},{6,5},{7,4},{4,7},{9,10},{10,9},{11,... | collective-permute-start | bytes 192008 | tf_op jit(solution)/shard_map/ppermute | solution.py:565
  50.4 6.5 %collective-permute-start.14 = (bf16[125,2,128]{2,1,0:T(2,128)(2,1)S(1)}, bf16[125,2,128]{2,1,0:T(2,128)(2,1)S(1)}, u32[]{:S(2)}, u32[]{:S(2)}) collective-permute-start(bf16[125,2,128]{2,1,0:T(2,128)(2,1)S(1)} %get-tuple-element.56), channel_id=1, source_target_pairs={{0,1},{1,0},{2,3},{3,2},{4,5},{5,4},{6,7},{7,6},{8,9},{9,8},{10,11... | collective-permute-start | bytes 192008 | tf_op jit(solution)/shard_map/ppermute | solution.py:565
  51.4 7.3 %collective-permute-start.15 = (bf16[125,4,128]{2,1,0:T(4,128)(2,1)S(1)}, bf16[125,4,128]{2,1,0:T(4,128)(2,1)S(1)}, u32[]{:S(2)}, u32[]{:S(2)}) collective-permute-start(bf16[125,4,128]{2,1,0:T(4,128)(2,1)S(1)} %get-tuple-element.59), channel_id=1, source_target_pairs={{0,4},{4,0},{8,12},{12,8},{16,20},{20,16},{24,28},{28,24},{1,5},{5... | collective-permute-start | bytes 384008 | tf_op jit(solution)/shard_map/ppermute | solution.py:556

commit v2 on v1

--- a/solution.py
+++ b/solution.py
@@ -267,11 +267,13 @@
 
 
 def add_az(out_ref, far, near, weight, final=False):
+    row = lax.broadcasted_iota(jnp.int32, (5, ROWS, LANES), 1)
+
     def add_side(face, at, rows, chunk, sign):
         terms = lifted(received(face, chunk), 1, sign, weight)
         for f, term in enumerate(original(terms) if final else terms):
-            for k, row in enumerate(rows):
-                out_ref[pl.ds(f * NODES + at, 5), row : row + 1, :] += term[:, k : k + 1]
+            spread = jnp.where(row == rows[1], term[:, 1:2], 0.0)
+            out_ref[pl.ds(f * NODES + at, 5)] += jnp.where(row == rows[0], term[:, 0:1], spread)
 
     def add(low, high):
         for a in range(5):
@@ -337,20 +339,27 @@
     pack_az(state_ref, az_far, az_near)
 
 
-def finish_first_kernel(
-    scale, state_in, source_ref, far, near, az_far, az_near, state_ref, *faces
-):
+def add_source(state_ref, source_ref, scale, nodes):
+    for node in nodes:
+        for c in range(3):
+            value = scale * source_ref[pl.ds((c * NODES + node) * ROWS, ROWS), :]
+            state_ref[(c + 1) * NODES + node] += value
+            if c == 0:
+                state_ref[node] += MACH * value
+
+
+def first_far_kernel(scale, state_in, source_ref, far, az_far, az_near, state_ref, far_out):
+    add_az(state_ref, az_far, az_near, scale)
     add_far(state_ref, far, scale)
+    add_source(state_ref, source_ref, scale, [*range(25), *range(100, NODES)])
+    pack_far(state_ref, far_out)
+
+
+def first_near_kernel(scale, state_in, source_ref, near, state_ref, near_out, *az_out):
     add_near(state_ref, near, scale)
-    add_az(state_ref, az_far, az_near, scale)
-
-    for node in range(3 * NODES):
-        value = scale * source_ref[pl.ds(node * ROWS, ROWS), :]
-        state_ref[NODES + node] += value
-        if node < NODES:
-            state_ref[node] += MACH * value
-
-    pack_faces(state_ref, *faces)
+    add_source(state_ref, source_ref, scale, range(25, 100))
+    pack_near(state_ref, near_out)
+    pack_az(state_ref, *az_out)
 
 
 def finish_far_kernel(scale, state_in, far, az_far, az_near, state_ref, far_out):
@@ -422,7 +431,7 @@
     tables_copy = pltpu.make_async_copy(tables_hbm, tables_ref, tables_sem.at[0])
     for copy in row_copies + [tables_copy, lamb_copy]:
         copy.start()
-    for copy in row_copies:
+    for copy in row_copies + [tables_copy, lamb_copy]:
         copy.wait()
 
     owner_row = owner_ref[...]
@@ -446,10 +455,8 @@
     slot_row = owner_row * capacity + position
     placing = (lax.broadcasted_iota(jnp.int32, (slots, flow), 0) == slot_row).astype(jnp.bfloat16)
 
-    tables_copy.wait()
     spare = jnp.zeros((LANES - NODES, lamb_ref.shape[2]), jnp.bfloat16)
     tables = jnp.concatenate([tables_ref[:, 0, :], spare, tables_ref[:, 1, :], spare], axis=0)
-    lamb_copy.wait()
     both = lax.dot_general(
         lamb_ref[...].reshape(3 * flow, lamb_ref.shape[2]),
         tables,
@@ -612,13 +619,20 @@
     az_far, az_near = turn(az_far, az_near)
     moved = call(functools.partial(volume_first_kernel, STEP_SCALES[0]), vmem_state, 1)(state)
     source = call(source_kernel, pltpu.VMEM(source_shape, f32), 1)(routed)
-    rate, far, near, az_far, az_near = call(
-        functools.partial(finish_first_kernel, STEP_SCALES[0]),
-        [vmem_state] + face_shapes,
-        6,
+    rate, far = call(
+        functools.partial(first_far_kernel, STEP_SCALES[0]),
+        [vmem_state, face_shapes[0]],
+        5,
         aliases={0: 0},
-    )(moved, source, far, near, az_far, az_near)
-    far, near = swap(far, near)
+    )(moved, source, far, az_far, az_near)
+    far, _ = swap(far, None)
+    rate, near, az_far, az_near = call(
+        functools.partial(first_near_kernel, STEP_SCALES[0]),
+        [vmem_state] + face_shapes[1:],
+        3,
+        aliases={0: 0},
+    )(rate, source, near)
+    _, near = swap(None, near)
     az_far, az_near = turn(az_far, az_near)
     moved, total, source = call(
         functools.partial(volume_and_source_kernel, STEP_SCALES[1]),

time: 60 us -> 60.3 us (level)
  transfers between devices with their start and end apart: 17 -> 17, of which waited for: 3 -> 3; matrix products, arithmetic and copies ran while one was open for 0% -> 0% of each run, Pallas kernels for 25% -> 27%
where the time goes in v2:
time: 60.3 us; the launch traced here: 60 us
  starting transfers between devices  29.4 us (49%)
  Pallas kernels  21.1 us (35%)
  waiting for transfers between devices  7.16 us (12%)
  local copies, waits for them, and re-layouts  1.47 us (2%)
  between operations  0.88 us (1%)
    ppermute x4, starting transfers between devices, swap(): lax.ppermute(near, 'ax', pairs[0])  13 us
    all_to_all x1, starting transfers between devices, body(): lax.all_to_all(buffer, ('ax', 'az'), split_axis=0, concat_axis=0, tiled=T...  7.3 us
    all_to_all x1, waiting for transfers between devices, body(): lax.all_to_all(buffer, ('ax', 'az'), split_axis=0, concat_axis=0, tiled=T...  4.04 us
    pallas_call x1, Pallas kernels, body(): call(functools.partial(contribution_kernel, capacity, devices), pltpu.HBM...  3.91 us
    ppermute x4, starting transfers between devices, turn(): lax.ppermute(near, 'az', pairs[0])  3.64 us
    ppermute x4, waiting for transfers between devices, swap(): lax.ppermute(near, 'ax', pairs[0])  3.09 us
    pallas_call x1, Pallas kernels, body(): call(load_kernel, [vmem_state] + face_shapes, [IN_HBM], scratch=[pltpu.Se...  2.97 us
    ppermute x4, starting transfers between devices, swap(): lax.ppermute(far, 'ax', pairs[1])  2.81 us
  transfers between devices with their start and end apart: 17, of which 3 were waited for; matrix products, arithmetic and copies ran while one was open for 0% of the time, Pallas kernels for 27%

profile of v2, /device:TPU:0, one launch (start us, length us, event | category | flops | bytes accessed | tf_op | source)
XLA Modules:
  0.0 60.0 jit_solution(575465032952889557)
XLA Ops:
  0.6 3.9 %shard_map.79 = s16[768,384]{1,0:T(8,128)(2,1)} custom-call(bf16[3,256,512]{2,1,0:T(8,128)(2,1)} %bitcast.14, s32[1,256]{1,0:T(1,128)} %bitcast.16, s32[1,256]{1,0:T(1,128)} %bitcast.17, s32[1,256]{1,0:T(1,128)} %bitcast.18, bf16[125,2,512]{2,1,0:T(2,128)(2,1)} %bitcast.15), custom_call_target="tpu_custom_call" | custom-call | tf_op jit(solution)/shard_map/pallas_call | solution.py:587
  4.5 7.3 %all-to-all-start = ((s16[32,24,384]{2,1,0:T(8,128)(2,1)}), s16[32,24,384]{2,1,0:T(8,128)(2,1)S(1)}, u32[]{:S(2)}, u32[]{:S(2)}) async-start(s16[32,24,384]{2,1,0:T(8,128)(2,1)} %bitcast.13), calls=%async_computation | async-start | bytes 1179648 | tf_op jit(solution)/shard_map/all_to_all | solution.py:610
  11.9 3.0 %shard_map.77 = (f32[625,8,128]{2,1,0:T(8,128)S(1)}, bf16[125,4,128]{2,1,0:T(4,128)(2,1)}, bf16[125,4,128]{2,1,0:T(4,128)(2,1)}, bf16[125,2,128]{2,1,0:T(2,128)(2,1)}, bf16[125,2,128]{2,1,0:T(2,128)(2,1)}) custom-call(f32[625,8,128]{2,1,0:T(8,128)} %bitcast.11), custom_call_target="tpu_custom_call" | custom-call | tf_op jit(solution)/shard_map/pallas_call | solution.py:612
  14.8 0.7 %collective-permute-start = (bf16[125,4,128]{2,1,0:T(4,128)(2,1)}, bf16[125,4,128]{2,1,0:T(4,128)(2,1)S(1)}, u32[]{:S(2)}, u32[]{:S(2)}) collective-permute-start(bf16[125,4,128]{2,1,0:T(4,128)(2,1)} %get-tuple-element.34), channel_id=1, source_target_pairs={{4,8},{8,4},{12,16},{16,12},{20,24},{24,20},{5,9},{9,5},{13,17},{1... | collective-permute-start | bytes 384008 | tf_op jit(solution)/shard_map/ppermute | solution.py:562
  15.5 4.5 %collective-permute-start.3 = (bf16[125,4,128]{2,1,0:T(4,128)(2,1)}, bf16[125,4,128]{2,1,0:T(4,128)(2,1)S(1)}, u32[]{:S(2)}, u32[]{:S(2)}) collective-permute-start(bf16[125,4,128]{2,1,0:T(4,128)(2,1)} %get-tuple-element.38), channel_id=1, source_target_pairs={{0,4},{4,0},{8,12},{12,8},{16,20},{20,16},{24,28},{28,24},{1,5},{5... | collective-permute-start | bytes 384008 | tf_op jit(solution)/shard_map/ppermute | solution.py:563
  20.0 0.7 %collective-permute-start.1 = (bf16[125,2,128]{2,1,0:T(2,128)(2,1)}, bf16[125,2,128]{2,1,0:T(2,128)(2,1)S(1)}, u32[]{:S(2)}, u32[]{:S(2)}) collective-permute-start(bf16[125,2,128]{2,1,0:T(2,128)(2,1)} %get-tuple-element.35), channel_id=1, source_target_pairs={{1,2},{2,1},{3,0},{0,3},{5,6},{6,5},{7,4},{4,7},{9,10},{10,9},{11,... | collective-permute-start | bytes 192008 | tf_op jit(solution)/shard_map/ppermute | solution.py:572
  20.7 0.9 %collective-permute-start.2 = (bf16[125,2,128]{2,1,0:T(2,128)(2,1)}, bf16[125,2,128]{2,1,0:T(2,128)(2,1)S(1)}, u32[]{:S(2)}, u32[]{:S(2)}) collective-permute-start(bf16[125,2,128]{2,1,0:T(2,128)(2,1)} %get-tuple-element.36), channel_id=1, source_target_pairs={{0,1},{1,0},{2,3},{3,2},{4,5},{5,4},{6,7},{7,6},{8,9},{9,8},{10,11... | collective-permute-start | bytes 192008 | tf_op jit(solution)/shard_map/ppermute | solution.py:572
  21.6 1.6 %shard_map.78.state_in = f32[625,8,128]{2,1,0:T(8,128)S(1)} custom-call(f32[625,8,128]{2,1,0:T(8,128)S(1)} %get-tuple-element.33.state_ref.sum_in), custom_call_target="tpu_custom_call" | custom-call | tf_op jit(solution)/shard_map/pallas_call | solution.py:620
  23.2 0.0 copy-start
  23.2 1.5 %copy-done = f32[625,8,128]{2,1,0:T(8,128)} copy-done((f32[625,8,128]{2,1,0:T(8,128)}, f32[625,8,128]{2,1,0:T(8,128)S(1)}, u32[]{:S(2)}) %copy-start) | copy-done | bytes 2560024
  24.7 4.0 %all-to-all-done = s16[32,24,384]{2,1,0:T(8,128)(2,1)S(1)} async-done(((s16[32,24,384]{2,1,0:T(8,128)(2,1)}), s16[32,24,384]{2,1,0:T(8,128)(2,1)S(1)}, u32[]{:S(2)}, u32[]{:S(2)}) %all-to-all-start) | async-done | bytes 589856 | tf_op jit(solution)/shard_map/all_to_all | solution.py:610
  28.7 1.7 %shard_map.80.source_ref = f32[3000,128]{1,0:T(8,128)S(1)} custom-call(s16[768,384]{1,0:T(8,128)(2,1)S(1)} %bitcast.10), custom_call_target="tpu_custom_call" | custom-call | tf_op jit(solution)/shard_map/pallas_call | solution.py:621
  30.4 0.0 collective-permute-done.1.az_far
  30.5 0.0 collective-permute-done.2.az_near
  30.5 0.0 collective-permute-done.far
  30.5 0.6 shard_map.81
  31.1 0.0 copy-start.1
  31.1 0.8 %collective-permute-start.4 = (bf16[125,4,128]{2,1,0:T(4,128)(2,1)S(1)}, bf16[125,4,128]{2,1,0:T(4,128)(2,1)S(1)}, u32[]{:S(2)}, u32[]{:S(2)}) collective-permute-start(bf16[125,4,128]{2,1,0:T(4,128)(2,1)S(1)} %get-tuple-element.41), channel_id=1, source_target_pairs={{4,8},{8,4},{12,16},{16,12},{20,24},{24,20},{5,9},{9,5},{13,17},{1... | collective-permute-start | bytes 384008 | tf_op jit(solution)/shard_map/ppermute | solution.py:562
  31.9 0.0 collective-permute-done.3.near
  31.9 0.5 shard_map.82
  32.5 1.0 %collective-permute-start.5 = (bf16[125,2,128]{2,1,0:T(2,128)(2,1)S(1)}, bf16[125,2,128]{2,1,0:T(2,128)(2,1)S(1)}, u32[]{:S(2)}, u32[]{:S(2)}) collective-permute-start(bf16[125,2,128]{2,1,0:T(2,128)(2,1)S(1)} %get-tuple-element.42), channel_id=1, source_target_pairs={{1,2},{2,1},{3,0},{0,3},{5,6},{6,5},{7,4},{4,7},{9,10},{10,9},{11,... | collective-permute-start | bytes 192008 | tf_op jit(solution)/shard_map/ppermute | solution.py:572
  33.5 0.6 %collective-permute-start.6 = (bf16[125,2,128]{2,1,0:T(2,128)(2,1)S(1)}, bf16[125,2,128]{2,1,0:T(2,128)(2,1)S(1)}, u32[]{:S(2)}, u32[]{:S(2)}) collective-permute-start(bf16[125,2,128]{2,1,0:T(2,128)(2,1)S(1)} %get-tuple-element.43), channel_id=1, source_target_pairs={{0,1},{1,0},{2,3},{3,2},{4,5},{5,4},{6,7},{7,6},{8,9},{9,8},{10,11... | collective-permute-start | bytes 192008 | tf_op jit(solution)/shard_map/ppermute | solution.py:572
  34.1 1.7 %shard_map.83 = (f32[625,8,128]{2,1,0:T(8,128)S(1)}, f32[625,8,128]{2,1,0:T(8,128)S(1)}, f32[3000,128]{1,0:T(8,128)}) custom-call(f32[625,8,128]{2,1,0:T(8,128)S(1)} %get-tuple-element.39.state_ref, f32[625,8,128]{2,1,0:T(8,128)S(1)} %copy-done.1, f32[3000,128]{1,0:T(8,128)S(1)} %shard_map.80.source_ref), custom_call_target="tpu_custom_call" | custom-call | tf_op jit(solution)/shard_map/pallas_call | solution.py:637
  35.8 3.1 %collective-permute-start.7 = (bf16[125,4,128]{2,1,0:T(4,128)(2,1)S(1)}, bf16[125,4,128]{2,1,0:T(4,128)(2,1)S(1)}, u32[]{:S(2)}, u32[]{:S(2)}) collective-permute-start(bf16[125,4,128]{2,1,0:T(4,128)(2,1)S(1)} %get-tuple-element.45), channel_id=1, source_target_pairs={{0,4},{4,0},{8,12},{12,8},{16,20},{20,16},{24,28},{28,24},{1,5},{5... | collective-permute-start | bytes 384008 | tf_op jit(solution)/shard_map/ppermute | solution.py:563
  39.0 0.0 collective-permute-done.5.az_far
  39.0 0.0 collective-permute-done.6.az_near
  39.0 0.0 collective-permute-done.4.far
  39.0 0.5 shard_map.84
  39.4 0.7 %collective-permute-start.8 = (bf16[125,4,128]{2,1,0:T(4,128)(2,1)S(1)}, bf16[125,4,128]{2,1,0:T(4,128)(2,1)S(1)}, u32[]{:S(2)}, u32[]{:S(2)}) collective-permute-start(bf16[125,4,128]{2,1,0:T(4,128)(2,1)S(1)} %get-tuple-element.49), channel_id=1, source_target_pairs={{4,8},{8,4},{12,16},{16,12},{20,24},{24,20},{5,9},{9,5},{13,17},{1... | collective-permute-start | bytes 384008 | tf_op jit(solution)/shard_map/ppermute | solution.py:562
  40.1 2.4 %collective-permute-done.7.near = bf16[125,4,128]{2,1,0:T(4,128)(2,1)S(1)} collective-permute-done((bf16[125,4,128]{2,1,0:T(4,128)(2,1)S(1)}, bf16[125,4,128]{2,1,0:T(4,128)(2,1)S(1)}, u32[]{:S(2)}, u32[]{:S(2)}) %collective-permute-start.7) | collective-permute-done | bytes 128032 | tf_op jit(solution)/shard_map/ppermute | solution.py:563
  42.6 0.4 shard_map.85
  42.9 0.5 collective-permute-start.9
  43.5 1.0 %collective-permute-start.10 = (bf16[125,2,128]{2,1,0:T(2,128)(2,1)S(1)}, bf16[125,2,128]{2,1,0:T(2,128)(2,1)S(1)}, u32[]{:S(2)}, u32[]{:S(2)}) collective-permute-start(bf16[125,2,128]{2,1,0:T(2,128)(2,1)S(1)} %get-tuple-element.51), channel_id=1, source_target_pairs={{0,1},{1,0},{2,3},{3,2},{4,5},{5,4},{6,7},{7,6},{8,9},{9,8},{10,11... | collective-permute-start | bytes 192008 | tf_op jit(solution)/shard_map/ppermute | solution.py:572
  44.5 1.8 %collective-permute-start.11 = (bf16[125,4,128]{2,1,0:T(4,128)(2,1)S(1)}, bf16[125,4,128]{2,1,0:T(4,128)(2,1)S(1)}, u32[]{:S(2)}, u32[]{:S(2)}) collective-permute-start(bf16[125,4,128]{2,1,0:T(4,128)(2,1)S(1)} %get-tuple-element.53), channel_id=1, source_target_pairs={{0,4},{4,0},{8,12},{12,8},{16,20},{20,16},{24,28},{28,24},{1,5},{5... | collective-permute-start | bytes 384008 | tf_op jit(solution)/shard_map/ppermute | solution.py:563
  46.3 1.8 %shard_map.86 = (f32[625,8,128]{2,1,0:T(8,128)S(1)}, f32[625,8,128]{2,1,0:T(8,128)S(1)}) custom-call(f32[625,8,128]{2,1,0:T(8,128)S(1)} %get-tuple-element.46.state_ref, f32[625,8,128]{2,1,0:T(8,128)S(1)} %get-tuple-element.47.sum_in), custom_call_target="tpu_custom_call" | custom-call | tf_op jit(solution)/shard_map/pallas_call | solution.py:663
  48.1 0.0 collective-permute-done.8.far
  48.1 0.5 shard_map.87
  48.6 0.7 %collective-permute-start.12 = (bf16[125,4,128]{2,1,0:T(4,128)(2,1)S(1)}, bf16[125,4,128]{2,1,0:T(4,128)(2,1)S(1)}, u32[]{:S(2)}, u32[]{:S(2)}) collective-permute-start(bf16[125,4,128]{2,1,0:T(4,128)(2,1)S(1)} %get-tuple-element.56), channel_id=1, source_target_pairs={{4,8},{8,4},{12,16},{16,12},{20,24},{24,20},{5,9},{9,5},{13,17},{1... | collective-permute-start | bytes 384008 | tf_op jit(solution)/shard_map/ppermute | solution.py:562
  49.3 0.6 %collective-permute-done.11.near = bf16[125,4,128]{2,1,0:T(4,128)(2,1)S(1)} collective-permute-done((bf16[125,4,128]{2,1,0:T(4,128)(2,1)S(1)}, bf16[125,4,128]{2,1,0:T(4,128)(2,1)S(1)}, u32[]{:S(2)}, u32[]{:S(2)}) %collective-permute-start.11) | collective-permute-done | bytes 128032 | tf_op jit(solution)/shard_map/ppermute | solution.py:563
  49.9 0.4 shard_map.88
  50.3 0.4 collective-permute-start.13
  50.7 1.0 %collective-permute-start.14 = (bf16[125,2,128]{2,1,0:T(2,128)(2,1)S(1)}, bf16[125,2,128]{2,1,0:T(2,128)(2,1)S(1)}, u32[]{:S(2)}, u32[]{:S(2)}) collective-permute-start(bf16[125,2,128]{2,1,0:T(2,128)(2,1)S(1)} %get-tuple-element.58), channel_id=1, source_target_pairs={{0,1},{1,0},{2,3},{3,2},{4,5},{5,4},{6,7},{7,6},{8,9},{9,8},{10,11... | collective-permute-start | bytes 192008 | tf_op jit(solution)/shard_map/ppermute | solution.py:572
  51.7 3.5 %collective-permute-start.15 = (bf16[125,4,128]{2,1,0:T(4,128)(2,1)S(1)}, bf16[125,4,128]{2,1,0:T(4,128)(2,1)S(1)}, u32[]{:S(2)}, u32[]{:S(2)}) collective-permute-start(bf16[125,4,128]{2,1,0:T(4,128)(2,1)S(1)} %get-tuple-element.61), channel_id=1, source_target_pairs={{0,4},{4,0},{8,12},{12,8},{16,20},{20,16},{24,28},{28,24},{1,5},{5... | collective-permute-start | bytes 384008 | tf_op jit(solution)/shard_map/ppermute | solution.py:563
  55.3 1.9 %shard_map.89.state_in = f32[625,8,128]{2,1,0:T(8,128)S(1)} custom-call(f32[625,8,128]{2,1,0:T(8,128)S(1)} %get-tuple-element.54.state_ref, f32[625,8,128]{2,1,0:T(8,128)S(1)} %get-tuple-element.55.sum_in), custom_call_target="tpu_custom_call" | custom-call | tf_op jit(solution)/shard_map/pallas_call | solution.py:667
  57.2 0.0 collective-permute-done.13.az_far
  57.2 0.0 collective-permute-done.12.far
  57.2 1.8 %shard_map.90 = (f32[625,8,128]{2,1,0:T(8,128)S(1)}, f32[625,8,128]{2,1,0:T(8,128)}) custom-call(f32[625,8,128]{2,1,0:T(8,128)S(1)} %shard_map.89.state_in, bf16[125,4,128]{2,1,0:T(4,128)(2,1)S(1)} %collective-permute-done.12.far, bf16[125,2,128]{2,1,0:T(2,128)(2,1)S(1)} %collective-permute-done.13.az_far, ...), custom_call_target="tpu_custom_call", output_to_operand_aliasing={{0}: (0, {})} | custom-call | flops 99999997952 | bytes 1000000000 | tf_op jit(solution)/shard_map/pallas_call | solution.py:674
  59.0 1.0 %shard_map.91 = (f32[625,8,128]{2,1,0:T(8,128)S(1)}, f32[625,8,128]{2,1,0:T(8,128)}) custom-call(f32[625,8,128]{2,1,0:T(8,128)S(1)} %get-tuple-element.59.state_in, f32[625,8,128]{2,1,0:T(8,128)} %get-tuple-element.60.out_in, bf16[125,4,128]{2,1,0:T(4,128)(2,1)S(1)} %collective-permute-done.15.near), custom_call_target="tpu_custom_call", output_to_operand_aliasing={{0}: (0, {}), {1}: (1, {})} | custom-call | tf_op jit(solution)/shard_map/pallas_call | solution.py:683
  (5 shorter events, 0.0 us)
Async XLA Ops:
  4.5 24.2 %all-to-all-start = ((s16[32,24,384]{2,1,0:T(8,128)(2,1)}), s16[32,24,384]{2,1,0:T(8,128)(2,1)S(1)}, u32[]{:S(2)}, u32[]{:S(2)}) async-start(s16[32,24,384]{2,1,0:T(8,128)(2,1)} %bitcast.13), calls=%async_computation | async-start | bytes 1179648 | tf_op jit(solution)/shard_map/all_to_all | solution.py:610
  14.8 15.6 %collective-permute-start = (bf16[125,4,128]{2,1,0:T(4,128)(2,1)}, bf16[125,4,128]{2,1,0:T(4,128)(2,1)S(1)}, u32[]{:S(2)}, u32[]{:S(2)}) collective-permute-start(bf16[125,4,128]{2,1,0:T(4,128)(2,1)} %get-tuple-element.34), channel_id=1, source_target_pairs={{4,8},{8,4},{12,16},{16,12},{20,24},{24,20},{5,9},{9,5},{13,17},{1... | collective-permute-start | bytes 384008 | tf_op jit(solution)/shard_map/ppermute | solution.py:562
  15.5 16.4 %collective-permute-start.3 = (bf16[125,4,128]{2,1,0:T(4,128)(2,1)}, bf16[125,4,128]{2,1,0:T(4,128)(2,1)S(1)}, u32[]{:S(2)}, u32[]{:S(2)}) collective-permute-start(bf16[125,4,128]{2,1,0:T(4,128)(2,1)} %get-tuple-element.38), channel_id=1, source_target_pairs={{0,4},{4,0},{8,12},{12,8},{16,20},{20,16},{24,28},{28,24},{1,5},{5... | collective-permute-start | bytes 384008 | tf_op jit(solution)/shard_map/ppermute | solution.py:563
  20.0 10.4 %collective-permute-start.1 = (bf16[125,2,128]{2,1,0:T(2,128)(2,1)}, bf16[125,2,128]{2,1,0:T(2,128)(2,1)S(1)}, u32[]{:S(2)}, u32[]{:S(2)}) collective-permute-start(bf16[125,2,128]{2,1,0:T(2,128)(2,1)} %get-tuple-element.35), channel_id=1, source_target_pairs={{1,2},{2,1},{3,0},{0,3},{5,6},{6,5},{7,4},{4,7},{9,10},{10,9},{11,... | collective-permute-start | bytes 192008 | tf_op jit(solution)/shard_map/ppermute | solution.py:572
  20.7 9.8 %collective-permute-start.2 = (bf16[125,2,128]{2,1,0:T(2,128)(2,1)}, bf16[125,2,128]{2,1,0:T(2,128)(2,1)S(1)}, u32[]{:S(2)}, u32[]{:S(2)}) collective-permute-start(bf16[125,2,128]{2,1,0:T(2,128)(2,1)} %get-tuple-element.36), channel_id=1, source_target_pairs={{0,1},{1,0},{2,3},{3,2},{4,5},{5,4},{6,7},{7,6},{8,9},{9,8},{10,11... | collective-permute-start | bytes 192008 | tf_op jit(solution)/shard_map/ppermute | solution.py:572
  23.2 1.5 %copy-start = (f32[625,8,128]{2,1,0:T(8,128)}, f32[625,8,128]{2,1,0:T(8,128)S(1)}, u32[]{:S(2)}) copy-start(f32[625,8,128]{2,1,0:T(8,128)S(1)} %get-tuple-element.33.state_ref.sum_in) | copy-start | bytes 7680004
  31.1 3.0 %copy-start.1 = (f32[625,8,128]{2,1,0:T(8,128)S(1)}, f32[625,8,128]{2,1,0:T(8,128)}, u32[]{:S(2)}) copy-start(f32[625,8,128]{2,1,0:T(8,128)} %copy-done) | copy-start | bytes 7680004
  31.1 7.9 %collective-permute-start.4 = (bf16[125,4,128]{2,1,0:T(4,128)(2,1)S(1)}, bf16[125,4,128]{2,1,0:T(4,128)(2,1)S(1)}, u32[]{:S(2)}, u32[]{:S(2)}) collective-permute-start(bf16[125,4,128]{2,1,0:T(4,128)(2,1)S(1)} %get-tuple-element.41), channel_id=1, source_target_pairs={{4,8},{8,4},{12,16},{16,12},{20,24},{24,20},{5,9},{9,5},{13,17},{1... | collective-permute-start | bytes 384008 | tf_op jit(solution)/shard_map/ppermute | solution.py:562
  32.5 6.5 %collective-permute-start.5 = (bf16[125,2,128]{2,1,0:T(2,128)(2,1)S(1)}, bf16[125,2,128]{2,1,0:T(2,128)(2,1)S(1)}, u32[]{:S(2)}, u32[]{:S(2)}) collective-permute-start(bf16[125,2,128]{2,1,0:T(2,128)(2,1)S(1)} %get-tuple-element.42), channel_id=1, source_target_pairs={{1,2},{2,1},{3,0},{0,3},{5,6},{6,5},{7,4},{4,7},{9,10},{10,9},{11,... | collective-permute-start | bytes 192008 | tf_op jit(solution)/shard_map/ppermute | solution.py:572
  33.5 5.5 %collective-permute-start.6 = (bf16[125,2,128]{2,1,0:T(2,128)(2,1)S(1)}, bf16[125,2,128]{2,1,0:T(2,128)(2,1)S(1)}, u32[]{:S(2)}, u32[]{:S(2)}) collective-permute-start(bf16[125,2,128]{2,1,0:T(2,128)(2,1)S(1)} %get-tuple-element.43), channel_id=1, source_target_pairs={{0,1},{1,0},{2,3},{3,2},{4,5},{5,4},{6,7},{7,6},{8,9},{9,8},{10,11... | collective-permute-start | bytes 192008 | tf_op jit(solution)/shard_map/ppermute | solution.py:572
  35.8 6.7 %collective-permute-start.7 = (bf16[125,4,128]{2,1,0:T(4,128)(2,1)S(1)}, bf16[125,4,128]{2,1,0:T(4,128)(2,1)S(1)}, u32[]{:S(2)}, u32[]{:S(2)}) collective-permute-start(bf16[125,4,128]{2,1,0:T(4,128)(2,1)S(1)} %get-tuple-element.45), channel_id=1, source_target_pairs={{0,4},{4,0},{8,12},{12,8},{16,20},{20,16},{24,28},{28,24},{1,5},{5... | collective-permute-start | bytes 384008 | tf_op jit(solution)/shard_map/ppermute | solution.py:563
  39.4 8.7 %collective-permute-start.8 = (bf16[125,4,128]{2,1,0:T(4,128)(2,1)S(1)}, bf16[125,4,128]{2,1,0:T(4,128)(2,1)S(1)}, u32[]{:S(2)}, u32[]{:S(2)}) collective-permute-start(bf16[125,4,128]{2,1,0:T(4,128)(2,1)S(1)} %get-tuple-element.49), channel_id=1, source_target_pairs={{4,8},{8,4},{12,16},{16,12},{20,24},{24,20},{5,9},{9,5},{13,17},{1... | collective-permute-start | bytes 384008 | tf_op jit(solution)/shard_map/ppermute | solution.py:562
  42.9 5.2 %collective-permute-start.9 = (bf16[125,2,128]{2,1,0:T(2,128)(2,1)S(1)}, bf16[125,2,128]{2,1,0:T(2,128)(2,1)S(1)}, u32[]{:S(2)}, u32[]{:S(2)}) collective-permute-start(bf16[125,2,128]{2,1,0:T(2,128)(2,1)S(1)} %get-tuple-element.50), channel_id=1, source_target_pairs={{1,2},{2,1},{3,0},{0,3},{5,6},{6,5},{7,4},{4,7},{9,10},{10,9},{11,... | collective-permute-start | bytes 192008 | tf_op jit(solution)/shard_map/ppermute | solution.py:572
  43.5 4.7 %collective-permute-start.10 = (bf16[125,2,128]{2,1,0:T(2,128)(2,1)S(1)}, bf16[125,2,128]{2,1,0:T(2,128)(2,1)S(1)}, u32[]{:S(2)}, u32[]{:S(2)}) collective-permute-start(bf16[125,2,128]{2,1,0:T(2,128)(2,1)S(1)} %get-tuple-element.51), channel_id=1, source_target_pairs={{0,1},{1,0},{2,3},{3,2},{4,5},{5,4},{6,7},{7,6},{8,9},{9,8},{10,11... | collective-permute-start | bytes 192008 | tf_op jit(solution)/shard_map/ppermute | solution.py:572
  44.5 5.4 %collective-permute-start.11 = (bf16[125,4,128]{2,1,0:T(4,128)(2,1)S(1)}, bf16[125,4,128]{2,1,0:T(4,128)(2,1)S(1)}, u32[]{:S(2)}, u32[]{:S(2)}) collective-permute-start(bf16[125,4,128]{2,1,0:T(4,128)(2,1)S(1)} %get-tuple-element.53), channel_id=1, source_target_pairs={{0,4},{4,0},{8,12},{12,8},{16,20},{20,16},{24,28},{28,24},{1,5},{5... | collective-permute-start | bytes 384008 | tf_op jit(solution)/shard_map/ppermute | solution.py:563
  48.6 8.6 %collective-permute-start.12 = (bf16[125,4,128]{2,1,0:T(4,128)(2,1)S(1)}, bf16[125,4,128]{2,1,0:T(4,128)(2,1)S(1)}, u32[]{:S(2)}, u32[]{:S(2)}) collective-permute-start(bf16[125,4,128]{2,1,0:T(4,128)(2,1)S(1)} %get-tuple-element.56), channel_id=1, source_target_pairs={{4,8},{8,4},{12,16},{16,12},{20,24},{24,20},{5,9},{9,5},{13,17},{1... | collective-permute-start | bytes 384008 | tf_op jit(solution)/shard_map/ppermute | solution.py:562
  50.3 6.9 %collective-permute-start.13 = (bf16[125,2,128]{2,1,0:T(2,128)(2,1)S(1)}, bf16[125,2,128]{2,1,0:T(2,128)(2,1)S(1)}, u32[]{:S(2)}, u32[]{:S(2)}) collective-permute-start(bf16[125,2,128]{2,1,0:T(2,128)(2,1)S(1)} %get-tuple-element.57), channel_id=1, source_target_pairs={{1,2},{2,1},{3,0},{0,3},{5,6},{6,5},{7,4},{4,7},{9,10},{10,9},{11,... | collective-permute-start | bytes 192008 | tf_op jit(solution)/shard_map/ppermute | solution.py:572
  50.7 6.5 %collective-permute-start.14 = (bf16[125,2,128]{2,1,0:T(2,128)(2,1)S(1)}, bf16[125,2,128]{2,1,0:T(2,128)(2,1)S(1)}, u32[]{:S(2)}, u32[]{:S(2)}) collective-permute-start(bf16[125,2,128]{2,1,0:T(2,128)(2,1)S(1)} %get-tuple-element.58), channel_id=1, source_target_pairs={{0,1},{1,0},{2,3},{3,2},{4,5},{5,4},{6,7},{7,6},{8,9},{9,8},{10,11... | collective-permute-start | bytes 192008 | tf_op jit(solution)/shard_map/ppermute | solution.py:572
  51.7 7.2 %collective-permute-start.15 = (bf16[125,4,128]{2,1,0:T(4,128)(2,1)S(1)}, bf16[125,4,128]{2,1,0:T(4,128)(2,1)S(1)}, u32[]{:S(2)}, u32[]{:S(2)}) collective-permute-start(bf16[125,4,128]{2,1,0:T(4,128)(2,1)S(1)} %get-tuple-element.61), channel_id=1, source_target_pairs={{0,4},{4,0},{8,12},{12,8},{16,20},{20,16},{24,28},{28,24},{1,5},{5... | collective-permute-start | bytes 384008 | tf_op jit(solution)/shard_map/ppermute | solution.py:563

commit v3 on v2

--- a/solution.py
+++ b/solution.py
@@ -236,6 +236,10 @@
     pl.when(parity == 1)(odd)
 
 
+def five(ref, f, at):
+    return (pl.ds(f * NODES + at, 5),) if len(ref.shape) == 3 else (f, at // 25, pl.ds(at % 25, 5))
+
+
 def received(ref, start):
     return [ref[pl.ds(f * 25 + start, 5)].astype(jnp.float32) for f in range(FIELDS)]
 
@@ -247,7 +251,7 @@
         terms = lifted(received(face, chunk * 5), 0, sign, weight)
         terms = original(terms) if final else terms
         for f, term in enumerate(terms):
-            out_ref[pl.ds(f * NODES + first + chunk * 5, 5), rows, :] += term
+            out_ref[*five(out_ref, f, first + chunk * 5), rows, :] += term
 
 
 def add_far(out_ref, face, weight, final=False):
@@ -273,7 +277,7 @@
         terms = lifted(received(face, chunk), 1, sign, weight)
         for f, term in enumerate(original(terms) if final else terms):
             spread = jnp.where(row == rows[1], term[:, 1:2], 0.0)
-            out_ref[pl.ds(f * NODES + at, 5)] += jnp.where(row == rows[0], term[:, 0:1], spread)
+            out_ref[*five(out_ref, f, at)] += jnp.where(row == rows[0], term[:, 0:1], spread)
 
     def add(low, high):
         for a in range(5):
@@ -375,30 +379,32 @@
 
 
 def last_far_kernel(weight, state_in, far, az_far, az_near, state_ref, out_hbm, sems):
+    far_plane = 4 * (lax.axis_index("ax") % 2)
+
+    def copy(k, plane, nodes):
+        part = (slice(None), plane, nodes)
+        return pltpu.make_async_copy(state_ref.at[*part], out_hbm.at[*part], sems.at[k])
+
+    inside = [copy(k, plane, pl.ds(5, 15)) for k, plane in enumerate((1, 2, 3))]
+    for part in inside:
+        part.start()
     add_az(state_ref, az_far, az_near, weight, final=True)
     add_far(state_ref, far, weight, final=True)
-    first = 25 * (lax.axis_index("ax") % 2)
-    copies = []
-    for f in range(FIELDS):
-        nodes = pl.ds(f * NODES + first, NODES - 25)
-        copy = pltpu.make_async_copy(state_ref.at[nodes], out_hbm.at[nodes], sems.at[f])
-        copy.start()
-        copies.append(copy)
-    for copy in copies:
-        copy.wait()
-
-
-def last_near_kernel(weight, state_in, out_in, near, state_ref, out_hbm, sems):
+    outside = [copy(3, far_plane, pl.ds(0, 25))]
+    outside += [copy(4 + k, k + 1, pl.ds(0, 5)) for k in range(3)]
+    outside += [copy(7 + k, k + 1, pl.ds(20, 5)) for k in range(3)]
+    for part in outside:
+        part.start()
+    for part in inside + outside:
+        part.wait()
+
+
+def last_near_kernel(weight, state_in, out_in, near, state_ref, out_hbm, sem):
     add_near(state_ref, near, weight, final=True)
-    first = 100 - 100 * (lax.axis_index("ax") % 2)
-    copies = []
-    for f in range(FIELDS):
-        nodes = pl.ds(f * NODES + first, 25)
-        copy = pltpu.make_async_copy(state_ref.at[nodes], out_hbm.at[nodes], sems.at[f])
-        copy.start()
-        copies.append(copy)
-    for copy in copies:
-        copy.wait()
+    part = (slice(None), 4 - 4 * (lax.axis_index("ax") % 2))
+    copy = pltpu.make_async_copy(state_ref.at[*part], out_hbm.at[*part], sem.at[0])
+    copy.start()
+    copy.wait()
 
 
 def contribution_kernel(
@@ -431,7 +437,7 @@
     tables_copy = pltpu.make_async_copy(tables_hbm, tables_ref, tables_sem.at[0])
     for copy in row_copies + [tables_copy, lamb_copy]:
         copy.start()
-    for copy in row_copies + [tables_copy, lamb_copy]:
+    for copy in row_copies:
         copy.wait()
 
     owner_row = owner_ref[...]
@@ -455,8 +461,10 @@
     slot_row = owner_row * capacity + position
     placing = (lax.broadcasted_iota(jnp.int32, (slots, flow), 0) == slot_row).astype(jnp.bfloat16)
 
+    tables_copy.wait()
     spare = jnp.zeros((LANES - NODES, lamb_ref.shape[2]), jnp.bfloat16)
     tables = jnp.concatenate([tables_ref[:, 0, :], spare, tables_ref[:, 1, :], spare], axis=0)
+    lamb_copy.wait()
     both = lax.dot_general(
         lamb_ref[...].reshape(3 * flow, lamb_ref.shape[2]),
         tables,
@@ -670,23 +678,24 @@
         2,
         scratch=[pltpu.VMEM(STATE, f32)],
     )(rate, total)
-    hbm_state = pltpu.HBM(STATE, f32)
+    planes = (FIELDS, 5, 25, ROWS, LANES)
+    vmem_planes, hbm_planes = pltpu.VMEM(planes, f32), pltpu.HBM(planes, f32)
     total, partial = call(
         functools.partial(last_far_kernel, STEP_SCALES[3]),
-        [vmem_state, hbm_state],
+        [vmem_planes, hbm_planes],
         4,
         [IN_VMEM, IN_HBM],
         aliases={0: 0},
         cost=LONG,
-        scratch=[pltpu.SemaphoreType.DMA((FIELDS,))],
-    )(total, far, az_far, az_near)
+        scratch=[pltpu.SemaphoreType.DMA((10,))],
+    )(total.reshape(planes), far, az_far, az_near)
     _, new_state = call(
         functools.partial(last_near_kernel, STEP_SCALES[3]),
-        [vmem_state, hbm_state],
+        [vmem_planes, hbm_planes],
         [IN_VMEM, IN_HBM, IN_VMEM],
         [IN_VMEM, IN_HBM],
         aliases={0: 0, 1: 1},
-        scratch=[pltpu.SemaphoreType.DMA((FIELDS,))],
+        scratch=[pltpu.SemaphoreType.DMA((1,))],
     )(total, partial, near)
     shape = acoustic_state.shape
     return new_state.reshape(shape), source.reshape((3,) + shape[1:])

time: 60.3 us -> 59.9 us (level)
  transfers between devices with their start and end apart: 17 -> 17, of which waited for: 3 -> 4; matrix products, arithmetic and copies ran while one was open for 0% -> 0% of each run, Pallas kernels for 27% -> 27%
where the time goes in v3:
time: 59.9 us; the launch traced here: 59.6 us
  starting transfers between devices  29.4 us (49%)
  Pallas kernels  20.5 us (34%)
  waiting for transfers between devices  7.31 us (12%)
  local copies, waits for them, and re-layouts  1.47 us (2%)
  between operations  0.88 us (1%)
    ppermute x4, starting transfers between devices, swap(): lax.ppermute(near, 'ax', pairs[0])  13 us
    all_to_all x1, starting transfers between devices, body(): lax.all_to_all(buffer, ('ax', 'az'), split_axis=0, concat_axis=0, tiled=T...  7.3 us
    all_to_all x1, waiting for transfers between devices, body(): lax.all_to_all(buffer, ('ax', 'az'), split_axis=0, concat_axis=0, tiled=T...  4.04 us
    pallas_call x1, Pallas kernels, body(): call(functools.partial(contribution_kernel, capacity, devices), pltpu.HBM...  3.7 us
    ppermute x4, starting transfers between devices, turn(): lax.ppermute(near, 'az', pairs[0])  3.64 us
    ppermute x4, waiting for transfers between devices, swap(): lax.ppermute(near, 'ax', pairs[0])  3.24 us
    pallas_call x1, Pallas kernels, body(): call(load_kernel, [vmem_state] + face_shapes, [IN_HBM], scratch=[pltpu.Se...  2.97 us
    ppermute x4, starting transfers between devices, swap(): lax.ppermute(far, 'ax', pairs[1])  2.81 us
  transfers between devices with their start and end apart: 17, of which 4 were waited for; matrix products, arithmetic and copies ran while one was open for 0% of the time, Pallas kernels for 27%

profile of v3, /device:TPU:0, one launch (start us, length us, event | category | flops | bytes accessed | tf_op | source)
XLA Modules:
  0.0 59.6 jit_solution(10087118859550893025)
XLA Ops:
  0.6 3.7 %shard_map.79 = s16[768,384]{1,0:T(8,128)(2,1)} custom-call(bf16[3,256,512]{2,1,0:T(8,128)(2,1)} %bitcast.16, s32[1,256]{1,0:T(1,128)} %bitcast.18, s32[1,256]{1,0:T(1,128)} %bitcast.19, s32[1,256]{1,0:T(1,128)} %bitcast.20, bf16[125,2,512]{2,1,0:T(2,128)(2,1)} %bitcast.17), custom_call_target="tpu_custom_call" | custom-call | tf_op jit(solution)/shard_map/pallas_call | solution.py:595
  4.3 7.3 %all-to-all-start = ((s16[32,24,384]{2,1,0:T(8,128)(2,1)}), s16[32,24,384]{2,1,0:T(8,128)(2,1)S(1)}, u32[]{:S(2)}, u32[]{:S(2)}) async-start(s16[32,24,384]{2,1,0:T(8,128)(2,1)} %bitcast.15), calls=%async_computation | async-start | bytes 1179648 | tf_op jit(solution)/shard_map/all_to_all | solution.py:618
  11.7 3.0 %shard_map.77 = (f32[625,8,128]{2,1,0:T(8,128)S(1)}, bf16[125,4,128]{2,1,0:T(4,128)(2,1)}, bf16[125,4,128]{2,1,0:T(4,128)(2,1)}, bf16[125,2,128]{2,1,0:T(2,128)(2,1)}, bf16[125,2,128]{2,1,0:T(2,128)(2,1)}) custom-call(f32[625,8,128]{2,1,0:T(8,128)} %bitcast.13), custom_call_target="tpu_custom_call" | custom-call | tf_op jit(solution)/shard_map/pallas_call | solution.py:620
  14.6 0.7 %collective-permute-start = (bf16[125,4,128]{2,1,0:T(4,128)(2,1)}, bf16[125,4,128]{2,1,0:T(4,128)(2,1)S(1)}, u32[]{:S(2)}, u32[]{:S(2)}) collective-permute-start(bf16[125,4,128]{2,1,0:T(4,128)(2,1)} %get-tuple-element.34), channel_id=1, source_target_pairs={{4,8},{8,4},{12,16},{16,12},{20,24},{24,20},{5,9},{9,5},{13,17},{1... | collective-permute-start | bytes 384008 | tf_op jit(solution)/shard_map/ppermute | solution.py:570
  15.3 4.5 %collective-permute-start.3 = (bf16[125,4,128]{2,1,0:T(4,128)(2,1)}, bf16[125,4,128]{2,1,0:T(4,128)(2,1)S(1)}, u32[]{:S(2)}, u32[]{:S(2)}) collective-permute-start(bf16[125,4,128]{2,1,0:T(4,128)(2,1)} %get-tuple-element.38), channel_id=1, source_target_pairs={{0,4},{4,0},{8,12},{12,8},{16,20},{20,16},{24,28},{28,24},{1,5},{5... | collective-permute-start | bytes 384008 | tf_op jit(solution)/shard_map/ppermute | solution.py:571
  19.8 0.7 %collective-permute-start.1 = (bf16[125,2,128]{2,1,0:T(2,128)(2,1)}, bf16[125,2,128]{2,1,0:T(2,128)(2,1)S(1)}, u32[]{:S(2)}, u32[]{:S(2)}) collective-permute-start(bf16[125,2,128]{2,1,0:T(2,128)(2,1)} %get-tuple-element.35), channel_id=1, source_target_pairs={{1,2},{2,1},{3,0},{0,3},{5,6},{6,5},{7,4},{4,7},{9,10},{10,9},{11,... | collective-permute-start | bytes 192008 | tf_op jit(solution)/shard_map/ppermute | solution.py:580
  20.5 0.9 %collective-permute-start.2 = (bf16[125,2,128]{2,1,0:T(2,128)(2,1)}, bf16[125,2,128]{2,1,0:T(2,128)(2,1)S(1)}, u32[]{:S(2)}, u32[]{:S(2)}) collective-permute-start(bf16[125,2,128]{2,1,0:T(2,128)(2,1)} %get-tuple-element.36), channel_id=1, source_target_pairs={{0,1},{1,0},{2,3},{3,2},{4,5},{5,4},{6,7},{7,6},{8,9},{9,8},{10,11... | collective-permute-start | bytes 192008 | tf_op jit(solution)/shard_map/ppermute | solution.py:580
  21.4 1.6 %shard_map.78.state_in = f32[625,8,128]{2,1,0:T(8,128)S(1)} custom-call(f32[625,8,128]{2,1,0:T(8,128)S(1)} %get-tuple-element.33.state_ref.sum_in), custom_call_target="tpu_custom_call" | custom-call | tf_op jit(solution)/shard_map/pallas_call | solution.py:628
  23.0 0.0 copy-start
  23.0 1.5 %copy-done = f32[625,8,128]{2,1,0:T(8,128)} copy-done((f32[625,8,128]{2,1,0:T(8,128)}, f32[625,8,128]{2,1,0:T(8,128)S(1)}, u32[]{:S(2)}) %copy-start) | copy-done | bytes 2560024
  24.5 4.0 %all-to-all-done = s16[32,24,384]{2,1,0:T(8,128)(2,1)S(1)} async-done(((s16[32,24,384]{2,1,0:T(8,128)(2,1)}), s16[32,24,384]{2,1,0:T(8,128)(2,1)S(1)}, u32[]{:S(2)}, u32[]{:S(2)}) %all-to-all-start) | async-done | bytes 589856 | tf_op jit(solution)/shard_map/all_to_all | solution.py:618
  28.5 1.7 %shard_map.80.source_ref = f32[3000,128]{1,0:T(8,128)S(1)} custom-call(s16[768,384]{1,0:T(8,128)(2,1)S(1)} %bitcast.12), custom_call_target="tpu_custom_call" | custom-call | tf_op jit(solution)/shard_map/pallas_call | solution.py:629
  30.2 0.0 collective-permute-done.1.az_far
  30.3 0.0 collective-permute-done.2.az_near
  30.3 0.0 collective-permute-done.far
  30.3 0.6 shard_map.81
  30.9 0.0 copy-start.1
  30.9 0.8 %collective-permute-start.4 = (bf16[125,4,128]{2,1,0:T(4,128)(2,1)S(1)}, bf16[125,4,128]{2,1,0:T(4,128)(2,1)S(1)}, u32[]{:S(2)}, u32[]{:S(2)}) collective-permute-start(bf16[125,4,128]{2,1,0:T(4,128)(2,1)S(1)} %get-tuple-element.41), channel_id=1, source_target_pairs={{4,8},{8,4},{12,16},{16,12},{20,24},{24,20},{5,9},{9,5},{13,17},{1... | collective-permute-start | bytes 384008 | tf_op jit(solution)/shard_map/ppermute | solution.py:570
  31.7 0.0 collective-permute-done.3.near
  31.7 0.5 shard_map.82
  32.3 1.0 %collective-permute-start.5 = (bf16[125,2,128]{2,1,0:T(2,128)(2,1)S(1)}, bf16[125,2,128]{2,1,0:T(2,128)(2,1)S(1)}, u32[]{:S(2)}, u32[]{:S(2)}) collective-permute-start(bf16[125,2,128]{2,1,0:T(2,128)(2,1)S(1)} %get-tuple-element.42), channel_id=1, source_target_pairs={{1,2},{2,1},{3,0},{0,3},{5,6},{6,5},{7,4},{4,7},{9,10},{10,9},{11,... | collective-permute-start | bytes 192008 | tf_op jit(solution)/shard_map/ppermute | solution.py:580
  33.3 0.6 %collective-permute-start.6 = (bf16[125,2,128]{2,1,0:T(2,128)(2,1)S(1)}, bf16[125,2,128]{2,1,0:T(2,128)(2,1)S(1)}, u32[]{:S(2)}, u32[]{:S(2)}) collective-permute-start(bf16[125,2,128]{2,1,0:T(2,128)(2,1)S(1)} %get-tuple-element.43), channel_id=1, source_target_pairs={{0,1},{1,0},{2,3},{3,2},{4,5},{5,4},{6,7},{7,6},{8,9},{9,8},{10,11... | collective-permute-start | bytes 192008 | tf_op jit(solution)/shard_map/ppermute | solution.py:580
  33.9 1.7 %shard_map.83 = (f32[625,8,128]{2,1,0:T(8,128)S(1)}, f32[625,8,128]{2,1,0:T(8,128)S(1)}, f32[3000,128]{1,0:T(8,128)}) custom-call(f32[625,8,128]{2,1,0:T(8,128)S(1)} %get-tuple-element.39.state_ref, f32[625,8,128]{2,1,0:T(8,128)S(1)} %copy-done.1, f32[3000,128]{1,0:T(8,128)S(1)} %shard_map.80.source_ref), custom_call_target="tpu_custom_call" | custom-call | tf_op jit(solution)/shard_map/pallas_call | solution.py:645
  35.6 3.1 %collective-permute-start.7 = (bf16[125,4,128]{2,1,0:T(4,128)(2,1)S(1)}, bf16[125,4,128]{2,1,0:T(4,128)(2,1)S(1)}, u32[]{:S(2)}, u32[]{:S(2)}) collective-permute-start(bf16[125,4,128]{2,1,0:T(4,128)(2,1)S(1)} %get-tuple-element.45), channel_id=1, source_target_pairs={{0,4},{4,0},{8,12},{12,8},{16,20},{20,16},{24,28},{28,24},{1,5},{5... | collective-permute-start | bytes 384008 | tf_op jit(solution)/shard_map/ppermute | solution.py:571
  38.8 0.0 collective-permute-done.5.az_far
  38.8 0.5 shard_map.84
  39.2 0.7 %collective-permute-start.8 = (bf16[125,4,128]{2,1,0:T(4,128)(2,1)S(1)}, bf16[125,4,128]{2,1,0:T(4,128)(2,1)S(1)}, u32[]{:S(2)}, u32[]{:S(2)}) collective-permute-start(bf16[125,4,128]{2,1,0:T(4,128)(2,1)S(1)} %get-tuple-element.49), channel_id=1, source_target_pairs={{4,8},{8,4},{12,16},{16,12},{20,24},{24,20},{5,9},{9,5},{13,17},{1... | collective-permute-start | bytes 384008 | tf_op jit(solution)/shard_map/ppermute | solution.py:570
  39.9 2.4 %collective-permute-done.7.near = bf16[125,4,128]{2,1,0:T(4,128)(2,1)S(1)} collective-permute-done((bf16[125,4,128]{2,1,0:T(4,128)(2,1)S(1)}, bf16[125,4,128]{2,1,0:T(4,128)(2,1)S(1)}, u32[]{:S(2)}, u32[]{:S(2)}) %collective-permute-start.7) | collective-permute-done | bytes 128032 | tf_op jit(solution)/shard_map/ppermute | solution.py:571
  42.4 0.4 shard_map.85
  42.7 0.5 collective-permute-start.9
  43.3 1.0 %collective-permute-start.10 = (bf16[125,2,128]{2,1,0:T(2,128)(2,1)S(1)}, bf16[125,2,128]{2,1,0:T(2,128)(2,1)S(1)}, u32[]{:S(2)}, u32[]{:S(2)}) collective-permute-start(bf16[125,2,128]{2,1,0:T(2,128)(2,1)S(1)} %get-tuple-element.51), channel_id=1, source_target_pairs={{0,1},{1,0},{2,3},{3,2},{4,5},{5,4},{6,7},{7,6},{8,9},{9,8},{10,11... | collective-permute-start | bytes 192008 | tf_op jit(solution)/shard_map/ppermute | solution.py:580
  44.3 1.8 %collective-permute-start.11 = (bf16[125,4,128]{2,1,0:T(4,128)(2,1)S(1)}, bf16[125,4,128]{2,1,0:T(4,128)(2,1)S(1)}, u32[]{:S(2)}, u32[]{:S(2)}) collective-permute-start(bf16[125,4,128]{2,1,0:T(4,128)(2,1)S(1)} %get-tuple-element.53), channel_id=1, source_target_pairs={{0,4},{4,0},{8,12},{12,8},{16,20},{20,16},{24,28},{28,24},{1,5},{5... | collective-permute-start | bytes 384008 | tf_op jit(solution)/shard_map/ppermute | solution.py:571
  46.1 1.8 %shard_map.86 = (f32[625,8,128]{2,1,0:T(8,128)S(1)}, f32[625,8,128]{2,1,0:T(8,128)S(1)}) custom-call(f32[625,8,128]{2,1,0:T(8,128)S(1)} %get-tuple-element.46.state_ref, f32[625,8,128]{2,1,0:T(8,128)S(1)} %get-tuple-element.47.sum_in), custom_call_target="tpu_custom_call" | custom-call | tf_op jit(solution)/shard_map/pallas_call | solution.py:671
  47.9 0.0 collective-permute-done.9.az_far
  47.9 0.0 collective-permute-done.10.az_near
  47.9 0.5 shard_map.87
  48.4 0.7 %collective-permute-start.12 = (bf16[125,4,128]{2,1,0:T(4,128)(2,1)S(1)}, bf16[125,4,128]{2,1,0:T(4,128)(2,1)S(1)}, u32[]{:S(2)}, u32[]{:S(2)}) collective-permute-start(bf16[125,4,128]{2,1,0:T(4,128)(2,1)S(1)} %get-tuple-element.56), channel_id=1, source_target_pairs={{4,8},{8,4},{12,16},{16,12},{20,24},{24,20},{5,9},{9,5},{13,17},{1... | collective-permute-start | bytes 384008 | tf_op jit(solution)/shard_map/ppermute | solution.py:570
  49.1 0.6 %collective-permute-done.11.near = bf16[125,4,128]{2,1,0:T(4,128)(2,1)S(1)} collective-permute-done((bf16[125,4,128]{2,1,0:T(4,128)(2,1)S(1)}, bf16[125,4,128]{2,1,0:T(4,128)(2,1)S(1)}, u32[]{:S(2)}, u32[]{:S(2)}) %collective-permute-start.11) | collective-permute-done | bytes 128032 | tf_op jit(solution)/shard_map/ppermute | solution.py:571
  49.7 0.4 shard_map.88
  50.1 0.4 collective-permute-start.13
  50.5 1.0 %collective-permute-start.14 = (bf16[125,2,128]{2,1,0:T(2,128)(2,1)S(1)}, bf16[125,2,128]{2,1,0:T(2,128)(2,1)S(1)}, u32[]{:S(2)}, u32[]{:S(2)}) collective-permute-start(bf16[125,2,128]{2,1,0:T(2,128)(2,1)S(1)} %get-tuple-element.58), channel_id=1, source_target_pairs={{0,1},{1,0},{2,3},{3,2},{4,5},{5,4},{6,7},{7,6},{8,9},{9,8},{10,11... | collective-permute-start | bytes 192008 | tf_op jit(solution)/shard_map/ppermute | solution.py:580
  51.5 3.5 %collective-permute-start.15 = (bf16[125,4,128]{2,1,0:T(4,128)(2,1)S(1)}, bf16[125,4,128]{2,1,0:T(4,128)(2,1)S(1)}, u32[]{:S(2)}, u32[]{:S(2)}) collective-permute-start(bf16[125,4,128]{2,1,0:T(4,128)(2,1)S(1)} %get-tuple-element.61), channel_id=1, source_target_pairs={{0,4},{4,0},{8,12},{12,8},{16,20},{20,16},{24,28},{28,24},{1,5},{5... | collective-permute-start | bytes 384008 | tf_op jit(solution)/shard_map/ppermute | solution.py:571
  55.1 1.9 %shard_map.89 = f32[625,8,128]{2,1,0:T(8,128)S(1)} custom-call(f32[625,8,128]{2,1,0:T(8,128)S(1)} %get-tuple-element.54.state_ref, f32[625,8,128]{2,1,0:T(8,128)S(1)} %get-tuple-element.55.sum_in), custom_call_target="tpu_custom_call" | custom-call | tf_op jit(solution)/shard_map/pallas_call | solution.py:675
  57.0 0.0 collective-permute-done.14.az_near
  57.0 0.0 collective-permute-done.12.far
  57.0 1.5 %shard_map.90 = (f32[5,5,25,8,128]{4,3,2,1,0:T(8,128)S(1)}, f32[5,5,25,8,128]{4,3,2,1,0:T(8,128)}) custom-call(f32[5,5,25,8,128]{4,3,2,1,0:T(8,128)S(1)} %bitcast.11, bf16[125,4,128]{2,1,0:T(4,128)(2,1)S(1)} %collective-permute-done.12.far, bf16[125,2,128]{2,1,0:T(2,128)(2,1)S(1)} %collective-permute-done.13.az_far, ...), custom_call_target="tpu_custom_call", output_to_operand_aliasing={{0}: (0, {})} | custom-call | flops 99999997952 | bytes 1000000000 | tf_op jit(solution)/shard_map/pallas_call | solution.py:683
  58.5 0.2 collective-permute-done.15.near
  58.7 0.9 %shard_map.91 = (f32[5,5,25,8,128]{4,3,2,1,0:T(8,128)S(1)}, f32[5,5,25,8,128]{4,3,2,1,0:T(8,128)}) custom-call(f32[5,5,25,8,128]{4,3,2,1,0:T(8,128)S(1)} %get-tuple-element.59.state_in, f32[5,5,25,8,128]{4,3,2,1,0:T(8,128)} %get-tuple-element.60.out_in, ...), custom_call_target="tpu_custom_call", output_to_operand_aliasing={{0}: (0, {}), {1}: (1, {})} | custom-call | tf_op jit(solution)/shard_map/pallas_call | solution.py:692
  (5 shorter events, 0.0 us)
Async XLA Ops:
  4.3 24.2 %all-to-all-start = ((s16[32,24,384]{2,1,0:T(8,128)(2,1)}), s16[32,24,384]{2,1,0:T(8,128)(2,1)S(1)}, u32[]{:S(2)}, u32[]{:S(2)}) async-start(s16[32,24,384]{2,1,0:T(8,128)(2,1)} %bitcast.15), calls=%async_computation | async-start | bytes 1179648 | tf_op jit(solution)/shard_map/all_to_all | solution.py:618
  14.6 15.6 %collective-permute-start = (bf16[125,4,128]{2,1,0:T(4,128)(2,1)}, bf16[125,4,128]{2,1,0:T(4,128)(2,1)S(1)}, u32[]{:S(2)}, u32[]{:S(2)}) collective-permute-start(bf16[125,4,128]{2,1,0:T(4,128)(2,1)} %get-tuple-element.34), channel_id=1, source_target_pairs={{4,8},{8,4},{12,16},{16,12},{20,24},{24,20},{5,9},{9,5},{13,17},{1... | collective-permute-start | bytes 384008 | tf_op jit(solution)/shard_map/ppermute | solution.py:570
  15.3 16.4 %collective-permute-start.3 = (bf16[125,4,128]{2,1,0:T(4,128)(2,1)}, bf16[125,4,128]{2,1,0:T(4,128)(2,1)S(1)}, u32[]{:S(2)}, u32[]{:S(2)}) collective-permute-start(bf16[125,4,128]{2,1,0:T(4,128)(2,1)} %get-tuple-element.38), channel_id=1, source_target_pairs={{0,4},{4,0},{8,12},{12,8},{16,20},{20,16},{24,28},{28,24},{1,5},{5... | collective-permute-start | bytes 384008 | tf_op jit(solution)/shard_map/ppermute | solution.py:571
  19.8 10.4 %collective-permute-start.1 = (bf16[125,2,128]{2,1,0:T(2,128)(2,1)}, bf16[125,2,128]{2,1,0:T(2,128)(2,1)S(1)}, u32[]{:S(2)}, u32[]{:S(2)}) collective-permute-start(bf16[125,2,128]{2,1,0:T(2,128)(2,1)} %get-tuple-element.35), channel_id=1, source_target_pairs={{1,2},{2,1},{3,0},{0,3},{5,6},{6,5},{7,4},{4,7},{9,10},{10,9},{11,... | collective-permute-start | bytes 192008 | tf_op jit(solution)/shard_map/ppermute | solution.py:580
  20.5 9.8 %collective-permute-start.2 = (bf16[125,2,128]{2,1,0:T(2,128)(2,1)}, bf16[125,2,128]{2,1,0:T(2,128)(2,1)S(1)}, u32[]{:S(2)}, u32[]{:S(2)}) collective-permute-start(bf16[125,2,128]{2,1,0:T(2,128)(2,1)} %get-tuple-element.36), channel_id=1, source_target_pairs={{0,1},{1,0},{2,3},{3,2},{4,5},{5,4},{6,7},{7,6},{8,9},{9,8},{10,11... | collective-permute-start | bytes 192008 | tf_op jit(solution)/shard_map/ppermute | solution.py:580
  23.0 1.5 %copy-start = (f32[625,8,128]{2,1,0:T(8,128)}, f32[625,8,128]{2,1,0:T(8,128)S(1)}, u32[]{:S(2)}) copy-start(f32[625,8,128]{2,1,0:T(8,128)S(1)} %get-tuple-element.33.state_ref.sum_in) | copy-start | bytes 7680004
  30.9 3.0 %copy-start.1 = (f32[625,8,128]{2,1,0:T(8,128)S(1)}, f32[625,8,128]{2,1,0:T(8,128)}, u32[]{:S(2)}) copy-start(f32[625,8,128]{2,1,0:T(8,128)} %copy-done) | copy-start | bytes 7680004
  30.9 7.9 %collective-permute-start.4 = (bf16[125,4,128]{2,1,0:T(4,128)(2,1)S(1)}, bf16[125,4,128]{2,1,0:T(4,128)(2,1)S(1)}, u32[]{:S(2)}, u32[]{:S(2)}) collective-permute-start(bf16[125,4,128]{2,1,0:T(4,128)(2,1)S(1)} %get-tuple-element.41), channel_id=1, source_target_pairs={{4,8},{8,4},{12,16},{16,12},{20,24},{24,20},{5,9},{9,5},{13,17},{1... | collective-permute-start | bytes 384008 | tf_op jit(solution)/shard_map/ppermute | solution.py:570
  32.3 6.5 %collective-permute-start.5 = (bf16[125,2,128]{2,1,0:T(2,128)(2,1)S(1)}, bf16[125,2,128]{2,1,0:T(2,128)(2,1)S(1)}, u32[]{:S(2)}, u32[]{:S(2)}) collective-permute-start(bf16[125,2,128]{2,1,0:T(2,128)(2,1)S(1)} %get-tuple-element.42), channel_id=1, source_target_pairs={{1,2},{2,1},{3,0},{0,3},{5,6},{6,5},{7,4},{4,7},{9,10},{10,9},{11,... | collective-permute-start | bytes 192008 | tf_op jit(solution)/shard_map/ppermute | solution.py:580
  33.3 5.5 %collective-permute-start.6 = (bf16[125,2,128]{2,1,0:T(2,128)(2,1)S(1)}, bf16[125,2,128]{2,1,0:T(2,128)(2,1)S(1)}, u32[]{:S(2)}, u32[]{:S(2)}) collective-permute-start(bf16[125,2,128]{2,1,0:T(2,128)(2,1)S(1)} %get-tuple-element.43), channel_id=1, source_target_pairs={{0,1},{1,0},{2,3},{3,2},{4,5},{5,4},{6,7},{7,6},{8,9},{9,8},{10,11... | collective-permute-start | bytes 192008 | tf_op jit(solution)/shard_map/ppermute | solution.py:580
  35.6 6.7 %collective-permute-start.7 = (bf16[125,4,128]{2,1,0:T(4,128)(2,1)S(1)}, bf16[125,4,128]{2,1,0:T(4,128)(2,1)S(1)}, u32[]{:S(2)}, u32[]{:S(2)}) collective-permute-start(bf16[125,4,128]{2,1,0:T(4,128)(2,1)S(1)} %get-tuple-element.45), channel_id=1, source_target_pairs={{0,4},{4,0},{8,12},{12,8},{16,20},{20,16},{24,28},{28,24},{1,5},{5... | collective-permute-start | bytes 384008 | tf_op jit(solution)/shard_map/ppermute | solution.py:571
  39.2 8.7 %collective-permute-start.8 = (bf16[125,4,128]{2,1,0:T(4,128)(2,1)S(1)}, bf16[125,4,128]{2,1,0:T(4,128)(2,1)S(1)}, u32[]{:S(2)}, u32[]{:S(2)}) collective-permute-start(bf16[125,4,128]{2,1,0:T(4,128)(2,1)S(1)} %get-tuple-element.49), channel_id=1, source_target_pairs={{4,8},{8,4},{12,16},{16,12},{20,24},{24,20},{5,9},{9,5},{13,17},{1... | collective-permute-start | bytes 384008 | tf_op jit(solution)/shard_map/ppermute | solution.py:570
  42.7 5.2 %collective-permute-start.9 = (bf16[125,2,128]{2,1,0:T(2,128)(2,1)S(1)}, bf16[125,2,128]{2,1,0:T(2,128)(2,1)S(1)}, u32[]{:S(2)}, u32[]{:S(2)}) collective-permute-start(bf16[125,2,128]{2,1,0:T(2,128)(2,1)S(1)} %get-tuple-element.50), channel_id=1, source_target_pairs={{1,2},{2,1},{3,0},{0,3},{5,6},{6,5},{7,4},{4,7},{9,10},{10,9},{11,... | collective-permute-start | bytes 192008 | tf_op jit(solution)/shard_map/ppermute | solution.py:580
  43.3 4.7 %collective-permute-start.10 = (bf16[125,2,128]{2,1,0:T(2,128)(2,1)S(1)}, bf16[125,2,128]{2,1,0:T(2,128)(2,1)S(1)}, u32[]{:S(2)}, u32[]{:S(2)}) collective-permute-start(bf16[125,2,128]{2,1,0:T(2,128)(2,1)S(1)} %get-tuple-element.51), channel_id=1, source_target_pairs={{0,1},{1,0},{2,3},{3,2},{4,5},{5,4},{6,7},{7,6},{8,9},{9,8},{10,11... | collective-permute-start | bytes 192008 | tf_op jit(solution)/shard_map/ppermute | solution.py:580
  44.3 5.4 %collective-permute-start.11 = (bf16[125,4,128]{2,1,0:T(4,128)(2,1)S(1)}, bf16[125,4,128]{2,1,0:T(4,128)(2,1)S(1)}, u32[]{:S(2)}, u32[]{:S(2)}) collective-permute-start(bf16[125,4,128]{2,1,0:T(4,128)(2,1)S(1)} %get-tuple-element.53), channel_id=1, source_target_pairs={{0,4},{4,0},{8,12},{12,8},{16,20},{20,16},{24,28},{28,24},{1,5},{5... | collective-permute-start | bytes 384008 | tf_op jit(solution)/shard_map/ppermute | solution.py:571
  48.4 8.6 %collective-permute-start.12 = (bf16[125,4,128]{2,1,0:T(4,128)(2,1)S(1)}, bf16[125,4,128]{2,1,0:T(4,128)(2,1)S(1)}, u32[]{:S(2)}, u32[]{:S(2)}) collective-permute-start(bf16[125,4,128]{2,1,0:T(4,128)(2,1)S(1)} %get-tuple-element.56), channel_id=1, source_target_pairs={{4,8},{8,4},{12,16},{16,12},{20,24},{24,20},{5,9},{9,5},{13,17},{1... | collective-permute-start | bytes 384008 | tf_op jit(solution)/shard_map/ppermute | solution.py:570
  50.1 6.9 %collective-permute-start.13 = (bf16[125,2,128]{2,1,0:T(2,128)(2,1)S(1)}, bf16[125,2,128]{2,1,0:T(2,128)(2,1)S(1)}, u32[]{:S(2)}, u32[]{:S(2)}) collective-permute-start(bf16[125,2,128]{2,1,0:T(2,128)(2,1)S(1)} %get-tuple-element.57), channel_id=1, source_target_pairs={{1,2},{2,1},{3,0},{0,3},{5,6},{6,5},{7,4},{4,7},{9,10},{10,9},{11,... | collective-permute-start | bytes 192008 | tf_op jit(solution)/shard_map/ppermute | solution.py:580
  50.5 6.5 %collective-permute-start.14 = (bf16[125,2,128]{2,1,0:T(2,128)(2,1)S(1)}, bf16[125,2,128]{2,1,0:T(2,128)(2,1)S(1)}, u32[]{:S(2)}, u32[]{:S(2)}) collective-permute-start(bf16[125,2,128]{2,1,0:T(2,128)(2,1)S(1)} %get-tuple-element.58), channel_id=1, source_target_pairs={{0,1},{1,0},{2,3},{3,2},{4,5},{5,4},{6,7},{7,6},{8,9},{9,8},{10,11... | collective-permute-start | bytes 192008 | tf_op jit(solution)/shard_map/ppermute | solution.py:580
  51.5 7.1 %collective-permute-start.15 = (bf16[125,4,128]{2,1,0:T(4,128)(2,1)S(1)}, bf16[125,4,128]{2,1,0:T(4,128)(2,1)S(1)}, u32[]{:S(2)}, u32[]{:S(2)}) collective-permute-start(bf16[125,4,128]{2,1,0:T(4,128)(2,1)S(1)} %get-tuple-element.61), channel_id=1, source_target_pairs={{0,4},{4,0},{8,12},{12,8},{16,20},{20,16},{24,28},{28,24},{1,5},{5... | collective-permute-start | bytes 384008 | tf_op jit(solution)/shard_map/ppermute | solution.py:571

commit v4 on v3

--- a/solution.py
+++ b/solution.py
@@ -205,7 +205,8 @@
 def volume_and_source_kernel(
     scale, state_ref, sum_in, source_ref, out_ref, sum_ref, out_hbm, sem
 ):
-    copy = pltpu.make_async_copy(source_ref, out_hbm, sem.at[0])
+    rows = pl.ds(0, out_hbm.shape[0])
+    copy = pltpu.make_async_copy(source_ref.at[rows], out_hbm, sem.at[0])
     copy.start()
     volume_kernel(scale, state_ref, sum_in, out_ref, sum_ref)
     copy.wait()
@@ -434,12 +435,17 @@
         pltpu.make_async_copy(class_hbm, rows_ref.at[1], row_sems.at[2]),
     ]
     lamb_copy = pltpu.make_async_copy(lamb_hbm, lamb_ref, lamb_sem.at[0])
-    tables_copy = pltpu.make_async_copy(tables_hbm, tables_ref, tables_sem.at[0])
+    tables_copy = pltpu.make_async_copy(
+        tables_hbm, tables_ref.at[pl.ds(0, NODES)], tables_sem.at[0]
+    )
     for copy in row_copies + [tables_copy, lamb_copy]:
         copy.start()
     for copy in row_copies:
         copy.wait()
 
+    tables_ref[pl.ds(NODES, LANES - NODES)] = jnp.zeros(
+        (LANES - NODES,) + tables_ref.shape[1:], jnp.bfloat16
+    )
     owner_row = owner_ref[...]
     rows = jnp.concatenate(
         [rows_ref[0], rows_ref[1], jnp.zeros((ROWS - 2, flow), jnp.int32)], axis=0
@@ -462,8 +468,7 @@
     placing = (lax.broadcasted_iota(jnp.int32, (slots, flow), 0) == slot_row).astype(jnp.bfloat16)
 
     tables_copy.wait()
-    spare = jnp.zeros((LANES - NODES, lamb_ref.shape[2]), jnp.bfloat16)
-    tables = jnp.concatenate([tables_ref[:, 0, :], spare, tables_ref[:, 1, :], spare], axis=0)
+    tables = jnp.concatenate([tables_ref[:, 0, :], tables_ref[:, 1, :]], axis=0)
     lamb_copy.wait()
     both = lax.dot_general(
         lamb_ref[...].reshape(3 * flow, lamb_ref.shape[2]),
@@ -528,8 +533,8 @@
         for c in range(3):
             for k in range(2):
                 start = c * NODES * ROWS + group * 2 + k
-                source_ref[pl.ds(start, NODES, stride=ROWS), :] = total[
-                    c * LANES : c * LANES + NODES, k * LANES : (k + 1) * LANES
+                source_ref[pl.ds(start, LANES, stride=ROWS), :] = total[
+                    c * LANES : (c + 1) * LANES, k * LANES : (k + 1) * LANES
                 ]
 
 STATE = (FIELDS * NODES, ROWS, LANES)
@@ -601,7 +606,7 @@
             pltpu.VMEM((3, flow, points), bf16),
             pltpu.VMEM((1, flow), jnp.int32),
             pltpu.VMEM((2, 1, flow), jnp.int32),
-            pltpu.VMEM((NODES, 2, points), bf16),
+            pltpu.VMEM((LANES, 2, points), bf16),
             pltpu.VMEM((3, slots, LANES), jnp.int16),
             pltpu.SemaphoreType.DMA((3,)),
             pltpu.SemaphoreType.DMA((1,)),
@@ -626,7 +631,8 @@
     far, near = swap(far, near)
     az_far, az_near = turn(az_far, az_near)
     moved = call(functools.partial(volume_first_kernel, STEP_SCALES[0]), vmem_state, 1)(state)
-    source = call(source_kernel, pltpu.VMEM(source_shape, f32), 1)(routed)
+    source_rows = 3 * NODES * ROWS + 3 * ROWS
+    source = call(source_kernel, pltpu.VMEM((source_rows, LANES), f32), 1)(routed)
     rate, far = call(
         functools.partial(first_far_kernel, STEP_SCALES[0]),
         [vmem_state, face_shapes[0]],

time: 59.9 us -> 59.8 us (level)
  no operation moved by 1% of the time
where the time goes in v4:
time: 59.8 us; the launch traced here: 59.5 us
  starting transfers between devices  29.4 us (49%)
  Pallas kernels  20.4 us (34%)
  waiting for transfers between devices  7.32 us (12%)
  local copies, waits for them, and re-layouts  1.47 us (2%)
  between operations  0.88 us (1%)
    ppermute x4, starting transfers between devices, swap(): lax.ppermute(near, 'ax', pairs[0])  13 us
    all_to_all x1, starting transfers between devices, body(): lax.all_to_all(buffer, ('ax', 'az'), split_axis=0, concat_axis=0, tiled=T...  7.3 us
    all_to_all x1, waiting for transfers between devices, body(): lax.all_to_all(buffer, ('ax', 'az'), split_axis=0, concat_axis=0, tiled=T...  4.04 us
    pallas_call x1, Pallas kernels, body(): call(functools.partial(contribution_kernel, capacity, devices), pltpu.HBM...  3.64 us
    ppermute x4, starting transfers between devices, turn(): lax.ppermute(near, 'az', pairs[0])  3.63 us
    ppermute x4, waiting for transfers between devices, swap(): lax.ppermute(near, 'ax', pairs[0])  3.24 us
    pallas_call x1, Pallas kernels, body(): call(load_kernel, [vmem_state] + face_shapes, [IN_HBM], scratch=[pltpu.Se...  2.97 us
    ppermute x4, starting transfers between devices, swap(): lax.ppermute(far, 'ax', pairs[1])  2.81 us
  transfers between devices with their start and end apart: 17, of which 4 were waited for; matrix products, arithmetic and copies ran while one was open for 0% of the time, Pallas kernels for 27%

profile of v4, /device:TPU:0, one launch (start us, length us, event | category | flops | bytes accessed | tf_op | source)
XLA Modules:
  0.0 59.5 jit_solution(13849913545000399760)
XLA Ops:
  0.6 3.6 %shard_map.79 = s16[768,384]{1,0:T(8,128)(2,1)} custom-call(bf16[3,256,512]{2,1,0:T(8,128)(2,1)} %bitcast.16, s32[1,256]{1,0:T(1,128)} %bitcast.18, s32[1,256]{1,0:T(1,128)} %bitcast.19, s32[1,256]{1,0:T(1,128)} %bitcast.20, bf16[125,2,512]{2,1,0:T(2,128)(2,1)} %bitcast.17), custom_call_target="tpu_custom_call" | custom-call | tf_op jit(solution)/shard_map/pallas_call | solution.py:600
  4.3 7.3 %all-to-all-start = ((s16[32,24,384]{2,1,0:T(8,128)(2,1)}), s16[32,24,384]{2,1,0:T(8,128)(2,1)S(1)}, u32[]{:S(2)}, u32[]{:S(2)}) async-start(s16[32,24,384]{2,1,0:T(8,128)(2,1)} %bitcast.15), calls=%async_computation | async-start | bytes 1179648 | tf_op jit(solution)/shard_map/all_to_all | solution.py:623
  11.6 3.0 %shard_map.77 = (f32[625,8,128]{2,1,0:T(8,128)S(1)}, bf16[125,4,128]{2,1,0:T(4,128)(2,1)}, bf16[125,4,128]{2,1,0:T(4,128)(2,1)}, bf16[125,2,128]{2,1,0:T(2,128)(2,1)}, bf16[125,2,128]{2,1,0:T(2,128)(2,1)}) custom-call(f32[625,8,128]{2,1,0:T(8,128)} %bitcast.13), custom_call_target="tpu_custom_call" | custom-call | tf_op jit(solution)/shard_map/pallas_call | solution.py:625
  14.6 0.7 %collective-permute-start = (bf16[125,4,128]{2,1,0:T(4,128)(2,1)}, bf16[125,4,128]{2,1,0:T(4,128)(2,1)S(1)}, u32[]{:S(2)}, u32[]{:S(2)}) collective-permute-start(bf16[125,4,128]{2,1,0:T(4,128)(2,1)} %get-tuple-element.34), channel_id=1, source_target_pairs={{4,8},{8,4},{12,16},{16,12},{20,24},{24,20},{5,9},{9,5},{13,17},{1... | collective-permute-start | bytes 384008 | tf_op jit(solution)/shard_map/ppermute | solution.py:575
  15.2 4.5 %collective-permute-start.3 = (bf16[125,4,128]{2,1,0:T(4,128)(2,1)}, bf16[125,4,128]{2,1,0:T(4,128)(2,1)S(1)}, u32[]{:S(2)}, u32[]{:S(2)}) collective-permute-start(bf16[125,4,128]{2,1,0:T(4,128)(2,1)} %get-tuple-element.38), channel_id=1, source_target_pairs={{0,4},{4,0},{8,12},{12,8},{16,20},{20,16},{24,28},{28,24},{1,5},{5... | collective-permute-start | bytes 384008 | tf_op jit(solution)/shard_map/ppermute | solution.py:576
  19.8 0.7 %collective-permute-start.1 = (bf16[125,2,128]{2,1,0:T(2,128)(2,1)}, bf16[125,2,128]{2,1,0:T(2,128)(2,1)S(1)}, u32[]{:S(2)}, u32[]{:S(2)}) collective-permute-start(bf16[125,2,128]{2,1,0:T(2,128)(2,1)} %get-tuple-element.35), channel_id=1, source_target_pairs={{1,2},{2,1},{3,0},{0,3},{5,6},{6,5},{7,4},{4,7},{9,10},{10,9},{11,... | collective-permute-start | bytes 192008 | tf_op jit(solution)/shard_map/ppermute | solution.py:585
  20.4 0.9 %collective-permute-start.2 = (bf16[125,2,128]{2,1,0:T(2,128)(2,1)}, bf16[125,2,128]{2,1,0:T(2,128)(2,1)S(1)}, u32[]{:S(2)}, u32[]{:S(2)}) collective-permute-start(bf16[125,2,128]{2,1,0:T(2,128)(2,1)} %get-tuple-element.36), channel_id=1, source_target_pairs={{0,1},{1,0},{2,3},{3,2},{4,5},{5,4},{6,7},{7,6},{8,9},{9,8},{10,11... | collective-permute-start | bytes 192008 | tf_op jit(solution)/shard_map/ppermute | solution.py:585
  21.4 1.6 %shard_map.78.state_in = f32[625,8,128]{2,1,0:T(8,128)S(1)} custom-call(f32[625,8,128]{2,1,0:T(8,128)S(1)} %get-tuple-element.33.state_ref.sum_in), custom_call_target="tpu_custom_call" | custom-call | tf_op jit(solution)/shard_map/pallas_call | solution.py:633
  22.9 0.0 copy-start
  23.0 1.5 %copy-done = f32[625,8,128]{2,1,0:T(8,128)} copy-done((f32[625,8,128]{2,1,0:T(8,128)}, f32[625,8,128]{2,1,0:T(8,128)S(1)}, u32[]{:S(2)}) %copy-start) | copy-done | bytes 2560024
  24.4 4.0 %all-to-all-done = s16[32,24,384]{2,1,0:T(8,128)(2,1)S(1)} async-done(((s16[32,24,384]{2,1,0:T(8,128)(2,1)}), s16[32,24,384]{2,1,0:T(8,128)(2,1)S(1)}, u32[]{:S(2)}, u32[]{:S(2)}) %all-to-all-start) | async-done | bytes 589856 | tf_op jit(solution)/shard_map/all_to_all | solution.py:623
  28.5 1.7 %shard_map.80.source_ref = f32[3024,128]{1,0:T(8,128)S(1)} custom-call(s16[768,384]{1,0:T(8,128)(2,1)S(1)} %bitcast.12), custom_call_target="tpu_custom_call" | custom-call | tf_op jit(solution)/shard_map/pallas_call | solution.py:635
  30.2 0.0 collective-permute-done.1.az_far
  30.2 0.0 collective-permute-done.2.az_near
  30.2 0.0 collective-permute-done.far
  30.2 0.6 shard_map.81
  30.8 0.0 copy-start.1
  30.8 0.8 %collective-permute-start.4 = (bf16[125,4,128]{2,1,0:T(4,128)(2,1)S(1)}, bf16[125,4,128]{2,1,0:T(4,128)(2,1)S(1)}, u32[]{:S(2)}, u32[]{:S(2)}) collective-permute-start(bf16[125,4,128]{2,1,0:T(4,128)(2,1)S(1)} %get-tuple-element.41), channel_id=1, source_target_pairs={{4,8},{8,4},{12,16},{16,12},{20,24},{24,20},{5,9},{9,5},{13,17},{1... | collective-permute-start | bytes 384008 | tf_op jit(solution)/shard_map/ppermute | solution.py:575
  31.6 0.0 collective-permute-done.3.near
  31.6 0.5 shard_map.82
  32.2 1.0 %collective-permute-start.5 = (bf16[125,2,128]{2,1,0:T(2,128)(2,1)S(1)}, bf16[125,2,128]{2,1,0:T(2,128)(2,1)S(1)}, u32[]{:S(2)}, u32[]{:S(2)}) collective-permute-start(bf16[125,2,128]{2,1,0:T(2,128)(2,1)S(1)} %get-tuple-element.42), channel_id=1, source_target_pairs={{1,2},{2,1},{3,0},{0,3},{5,6},{6,5},{7,4},{4,7},{9,10},{10,9},{11,... | collective-permute-start | bytes 192008 | tf_op jit(solution)/shard_map/ppermute | solution.py:585
  33.2 0.6 %collective-permute-start.6 = (bf16[125,2,128]{2,1,0:T(2,128)(2,1)S(1)}, bf16[125,2,128]{2,1,0:T(2,128)(2,1)S(1)}, u32[]{:S(2)}, u32[]{:S(2)}) collective-permute-start(bf16[125,2,128]{2,1,0:T(2,128)(2,1)S(1)} %get-tuple-element.43), channel_id=1, source_target_pairs={{0,1},{1,0},{2,3},{3,2},{4,5},{5,4},{6,7},{7,6},{8,9},{9,8},{10,11... | collective-permute-start | bytes 192008 | tf_op jit(solution)/shard_map/ppermute | solution.py:585
  33.8 1.6 %shard_map.83 = (f32[625,8,128]{2,1,0:T(8,128)S(1)}, f32[625,8,128]{2,1,0:T(8,128)S(1)}, f32[3000,128]{1,0:T(8,128)}) custom-call(f32[625,8,128]{2,1,0:T(8,128)S(1)} %get-tuple-element.39.state_ref, f32[625,8,128]{2,1,0:T(8,128)S(1)} %copy-done.1, f32[3024,128]{1,0:T(8,128)S(1)} %shard_map.80.source_ref), custom_call_target="tpu_custom_call" | custom-call | tf_op jit(solution)/shard_map/pallas_call | solution.py:651
  35.5 3.1 %collective-permute-start.7 = (bf16[125,4,128]{2,1,0:T(4,128)(2,1)S(1)}, bf16[125,4,128]{2,1,0:T(4,128)(2,1)S(1)}, u32[]{:S(2)}, u32[]{:S(2)}) collective-permute-start(bf16[125,4,128]{2,1,0:T(4,128)(2,1)S(1)} %get-tuple-element.45), channel_id=1, source_target_pairs={{0,4},{4,0},{8,12},{12,8},{16,20},{20,16},{24,28},{28,24},{1,5},{5... | collective-permute-start | bytes 384008 | tf_op jit(solution)/shard_map/ppermute | solution.py:576
  38.6 0.0 collective-permute-done.5.az_far
  38.6 0.5 shard_map.84
  39.1 0.7 %collective-permute-start.8 = (bf16[125,4,128]{2,1,0:T(4,128)(2,1)S(1)}, bf16[125,4,128]{2,1,0:T(4,128)(2,1)S(1)}, u32[]{:S(2)}, u32[]{:S(2)}) collective-permute-start(bf16[125,4,128]{2,1,0:T(4,128)(2,1)S(1)} %get-tuple-element.49), channel_id=1, source_target_pairs={{4,8},{8,4},{12,16},{16,12},{20,24},{24,20},{5,9},{9,5},{13,17},{1... | collective-permute-start | bytes 384008 | tf_op jit(solution)/shard_map/ppermute | solution.py:575
  39.8 2.5 %collective-permute-done.7.near = bf16[125,4,128]{2,1,0:T(4,128)(2,1)S(1)} collective-permute-done((bf16[125,4,128]{2,1,0:T(4,128)(2,1)S(1)}, bf16[125,4,128]{2,1,0:T(4,128)(2,1)S(1)}, u32[]{:S(2)}, u32[]{:S(2)}) %collective-permute-start.7) | collective-permute-done | bytes 128032 | tf_op jit(solution)/shard_map/ppermute | solution.py:576
  42.2 0.4 shard_map.85
  42.6 0.5 collective-permute-start.9
  43.1 1.0 %collective-permute-start.10 = (bf16[125,2,128]{2,1,0:T(2,128)(2,1)S(1)}, bf16[125,2,128]{2,1,0:T(2,128)(2,1)S(1)}, u32[]{:S(2)}, u32[]{:S(2)}) collective-permute-start(bf16[125,2,128]{2,1,0:T(2,128)(2,1)S(1)} %get-tuple-element.51), channel_id=1, source_target_pairs={{0,1},{1,0},{2,3},{3,2},{4,5},{5,4},{6,7},{7,6},{8,9},{9,8},{10,11... | collective-permute-start | bytes 192008 | tf_op jit(solution)/shard_map/ppermute | solution.py:585
  44.2 1.8 %collective-permute-start.11 = (bf16[125,4,128]{2,1,0:T(4,128)(2,1)S(1)}, bf16[125,4,128]{2,1,0:T(4,128)(2,1)S(1)}, u32[]{:S(2)}, u32[]{:S(2)}) collective-permute-start(bf16[125,4,128]{2,1,0:T(4,128)(2,1)S(1)} %get-tuple-element.53), channel_id=1, source_target_pairs={{0,4},{4,0},{8,12},{12,8},{16,20},{20,16},{24,28},{28,24},{1,5},{5... | collective-permute-start | bytes 384008 | tf_op jit(solution)/shard_map/ppermute | solution.py:576
  46.0 1.8 %shard_map.86 = (f32[625,8,128]{2,1,0:T(8,128)S(1)}, f32[625,8,128]{2,1,0:T(8,128)S(1)}) custom-call(f32[625,8,128]{2,1,0:T(8,128)S(1)} %get-tuple-element.46.state_ref, f32[625,8,128]{2,1,0:T(8,128)S(1)} %get-tuple-element.47.sum_in), custom_call_target="tpu_custom_call" | custom-call | tf_op jit(solution)/shard_map/pallas_call | solution.py:677
  47.8 0.0 collective-permute-done.9.az_far
  47.8 0.0 collective-permute-done.10.az_near
  47.8 0.5 shard_map.87
  48.3 0.7 %collective-permute-start.12 = (bf16[125,4,128]{2,1,0:T(4,128)(2,1)S(1)}, bf16[125,4,128]{2,1,0:T(4,128)(2,1)S(1)}, u32[]{:S(2)}, u32[]{:S(2)}) collective-permute-start(bf16[125,4,128]{2,1,0:T(4,128)(2,1)S(1)} %get-tuple-element.56), channel_id=1, source_target_pairs={{4,8},{8,4},{12,16},{16,12},{20,24},{24,20},{5,9},{9,5},{13,17},{1... | collective-permute-start | bytes 384008 | tf_op jit(solution)/shard_map/ppermute | solution.py:575
  49.0 0.6 %collective-permute-done.11.near = bf16[125,4,128]{2,1,0:T(4,128)(2,1)S(1)} collective-permute-done((bf16[125,4,128]{2,1,0:T(4,128)(2,1)S(1)}, bf16[125,4,128]{2,1,0:T(4,128)(2,1)S(1)}, u32[]{:S(2)}, u32[]{:S(2)}) %collective-permute-start.11) | collective-permute-done | bytes 128032 | tf_op jit(solution)/shard_map/ppermute | solution.py:576
  49.6 0.4 shard_map.88
  50.0 0.4 collective-permute-start.13
  50.4 1.0 %collective-permute-start.14 = (bf16[125,2,128]{2,1,0:T(2,128)(2,1)S(1)}, bf16[125,2,128]{2,1,0:T(2,128)(2,1)S(1)}, u32[]{:S(2)}, u32[]{:S(2)}) collective-permute-start(bf16[125,2,128]{2,1,0:T(2,128)(2,1)S(1)} %get-tuple-element.58), channel_id=1, source_target_pairs={{0,1},{1,0},{2,3},{3,2},{4,5},{5,4},{6,7},{7,6},{8,9},{9,8},{10,11... | collective-permute-start | bytes 192008 | tf_op jit(solution)/shard_map/ppermute | solution.py:585
  51.4 3.5 %collective-permute-start.15 = (bf16[125,4,128]{2,1,0:T(4,128)(2,1)S(1)}, bf16[125,4,128]{2,1,0:T(4,128)(2,1)S(1)}, u32[]{:S(2)}, u32[]{:S(2)}) collective-permute-start(bf16[125,4,128]{2,1,0:T(4,128)(2,1)S(1)} %get-tuple-element.61), channel_id=1, source_target_pairs={{0,4},{4,0},{8,12},{12,8},{16,20},{20,16},{24,28},{28,24},{1,5},{5... | collective-permute-start | bytes 384008 | tf_op jit(solution)/shard_map/ppermute | solution.py:576
  54.9 1.9 %shard_map.89 = f32[625,8,128]{2,1,0:T(8,128)S(1)} custom-call(f32[625,8,128]{2,1,0:T(8,128)S(1)} %get-tuple-element.54.state_ref, f32[625,8,128]{2,1,0:T(8,128)S(1)} %get-tuple-element.55.sum_in), custom_call_target="tpu_custom_call" | custom-call | tf_op jit(solution)/shard_map/pallas_call | solution.py:681
  56.8 0.0 collective-permute-done.13.az_far
  56.9 0.0 collective-permute-done.14.az_near
  56.9 1.5 %shard_map.90 = (f32[5,5,25,8,128]{4,3,2,1,0:T(8,128)S(1)}, f32[5,5,25,8,128]{4,3,2,1,0:T(8,128)}) custom-call(f32[5,5,25,8,128]{4,3,2,1,0:T(8,128)S(1)} %bitcast.11, bf16[125,4,128]{2,1,0:T(4,128)(2,1)S(1)} %collective-permute-done.12.far, bf16[125,2,128]{2,1,0:T(2,128)(2,1)S(1)} %collective-permute-done.13.az_far, ...), custom_call_target="tpu_custom_call", output_to_operand_aliasing={{0}: (0, {})} | custom-call | flops 99999997952 | bytes 1000000000 | tf_op jit(solution)/shard_map/pallas_call | solution.py:689
  58.4 0.2 collective-permute-done.15.near
  58.5 0.9 %shard_map.91 = (f32[5,5,25,8,128]{4,3,2,1,0:T(8,128)S(1)}, f32[5,5,25,8,128]{4,3,2,1,0:T(8,128)}) custom-call(f32[5,5,25,8,128]{4,3,2,1,0:T(8,128)S(1)} %get-tuple-element.59.state_in, f32[5,5,25,8,128]{4,3,2,1,0:T(8,128)} %get-tuple-element.60.out_in, ...), custom_call_target="tpu_custom_call", output_to_operand_aliasing={{0}: (0, {}), {1}: (1, {})} | custom-call | tf_op jit(solution)/shard_map/pallas_call | solution.py:698
  (5 shorter events, 0.0 us)
Async XLA Ops:
  4.3 24.2 %all-to-all-start = ((s16[32,24,384]{2,1,0:T(8,128)(2,1)}), s16[32,24,384]{2,1,0:T(8,128)(2,1)S(1)}, u32[]{:S(2)}, u32[]{:S(2)}) async-start(s16[32,24,384]{2,1,0:T(8,128)(2,1)} %bitcast.15), calls=%async_computation | async-start | bytes 1179648 | tf_op jit(solution)/shard_map/all_to_all | solution.py:623
  14.6 15.6 %collective-permute-start = (bf16[125,4,128]{2,1,0:T(4,128)(2,1)}, bf16[125,4,128]{2,1,0:T(4,128)(2,1)S(1)}, u32[]{:S(2)}, u32[]{:S(2)}) collective-permute-start(bf16[125,4,128]{2,1,0:T(4,128)(2,1)} %get-tuple-element.34), channel_id=1, source_target_pairs={{4,8},{8,4},{12,16},{16,12},{20,24},{24,20},{5,9},{9,5},{13,17},{1... | collective-permute-start | bytes 384008 | tf_op jit(solution)/shard_map/ppermute | solution.py:575
  15.2 16.4 %collective-permute-start.3 = (bf16[125,4,128]{2,1,0:T(4,128)(2,1)}, bf16[125,4,128]{2,1,0:T(4,128)(2,1)S(1)}, u32[]{:S(2)}, u32[]{:S(2)}) collective-permute-start(bf16[125,4,128]{2,1,0:T(4,128)(2,1)} %get-tuple-element.38), channel_id=1, source_target_pairs={{0,4},{4,0},{8,12},{12,8},{16,20},{20,16},{24,28},{28,24},{1,5},{5... | collective-permute-start | bytes 384008 | tf_op jit(solution)/shard_map/ppermute | solution.py:576
  19.8 10.4 %collective-permute-start.1 = (bf16[125,2,128]{2,1,0:T(2,128)(2,1)}, bf16[125,2,128]{2,1,0:T(2,128)(2,1)S(1)}, u32[]{:S(2)}, u32[]{:S(2)}) collective-permute-start(bf16[125,2,128]{2,1,0:T(2,128)(2,1)} %get-tuple-element.35), channel_id=1, source_target_pairs={{1,2},{2,1},{3,0},{0,3},{5,6},{6,5},{7,4},{4,7},{9,10},{10,9},{11,... | collective-permute-start | bytes 192008 | tf_op jit(solution)/shard_map/ppermute | solution.py:585
  20.4 9.8 %collective-permute-start.2 = (bf16[125,2,128]{2,1,0:T(2,128)(2,1)}, bf16[125,2,128]{2,1,0:T(2,128)(2,1)S(1)}, u32[]{:S(2)}, u32[]{:S(2)}) collective-permute-start(bf16[125,2,128]{2,1,0:T(2,128)(2,1)} %get-tuple-element.36), channel_id=1, source_target_pairs={{0,1},{1,0},{2,3},{3,2},{4,5},{5,4},{6,7},{7,6},{8,9},{9,8},{10,11... | collective-permute-start | bytes 192008 | tf_op jit(solution)/shard_map/ppermute | solution.py:585
  22.9 1.5 %copy-start = (f32[625,8,128]{2,1,0:T(8,128)}, f32[625,8,128]{2,1,0:T(8,128)S(1)}, u32[]{:S(2)}) copy-start(f32[625,8,128]{2,1,0:T(8,128)S(1)} %get-tuple-element.33.state_ref.sum_in) | copy-start | bytes 7680004
  30.8 3.0 %copy-start.1 = (f32[625,8,128]{2,1,0:T(8,128)S(1)}, f32[625,8,128]{2,1,0:T(8,128)}, u32[]{:S(2)}) copy-start(f32[625,8,128]{2,1,0:T(8,128)} %copy-done) | copy-start | bytes 7680004
  30.8 7.8 %collective-permute-start.4 = (bf16[125,4,128]{2,1,0:T(4,128)(2,1)S(1)}, bf16[125,4,128]{2,1,0:T(4,128)(2,1)S(1)}, u32[]{:S(2)}, u32[]{:S(2)}) collective-permute-start(bf16[125,4,128]{2,1,0:T(4,128)(2,1)S(1)} %get-tuple-element.41), channel_id=1, source_target_pairs={{4,8},{8,4},{12,16},{16,12},{20,24},{24,20},{5,9},{9,5},{13,17},{1... | collective-permute-start | bytes 384008 | tf_op jit(solution)/shard_map/ppermute | solution.py:575
  32.2 6.4 %collective-permute-start.5 = (bf16[125,2,128]{2,1,0:T(2,128)(2,1)S(1)}, bf16[125,2,128]{2,1,0:T(2,128)(2,1)S(1)}, u32[]{:S(2)}, u32[]{:S(2)}) collective-permute-start(bf16[125,2,128]{2,1,0:T(2,128)(2,1)S(1)} %get-tuple-element.42), channel_id=1, source_target_pairs={{1,2},{2,1},{3,0},{0,3},{5,6},{6,5},{7,4},{4,7},{9,10},{10,9},{11,... | collective-permute-start | bytes 192008 | tf_op jit(solution)/shard_map/ppermute | solution.py:585
  33.2 5.4 %collective-permute-start.6 = (bf16[125,2,128]{2,1,0:T(2,128)(2,1)S(1)}, bf16[125,2,128]{2,1,0:T(2,128)(2,1)S(1)}, u32[]{:S(2)}, u32[]{:S(2)}) collective-permute-start(bf16[125,2,128]{2,1,0:T(2,128)(2,1)S(1)} %get-tuple-element.43), channel_id=1, source_target_pairs={{0,1},{1,0},{2,3},{3,2},{4,5},{5,4},{6,7},{7,6},{8,9},{9,8},{10,11... | collective-permute-start | bytes 192008 | tf_op jit(solution)/shard_map/ppermute | solution.py:585
  35.5 6.8 %collective-permute-start.7 = (bf16[125,4,128]{2,1,0:T(4,128)(2,1)S(1)}, bf16[125,4,128]{2,1,0:T(4,128)(2,1)S(1)}, u32[]{:S(2)}, u32[]{:S(2)}) collective-permute-start(bf16[125,4,128]{2,1,0:T(4,128)(2,1)S(1)} %get-tuple-element.45), channel_id=1, source_target_pairs={{0,4},{4,0},{8,12},{12,8},{16,20},{20,16},{24,28},{28,24},{1,5},{5... | collective-permute-start | bytes 384008 | tf_op jit(solution)/shard_map/ppermute | solution.py:576
  39.1 8.7 %collective-permute-start.8 = (bf16[125,4,128]{2,1,0:T(4,128)(2,1)S(1)}, bf16[125,4,128]{2,1,0:T(4,128)(2,1)S(1)}, u32[]{:S(2)}, u32[]{:S(2)}) collective-permute-start(bf16[125,4,128]{2,1,0:T(4,128)(2,1)S(1)} %get-tuple-element.49), channel_id=1, source_target_pairs={{4,8},{8,4},{12,16},{16,12},{20,24},{24,20},{5,9},{9,5},{13,17},{1... | collective-permute-start | bytes 384008 | tf_op jit(solution)/shard_map/ppermute | solution.py:575
  42.6 5.2 %collective-permute-start.9 = (bf16[125,2,128]{2,1,0:T(2,128)(2,1)S(1)}, bf16[125,2,128]{2,1,0:T(2,128)(2,1)S(1)}, u32[]{:S(2)}, u32[]{:S(2)}) collective-permute-start(bf16[125,2,128]{2,1,0:T(2,128)(2,1)S(1)} %get-tuple-element.50), channel_id=1, source_target_pairs={{1,2},{2,1},{3,0},{0,3},{5,6},{6,5},{7,4},{4,7},{9,10},{10,9},{11,... | collective-permute-start | bytes 192008 | tf_op jit(solution)/shard_map/ppermute | solution.py:585
  43.1 4.6 %collective-permute-start.10 = (bf16[125,2,128]{2,1,0:T(2,128)(2,1)S(1)}, bf16[125,2,128]{2,1,0:T(2,128)(2,1)S(1)}, u32[]{:S(2)}, u32[]{:S(2)}) collective-permute-start(bf16[125,2,128]{2,1,0:T(2,128)(2,1)S(1)} %get-tuple-element.51), channel_id=1, source_target_pairs={{0,1},{1,0},{2,3},{3,2},{4,5},{5,4},{6,7},{7,6},{8,9},{9,8},{10,11... | collective-permute-start | bytes 192008 | tf_op jit(solution)/shard_map/ppermute | solution.py:585
  44.2 5.4 %collective-permute-start.11 = (bf16[125,4,128]{2,1,0:T(4,128)(2,1)S(1)}, bf16[125,4,128]{2,1,0:T(4,128)(2,1)S(1)}, u32[]{:S(2)}, u32[]{:S(2)}) collective-permute-start(bf16[125,4,128]{2,1,0:T(4,128)(2,1)S(1)} %get-tuple-element.53), channel_id=1, source_target_pairs={{0,4},{4,0},{8,12},{12,8},{16,20},{20,16},{24,28},{28,24},{1,5},{5... | collective-permute-start | bytes 384008 | tf_op jit(solution)/shard_map/ppermute | solution.py:576
  48.3 8.6 %collective-permute-start.12 = (bf16[125,4,128]{2,1,0:T(4,128)(2,1)S(1)}, bf16[125,4,128]{2,1,0:T(4,128)(2,1)S(1)}, u32[]{:S(2)}, u32[]{:S(2)}) collective-permute-start(bf16[125,4,128]{2,1,0:T(4,128)(2,1)S(1)} %get-tuple-element.56), channel_id=1, source_target_pairs={{4,8},{8,4},{12,16},{16,12},{20,24},{24,20},{5,9},{9,5},{13,17},{1... | collective-permute-start | bytes 384008 | tf_op jit(solution)/shard_map/ppermute | solution.py:575
  50.0 6.9 %collective-permute-start.13 = (bf16[125,2,128]{2,1,0:T(2,128)(2,1)S(1)}, bf16[125,2,128]{2,1,0:T(2,128)(2,1)S(1)}, u32[]{:S(2)}, u32[]{:S(2)}) collective-permute-start(bf16[125,2,128]{2,1,0:T(2,128)(2,1)S(1)} %get-tuple-element.57), channel_id=1, source_target_pairs={{1,2},{2,1},{3,0},{0,3},{5,6},{6,5},{7,4},{4,7},{9,10},{10,9},{11,... | collective-permute-start | bytes 192008 | tf_op jit(solution)/shard_map/ppermute | solution.py:585
  50.4 6.5 %collective-permute-start.14 = (bf16[125,2,128]{2,1,0:T(2,128)(2,1)S(1)}, bf16[125,2,128]{2,1,0:T(2,128)(2,1)S(1)}, u32[]{:S(2)}, u32[]{:S(2)}) collective-permute-start(bf16[125,2,128]{2,1,0:T(2,128)(2,1)S(1)} %get-tuple-element.58), channel_id=1, source_target_pairs={{0,1},{1,0},{2,3},{3,2},{4,5},{5,4},{6,7},{7,6},{8,9},{9,8},{10,11... | collective-permute-start | bytes 192008 | tf_op jit(solution)/shard_map/ppermute | solution.py:585
  51.4 7.1 %collective-permute-start.15 = (bf16[125,4,128]{2,1,0:T(4,128)(2,1)S(1)}, bf16[125,4,128]{2,1,0:T(4,128)(2,1)S(1)}, u32[]{:S(2)}, u32[]{:S(2)}) collective-permute-start(bf16[125,4,128]{2,1,0:T(4,128)(2,1)S(1)} %get-tuple-element.61), channel_id=1, source_target_pairs={{0,4},{4,0},{8,12},{12,8},{16,20},{20,16},{24,28},{28,24},{1,5},{5... | collective-permute-start | bytes 384008 | tf_op jit(solution)/shard_map/ppermute | solution.py:576

commit v5 on v4

--- a/solution.py
+++ b/solution.py
@@ -52,29 +52,10 @@
     return results
 
 
-def flux(q, direction):
-    g, u, v, w, e = q
-    if direction == 0:
-        return [(2.0 * MACH) * g + (1.0 - MACH**2) * u, g, None, None, MACH * e]
-    if direction == 1:
-        return [v, None, g, None, None]
-    return [w, None, None, g, None]
-
-
 def original(q):
     g, u, v, w, e = q
     p = g - MACH * u
     return [p, u, v, w, e + p]
-
-
-def lifted(q, direction, normal, rusanov_sign):
-    result = []
-    for value, flow in zip(q, flux(q, direction)):
-        term = (LIFT * RUSANOV * rusanov_sign) * value
-        if flow is not None:
-            term = term + (LIFT * normal) * flow
-        result.append(term)
-    return result
 
 
 def coupled(jump, direction, normal, scale):
@@ -246,10 +227,9 @@
 
 
 def add_ax(out_ref, face, high, weight, final):
-    sign = -weight if high else weight
     first, rows = (100, slice(4, 8)) if high else (0, slice(0, 4))
     for chunk in range(5):
-        terms = lifted(received(face, chunk * 5), 0, sign, weight)
+        terms = coupled(received(face, chunk * 5), 0, 1.0 if high else -1.0, -weight)
         terms = original(terms) if final else terms
         for f, term in enumerate(terms):
             out_ref[*five(out_ref, f, first + chunk * 5), rows, :] += term
@@ -274,16 +254,16 @@
 def add_az(out_ref, far, near, weight, final=False):
     row = lax.broadcasted_iota(jnp.int32, (5, ROWS, LANES), 1)
 
-    def add_side(face, at, rows, chunk, sign):
-        terms = lifted(received(face, chunk), 1, sign, weight)
+    def add_side(face, at, rows, chunk, normal):
+        terms = coupled(received(face, chunk), 1, normal, -weight)
         for f, term in enumerate(original(terms) if final else terms):
             spread = jnp.where(row == rows[1], term[:, 1:2], 0.0)
             out_ref[*five(out_ref, f, at)] += jnp.where(row == rows[0], term[:, 0:1], spread)
 
     def add(low, high):
         for a in range(5):
-            add_side(low, a * 25, (0, 4), a * 5, weight)
-            add_side(high, a * 25 + 20, (3, 7), a * 5, -weight)
+            add_side(low, a * 25, (0, 4), a * 5, -1.0)
+            add_side(high, a * 25 + 20, (3, 7), a * 5, 1.0)
 
     on_parity("az", lambda: add(far, near), lambda: add(near, far))
 
@@ -353,8 +333,11 @@
                 state_ref[node] += MACH * value
 
 
-def first_far_kernel(scale, state_in, source_ref, far, az_far, az_near, state_ref, far_out):
+def first_az_kernel(scale, state_in, az_far, az_near, state_ref):
     add_az(state_ref, az_far, az_near, scale)
+
+
+def first_far_kernel(scale, state_in, source_ref, far, state_ref, far_out):
     add_far(state_ref, far, scale)
     add_source(state_ref, source_ref, scale, [*range(25), *range(100, NODES)])
     pack_far(state_ref, far_out)
@@ -631,14 +614,17 @@
     far, near = swap(far, near)
     az_far, az_near = turn(az_far, az_near)
     moved = call(functools.partial(volume_first_kernel, STEP_SCALES[0]), vmem_state, 1)(state)
+    moved = call(
+        functools.partial(first_az_kernel, STEP_SCALES[0]), vmem_state, 3, aliases={0: 0}
+    )(moved, az_far, az_near)
     source_rows = 3 * NODES * ROWS + 3 * ROWS
     source = call(source_kernel, pltpu.VMEM((source_rows, LANES), f32), 1)(routed)
     rate, far = call(
         functools.partial(first_far_kernel, STEP_SCALES[0]),
         [vmem_state, face_shapes[0]],
-        5,
+        3,
         aliases={0: 0},
-    )(moved, source, far, az_far, az_near)
+    )(moved, source, far)
     far, _ = swap(far, None)
     rate, near, az_far, az_near = call(
         functools.partial(first_near_kernel, STEP_SCALES[0]),

time: 59.8 us -> 59.4 us (level)
  local copies, waits for them, and re-layouts: 1.47 us -> 0.01 us
  waiting for transfers between devices: 7.32 us -> 8.62 us
    unnamed x4, local copies, waits for them, and re-layouts: 1.47 us -> 0.01 us
    all_to_all x1, waiting for transfers between devices: 4.04 us -> 5.29 us  [body(): lax.all_to_all(buffer, ('ax', 'az'), split_axis=0, concat_axis=0, tiled=T...]
    ppermute x4, starting transfers between devices: 2.62 us -> 3.54 us  [turn(): lax.ppermute(far, 'az', pairs[1])]
  transfers between devices with their start and end apart: 17 -> 17, of which waited for: 4 -> 4; matrix products, arithmetic and copies ran while one was open for 0% -> 0% of each run, Pallas kernels for 27% -> 26%
where the time goes in v5:
time: 59.4 us; the launch traced here: 59 us
  starting transfers between devices  29.4 us (49%)
  Pallas kernels  20.1 us (34%)
  waiting for transfers between devices  8.62 us (15%)
  between operations  0.89 us (1%)
    ppermute x4, starting transfers between devices, swap(): lax.ppermute(near, 'ax', pairs[0])  12.7 us
    all_to_all x1, starting transfers between devices, body(): lax.all_to_all(buffer, ('ax', 'az'), split_axis=0, concat_axis=0, tiled=T...  7.3 us
    all_to_all x1, waiting for transfers between devices, body(): lax.all_to_all(buffer, ('ax', 'az'), split_axis=0, concat_axis=0, tiled=T...  5.29 us
    pallas_call x1, Pallas kernels, body(): call(functools.partial(contribution_kernel, capacity, devices), pltpu.HBM...  3.64 us
    ppermute x4, starting transfers between devices, turn(): lax.ppermute(far, 'az', pairs[1])  3.54 us
    ppermute x4, waiting for transfers between devices, swap(): lax.ppermute(near, 'ax', pairs[0])  3.3 us
    ppermute x4, starting transfers between devices, turn(): lax.ppermute(near, 'az', pairs[0])  3.07 us
    pallas_call x1, Pallas kernels, body(): call(load_kernel, [vmem_state] + face_shapes, [IN_HBM], scratch=[pltpu.Se...  2.85 us
  transfers between devices with their start and end apart: 17, of which 4 were waited for; matrix products, arithmetic and copies ran while one was open for 0% of the time, Pallas kernels for 26%

profile of v5, /device:TPU:0, one launch (start us, length us, event | category | flops | bytes accessed | tf_op | source)
XLA Modules:
  0.0 59.0 jit_solution(12935862480765252715)
XLA Ops:
  0.6 3.6 %shard_map.80 = s16[768,384]{1,0:T(8,128)(2,1)} custom-call(bf16[3,256,512]{2,1,0:T(8,128)(2,1)} %bitcast.16, s32[1,256]{1,0:T(1,128)} %bitcast.18, s32[1,256]{1,0:T(1,128)} %bitcast.19, s32[1,256]{1,0:T(1,128)} %bitcast.20, bf16[125,2,512]{2,1,0:T(2,128)(2,1)} %bitcast.17), custom_call_target="tpu_custom_call" | custom-call | tf_op jit(solution)/shard_map/pallas_call | solution.py:583
  4.3 7.3 %all-to-all-start = ((s16[32,24,384]{2,1,0:T(8,128)(2,1)}), s16[32,24,384]{2,1,0:T(8,128)(2,1)S(1)}, u32[]{:S(2)}, u32[]{:S(2)}) async-start(s16[32,24,384]{2,1,0:T(8,128)(2,1)} %bitcast.15), calls=%async_computation | async-start | bytes 1179648 | tf_op jit(solution)/shard_map/all_to_all | solution.py:606
  11.6 2.8 %shard_map.77 = (f32[625,8,128]{2,1,0:T(8,128)S(1)}, bf16[125,4,128]{2,1,0:T(4,128)(2,1)}, bf16[125,4,128]{2,1,0:T(4,128)(2,1)S(1)}, bf16[125,2,128]{2,1,0:T(2,128)(2,1)S(1)}, bf16[125,2,128]{2,1,0:T(2,128)(2,1)S(1)}) custom-call(f32[625,8,128]{2,1,0:T(8,128)} %bitcast.13), custom_call_target="tpu_custom_call" | custom-call | tf_op jit(solution)/shard_map/pallas_call | solution.py:608
  14.4 0.0 copy-start
  14.5 0.7 %collective-permute-start.2 = (bf16[125,4,128]{2,1,0:T(4,128)(2,1)}, bf16[125,4,128]{2,1,0:T(4,128)(2,1)S(1)}, u32[]{:S(2)}, u32[]{:S(2)}) collective-permute-start(bf16[125,4,128]{2,1,0:T(4,128)(2,1)} %get-tuple-element.36), channel_id=1, source_target_pairs={{4,8},{8,4},{12,16},{16,12},{20,24},{24,20},{5,9},{9,5},{13,17},{1... | collective-permute-start | bytes 384008 | tf_op jit(solution)/shard_map/ppermute | solution.py:558
  15.1 1.6 %collective-permute-start = (bf16[125,2,128]{2,1,0:T(2,128)(2,1)S(1)}, bf16[125,2,128]{2,1,0:T(2,128)(2,1)S(1)}, u32[]{:S(2)}, u32[]{:S(2)}) collective-permute-start(bf16[125,2,128]{2,1,0:T(2,128)(2,1)S(1)} %get-tuple-element.34), channel_id=1, source_target_pairs={{1,2},{2,1},{3,0},{0,3},{5,6},{6,5},{7,4},{4,7},{9,10},{10,9},{11,... | collective-permute-start | bytes 192008 | tf_op jit(solution)/shard_map/ppermute | solution.py:568
  16.7 0.4 collective-permute-start.1
  17.1 4.2 %collective-permute-start.3 = (bf16[125,4,128]{2,1,0:T(4,128)(2,1)S(1)}, bf16[125,4,128]{2,1,0:T(4,128)(2,1)S(1)}, u32[]{:S(2)}, u32[]{:S(2)}) collective-permute-start(bf16[125,4,128]{2,1,0:T(4,128)(2,1)S(1)} %get-tuple-element.38), channel_id=1, source_target_pairs={{0,4},{4,0},{8,12},{12,8},{16,20},{20,16},{24,28},{28,24},{1,5},{5... | collective-permute-start | bytes 384008 | tf_op jit(solution)/shard_map/ppermute | solution.py:559
  21.2 1.6 %shard_map.78.state_in = f32[625,8,128]{2,1,0:T(8,128)S(1)} custom-call(f32[625,8,128]{2,1,0:T(8,128)S(1)} %get-tuple-element.33.state_ref.sum_in), custom_call_target="tpu_custom_call" | custom-call | tf_op jit(solution)/shard_map/pallas_call | solution.py:616
  22.9 0.0 collective-permute-done.az_far
  22.9 0.0 collective-permute-done.1.az_near
  22.9 0.3 shard_map.79.state_in
  23.2 5.3 %all-to-all-done = s16[32,24,384]{2,1,0:T(8,128)(2,1)S(1)} async-done(((s16[32,24,384]{2,1,0:T(8,128)(2,1)}), s16[32,24,384]{2,1,0:T(8,128)(2,1)S(1)}, u32[]{:S(2)}, u32[]{:S(2)}) %all-to-all-start) | async-done | bytes 589856 | tf_op jit(solution)/shard_map/all_to_all | solution.py:606
  28.5 1.7 %shard_map.81.source_ref = f32[3024,128]{1,0:T(8,128)S(1)} custom-call(s16[768,384]{1,0:T(8,128)(2,1)S(1)} %bitcast.12), custom_call_target="tpu_custom_call" | custom-call | tf_op jit(solution)/shard_map/pallas_call | solution.py:621
  30.2 0.0 collective-permute-done.2.far
  30.2 0.3 shard_map.82
  30.5 0.0 copy-start.1
  30.5 0.8 %collective-permute-start.4 = (bf16[125,4,128]{2,1,0:T(4,128)(2,1)S(1)}, bf16[125,4,128]{2,1,0:T(4,128)(2,1)S(1)}, u32[]{:S(2)}, u32[]{:S(2)}) collective-permute-start(bf16[125,4,128]{2,1,0:T(4,128)(2,1)S(1)} %get-tuple-element.41), channel_id=1, source_target_pairs={{4,8},{8,4},{12,16},{16,12},{20,24},{24,20},{5,9},{9,5},{13,17},{1... | collective-permute-start | bytes 384008 | tf_op jit(solution)/shard_map/ppermute | solution.py:558
  31.3 0.5 shard_map.83
  31.8 1.0 %collective-permute-start.5 = (bf16[125,2,128]{2,1,0:T(2,128)(2,1)S(1)}, bf16[125,2,128]{2,1,0:T(2,128)(2,1)S(1)}, u32[]{:S(2)}, u32[]{:S(2)}) collective-permute-start(bf16[125,2,128]{2,1,0:T(2,128)(2,1)S(1)} %get-tuple-element.42), channel_id=1, source_target_pairs={{1,2},{2,1},{3,0},{0,3},{5,6},{6,5},{7,4},{4,7},{9,10},{10,9},{11,... | collective-permute-start | bytes 192008 | tf_op jit(solution)/shard_map/ppermute | solution.py:568
  32.9 0.6 %collective-permute-start.6 = (bf16[125,2,128]{2,1,0:T(2,128)(2,1)S(1)}, bf16[125,2,128]{2,1,0:T(2,128)(2,1)S(1)}, u32[]{:S(2)}, u32[]{:S(2)}) collective-permute-start(bf16[125,2,128]{2,1,0:T(2,128)(2,1)S(1)} %get-tuple-element.43), channel_id=1, source_target_pairs={{0,1},{1,0},{2,3},{3,2},{4,5},{5,4},{6,7},{7,6},{8,9},{9,8},{10,11... | collective-permute-start | bytes 192008 | tf_op jit(solution)/shard_map/ppermute | solution.py:568
  33.5 1.6 %shard_map.84 = (f32[625,8,128]{2,1,0:T(8,128)S(1)}, f32[625,8,128]{2,1,0:T(8,128)S(1)}, f32[3000,128]{1,0:T(8,128)}) custom-call(f32[625,8,128]{2,1,0:T(8,128)S(1)} %get-tuple-element.39.state_ref, f32[625,8,128]{2,1,0:T(8,128)S(1)} %copy-done.1, f32[3024,128]{1,0:T(8,128)S(1)} %shard_map.81.source_ref), custom_call_target="tpu_custom_call" | custom-call | tf_op jit(solution)/shard_map/pallas_call | solution.py:637
  35.1 3.1 %collective-permute-start.7 = (bf16[125,4,128]{2,1,0:T(4,128)(2,1)S(1)}, bf16[125,4,128]{2,1,0:T(4,128)(2,1)S(1)}, u32[]{:S(2)}, u32[]{:S(2)}) collective-permute-start(bf16[125,4,128]{2,1,0:T(4,128)(2,1)S(1)} %get-tuple-element.45), channel_id=1, source_target_pairs={{0,4},{4,0},{8,12},{12,8},{16,20},{20,16},{24,28},{28,24},{1,5},{5... | collective-permute-start | bytes 384008 | tf_op jit(solution)/shard_map/ppermute | solution.py:559
  38.3 0.0 collective-permute-done.5.az_far
  38.3 0.0 collective-permute-done.6.az_near
  38.3 0.4 shard_map.85
  38.7 0.7 %collective-permute-start.8 = (bf16[125,4,128]{2,1,0:T(4,128)(2,1)S(1)}, bf16[125,4,128]{2,1,0:T(4,128)(2,1)S(1)}, u32[]{:S(2)}, u32[]{:S(2)}) collective-permute-start(bf16[125,4,128]{2,1,0:T(4,128)(2,1)S(1)} %get-tuple-element.49), channel_id=1, source_target_pairs={{4,8},{8,4},{12,16},{16,12},{20,24},{24,20},{5,9},{9,5},{13,17},{1... | collective-permute-start | bytes 384008 | tf_op jit(solution)/shard_map/ppermute | solution.py:558
  39.4 2.5 %collective-permute-done.7.near = bf16[125,4,128]{2,1,0:T(4,128)(2,1)S(1)} collective-permute-done((bf16[125,4,128]{2,1,0:T(4,128)(2,1)S(1)}, bf16[125,4,128]{2,1,0:T(4,128)(2,1)S(1)}, u32[]{:S(2)}, u32[]{:S(2)}) %collective-permute-start.7) | collective-permute-done | bytes 128032 | tf_op jit(solution)/shard_map/ppermute | solution.py:559
  41.9 0.3 shard_map.86
  42.2 0.5 collective-permute-start.9
  42.8 1.0 %collective-permute-start.10 = (bf16[125,2,128]{2,1,0:T(2,128)(2,1)S(1)}, bf16[125,2,128]{2,1,0:T(2,128)(2,1)S(1)}, u32[]{:S(2)}, u32[]{:S(2)}) collective-permute-start(bf16[125,2,128]{2,1,0:T(2,128)(2,1)S(1)} %get-tuple-element.51), channel_id=1, source_target_pairs={{0,1},{1,0},{2,3},{3,2},{4,5},{5,4},{6,7},{7,6},{8,9},{9,8},{10,11... | collective-permute-start | bytes 192008 | tf_op jit(solution)/shard_map/ppermute | solution.py:568
  43.8 1.8 %collective-permute-start.11 = (bf16[125,4,128]{2,1,0:T(4,128)(2,1)S(1)}, bf16[125,4,128]{2,1,0:T(4,128)(2,1)S(1)}, u32[]{:S(2)}, u32[]{:S(2)}) collective-permute-start(bf16[125,4,128]{2,1,0:T(4,128)(2,1)S(1)} %get-tuple-element.53), channel_id=1, source_target_pairs={{0,4},{4,0},{8,12},{12,8},{16,20},{20,16},{24,28},{28,24},{1,5},{5... | collective-permute-start | bytes 384008 | tf_op jit(solution)/shard_map/ppermute | solution.py:559
  45.6 1.8 %shard_map.87 = (f32[625,8,128]{2,1,0:T(8,128)S(1)}, f32[625,8,128]{2,1,0:T(8,128)S(1)}) custom-call(f32[625,8,128]{2,1,0:T(8,128)S(1)} %get-tuple-element.46.state_ref, f32[625,8,128]{2,1,0:T(8,128)S(1)} %get-tuple-element.47.sum_in), custom_call_target="tpu_custom_call" | custom-call | tf_op jit(solution)/shard_map/pallas_call | solution.py:663
  47.4 0.0 collective-permute-done.9.az_far
  47.4 0.0 collective-permute-done.8.far
  47.4 0.5 shard_map.88
  47.9 0.7 %collective-permute-start.12 = (bf16[125,4,128]{2,1,0:T(4,128)(2,1)S(1)}, bf16[125,4,128]{2,1,0:T(4,128)(2,1)S(1)}, u32[]{:S(2)}, u32[]{:S(2)}) collective-permute-start(bf16[125,4,128]{2,1,0:T(4,128)(2,1)S(1)} %get-tuple-element.56), channel_id=1, source_target_pairs={{4,8},{8,4},{12,16},{16,12},{20,24},{24,20},{5,9},{9,5},{13,17},{1... | collective-permute-start | bytes 384008 | tf_op jit(solution)/shard_map/ppermute | solution.py:558
  48.6 0.7 %collective-permute-done.11.near = bf16[125,4,128]{2,1,0:T(4,128)(2,1)S(1)} collective-permute-done((bf16[125,4,128]{2,1,0:T(4,128)(2,1)S(1)}, bf16[125,4,128]{2,1,0:T(4,128)(2,1)S(1)}, u32[]{:S(2)}, u32[]{:S(2)}) %collective-permute-start.11) | collective-permute-done | bytes 128032 | tf_op jit(solution)/shard_map/ppermute | solution.py:559
  49.2 0.3 shard_map.89
  49.6 0.4 collective-permute-start.13
  50.0 1.0 %collective-permute-start.14 = (bf16[125,2,128]{2,1,0:T(2,128)(2,1)S(1)}, bf16[125,2,128]{2,1,0:T(2,128)(2,1)S(1)}, u32[]{:S(2)}, u32[]{:S(2)}) collective-permute-start(bf16[125,2,128]{2,1,0:T(2,128)(2,1)S(1)} %get-tuple-element.58), channel_id=1, source_target_pairs={{0,1},{1,0},{2,3},{3,2},{4,5},{5,4},{6,7},{7,6},{8,9},{9,8},{10,11... | collective-permute-start | bytes 192008 | tf_op jit(solution)/shard_map/ppermute | solution.py:568
  51.0 3.5 %collective-permute-start.15 = (bf16[125,4,128]{2,1,0:T(4,128)(2,1)S(1)}, bf16[125,4,128]{2,1,0:T(4,128)(2,1)S(1)}, u32[]{:S(2)}, u32[]{:S(2)}) collective-permute-start(bf16[125,4,128]{2,1,0:T(4,128)(2,1)S(1)} %get-tuple-element.61), channel_id=1, source_target_pairs={{0,4},{4,0},{8,12},{12,8},{16,20},{20,16},{24,28},{28,24},{1,5},{5... | collective-permute-start | bytes 384008 | tf_op jit(solution)/shard_map/ppermute | solution.py:559
  54.5 1.9 %shard_map.90 = f32[625,8,128]{2,1,0:T(8,128)S(1)} custom-call(f32[625,8,128]{2,1,0:T(8,128)S(1)} %get-tuple-element.54.state_ref, f32[625,8,128]{2,1,0:T(8,128)S(1)} %get-tuple-element.55.sum_in), custom_call_target="tpu_custom_call" | custom-call | tf_op jit(solution)/shard_map/pallas_call | solution.py:667
  56.4 0.0 collective-permute-done.13.az_far
  56.5 0.0 collective-permute-done.12.far
  56.5 1.5 %shard_map.91 = (f32[5,5,25,8,128]{4,3,2,1,0:T(8,128)S(1)}, f32[5,5,25,8,128]{4,3,2,1,0:T(8,128)}) custom-call(f32[5,5,25,8,128]{4,3,2,1,0:T(8,128)S(1)} %bitcast.11, bf16[125,4,128]{2,1,0:T(4,128)(2,1)S(1)} %collective-permute-done.12.far, bf16[125,2,128]{2,1,0:T(2,128)(2,1)S(1)} %collective-permute-done.13.az_far, ...), custom_call_target="tpu_custom_call", output_to_operand_aliasing={{0}: (0, {})} | custom-call | flops 99999997952 | bytes 1000000000 | tf_op jit(solution)/shard_map/pallas_call | solution.py:675
  58.0 0.2 collective-permute-done.15.near
  58.1 0.9 %shard_map.92 = (f32[5,5,25,8,128]{4,3,2,1,0:T(8,128)S(1)}, f32[5,5,25,8,128]{4,3,2,1,0:T(8,128)}) custom-call(f32[5,5,25,8,128]{4,3,2,1,0:T(8,128)S(1)} %get-tuple-element.59.state_in, f32[5,5,25,8,128]{4,3,2,1,0:T(8,128)} %get-tuple-element.60.out_in, ...), custom_call_target="tpu_custom_call", output_to_operand_aliasing={{0}: (0, {}), {1}: (1, {})} | custom-call | tf_op jit(solution)/shard_map/pallas_call | solution.py:684
  (6 shorter events, 0.0 us)
Async XLA Ops:
  4.3 24.2 %all-to-all-start = ((s16[32,24,384]{2,1,0:T(8,128)(2,1)}), s16[32,24,384]{2,1,0:T(8,128)(2,1)S(1)}, u32[]{:S(2)}, u32[]{:S(2)}) async-start(s16[32,24,384]{2,1,0:T(8,128)(2,1)} %bitcast.15), calls=%async_computation | async-start | bytes 1179648 | tf_op jit(solution)/shard_map/all_to_all | solution.py:606
  14.4 8.4 %copy-start = (f32[625,8,128]{2,1,0:T(8,128)}, f32[625,8,128]{2,1,0:T(8,128)S(1)}, u32[]{:S(2)}) copy-start(f32[625,8,128]{2,1,0:T(8,128)S(1)} %get-tuple-element.33.state_ref.sum_in) | copy-start | bytes 7680004
  14.5 15.7 %collective-permute-start.2 = (bf16[125,4,128]{2,1,0:T(4,128)(2,1)}, bf16[125,4,128]{2,1,0:T(4,128)(2,1)S(1)}, u32[]{:S(2)}, u32[]{:S(2)}) collective-permute-start(bf16[125,4,128]{2,1,0:T(4,128)(2,1)} %get-tuple-element.36), channel_id=1, source_target_pairs={{4,8},{8,4},{12,16},{16,12},{20,24},{24,20},{5,9},{9,5},{13,17},{1... | collective-permute-start | bytes 384008 | tf_op jit(solution)/shard_map/ppermute | solution.py:558
  15.1 7.7 %collective-permute-start = (bf16[125,2,128]{2,1,0:T(2,128)(2,1)S(1)}, bf16[125,2,128]{2,1,0:T(2,128)(2,1)S(1)}, u32[]{:S(2)}, u32[]{:S(2)}) collective-permute-start(bf16[125,2,128]{2,1,0:T(2,128)(2,1)S(1)} %get-tuple-element.34), channel_id=1, source_target_pairs={{1,2},{2,1},{3,0},{0,3},{5,6},{6,5},{7,4},{4,7},{9,10},{10,9},{11,... | collective-permute-start | bytes 192008 | tf_op jit(solution)/shard_map/ppermute | solution.py:568
  16.7 6.1 %collective-permute-start.1 = (bf16[125,2,128]{2,1,0:T(2,128)(2,1)S(1)}, bf16[125,2,128]{2,1,0:T(2,128)(2,1)S(1)}, u32[]{:S(2)}, u32[]{:S(2)}) collective-permute-start(bf16[125,2,128]{2,1,0:T(2,128)(2,1)S(1)} %get-tuple-element.35), channel_id=1, source_target_pairs={{0,1},{1,0},{2,3},{3,2},{4,5},{5,4},{6,7},{7,6},{8,9},{9,8},{10,11... | collective-permute-start | bytes 192008 | tf_op jit(solution)/shard_map/ppermute | solution.py:568
  17.1 14.2 %collective-permute-start.3 = (bf16[125,4,128]{2,1,0:T(4,128)(2,1)S(1)}, bf16[125,4,128]{2,1,0:T(4,128)(2,1)S(1)}, u32[]{:S(2)}, u32[]{:S(2)}) collective-permute-start(bf16[125,4,128]{2,1,0:T(4,128)(2,1)S(1)} %get-tuple-element.38), channel_id=1, source_target_pairs={{0,4},{4,0},{8,12},{12,8},{16,20},{20,16},{24,28},{28,24},{1,5},{5... | collective-permute-start | bytes 384008 | tf_op jit(solution)/shard_map/ppermute | solution.py:559
  30.5 3.0 %copy-start.1 = (f32[625,8,128]{2,1,0:T(8,128)S(1)}, f32[625,8,128]{2,1,0:T(8,128)}, u32[]{:S(2)}) copy-start(f32[625,8,128]{2,1,0:T(8,128)} %copy-done) | copy-start | bytes 7680004
  30.5 7.8 %collective-permute-start.4 = (bf16[125,4,128]{2,1,0:T(4,128)(2,1)S(1)}, bf16[125,4,128]{2,1,0:T(4,128)(2,1)S(1)}, u32[]{:S(2)}, u32[]{:S(2)}) collective-permute-start(bf16[125,4,128]{2,1,0:T(4,128)(2,1)S(1)} %get-tuple-element.41), channel_id=1, source_target_pairs={{4,8},{8,4},{12,16},{16,12},{20,24},{24,20},{5,9},{9,5},{13,17},{1... | collective-permute-start | bytes 384008 | tf_op jit(solution)/shard_map/ppermute | solution.py:558
  31.8 6.4 %collective-permute-start.5 = (bf16[125,2,128]{2,1,0:T(2,128)(2,1)S(1)}, bf16[125,2,128]{2,1,0:T(2,128)(2,1)S(1)}, u32[]{:S(2)}, u32[]{:S(2)}) collective-permute-start(bf16[125,2,128]{2,1,0:T(2,128)(2,1)S(1)} %get-tuple-element.42), channel_id=1, source_target_pairs={{1,2},{2,1},{3,0},{0,3},{5,6},{6,5},{7,4},{4,7},{9,10},{10,9},{11,... | collective-permute-start | bytes 192008 | tf_op jit(solution)/shard_map/ppermute | solution.py:568
  32.9 5.4 %collective-permute-start.6 = (bf16[125,2,128]{2,1,0:T(2,128)(2,1)S(1)}, bf16[125,2,128]{2,1,0:T(2,128)(2,1)S(1)}, u32[]{:S(2)}, u32[]{:S(2)}) collective-permute-start(bf16[125,2,128]{2,1,0:T(2,128)(2,1)S(1)} %get-tuple-element.43), channel_id=1, source_target_pairs={{0,1},{1,0},{2,3},{3,2},{4,5},{5,4},{6,7},{7,6},{8,9},{9,8},{10,11... | collective-permute-start | bytes 192008 | tf_op jit(solution)/shard_map/ppermute | solution.py:568
  35.1 6.8 %collective-permute-start.7 = (bf16[125,4,128]{2,1,0:T(4,128)(2,1)S(1)}, bf16[125,4,128]{2,1,0:T(4,128)(2,1)S(1)}, u32[]{:S(2)}, u32[]{:S(2)}) collective-permute-start(bf16[125,4,128]{2,1,0:T(4,128)(2,1)S(1)} %get-tuple-element.45), channel_id=1, source_target_pairs={{0,4},{4,0},{8,12},{12,8},{16,20},{20,16},{24,28},{28,24},{1,5},{5... | collective-permute-start | bytes 384008 | tf_op jit(solution)/shard_map/ppermute | solution.py:559
  38.7 8.7 %collective-permute-start.8 = (bf16[125,4,128]{2,1,0:T(4,128)(2,1)S(1)}, bf16[125,4,128]{2,1,0:T(4,128)(2,1)S(1)}, u32[]{:S(2)}, u32[]{:S(2)}) collective-permute-start(bf16[125,4,128]{2,1,0:T(4,128)(2,1)S(1)} %get-tuple-element.49), channel_id=1, source_target_pairs={{4,8},{8,4},{12,16},{16,12},{20,24},{24,20},{5,9},{9,5},{13,17},{1... | collective-permute-start | bytes 384008 | tf_op jit(solution)/shard_map/ppermute | solution.py:558
  42.2 5.2 %collective-permute-start.9 = (bf16[125,2,128]{2,1,0:T(2,128)(2,1)S(1)}, bf16[125,2,128]{2,1,0:T(2,128)(2,1)S(1)}, u32[]{:S(2)}, u32[]{:S(2)}) collective-permute-start(bf16[125,2,128]{2,1,0:T(2,128)(2,1)S(1)} %get-tuple-element.50), channel_id=1, source_target_pairs={{1,2},{2,1},{3,0},{0,3},{5,6},{6,5},{7,4},{4,7},{9,10},{10,9},{11,... | collective-permute-start | bytes 192008 | tf_op jit(solution)/shard_map/ppermute | solution.py:568
  42.8 4.7 %collective-permute-start.10 = (bf16[125,2,128]{2,1,0:T(2,128)(2,1)S(1)}, bf16[125,2,128]{2,1,0:T(2,128)(2,1)S(1)}, u32[]{:S(2)}, u32[]{:S(2)}) collective-permute-start(bf16[125,2,128]{2,1,0:T(2,128)(2,1)S(1)} %get-tuple-element.51), channel_id=1, source_target_pairs={{0,1},{1,0},{2,3},{3,2},{4,5},{5,4},{6,7},{7,6},{8,9},{9,8},{10,11... | collective-permute-start | bytes 192008 | tf_op jit(solution)/shard_map/ppermute | solution.py:568
  43.8 5.4 %collective-permute-start.11 = (bf16[125,4,128]{2,1,0:T(4,128)(2,1)S(1)}, bf16[125,4,128]{2,1,0:T(4,128)(2,1)S(1)}, u32[]{:S(2)}, u32[]{:S(2)}) collective-permute-start(bf16[125,4,128]{2,1,0:T(4,128)(2,1)S(1)} %get-tuple-element.53), channel_id=1, source_target_pairs={{0,4},{4,0},{8,12},{12,8},{16,20},{20,16},{24,28},{28,24},{1,5},{5... | collective-permute-start | bytes 384008 | tf_op jit(solution)/shard_map/ppermute | solution.py:559
  47.9 8.6 %collective-permute-start.12 = (bf16[125,4,128]{2,1,0:T(4,128)(2,1)S(1)}, bf16[125,4,128]{2,1,0:T(4,128)(2,1)S(1)}, u32[]{:S(2)}, u32[]{:S(2)}) collective-permute-start(bf16[125,4,128]{2,1,0:T(4,128)(2,1)S(1)} %get-tuple-element.56), channel_id=1, source_target_pairs={{4,8},{8,4},{12,16},{16,12},{20,24},{24,20},{5,9},{9,5},{13,17},{1... | collective-permute-start | bytes 384008 | tf_op jit(solution)/shard_map/ppermute | solution.py:558
  49.6 6.9 %collective-permute-start.13 = (bf16[125,2,128]{2,1,0:T(2,128)(2,1)S(1)}, bf16[125,2,128]{2,1,0:T(2,128)(2,1)S(1)}, u32[]{:S(2)}, u32[]{:S(2)}) collective-permute-start(bf16[125,2,128]{2,1,0:T(2,128)(2,1)S(1)} %get-tuple-element.57), channel_id=1, source_target_pairs={{1,2},{2,1},{3,0},{0,3},{5,6},{6,5},{7,4},{4,7},{9,10},{10,9},{11,... | collective-permute-start | bytes 192008 | tf_op jit(solution)/shard_map/ppermute | solution.py:568
  50.0 6.5 %collective-permute-start.14 = (bf16[125,2,128]{2,1,0:T(2,128)(2,1)S(1)}, bf16[125,2,128]{2,1,0:T(2,128)(2,1)S(1)}, u32[]{:S(2)}, u32[]{:S(2)}) collective-permute-start(bf16[125,2,128]{2,1,0:T(2,128)(2,1)S(1)} %get-tuple-element.58), channel_id=1, source_target_pairs={{0,1},{1,0},{2,3},{3,2},{4,5},{5,4},{6,7},{7,6},{8,9},{9,8},{10,11... | collective-permute-start | bytes 192008 | tf_op jit(solution)/shard_map/ppermute | solution.py:568
  51.0 7.1 %collective-permute-start.15 = (bf16[125,4,128]{2,1,0:T(4,128)(2,1)S(1)}, bf16[125,4,128]{2,1,0:T(4,128)(2,1)S(1)}, u32[]{:S(2)}, u32[]{:S(2)}) collective-permute-start(bf16[125,4,128]{2,1,0:T(4,128)(2,1)S(1)} %get-tuple-element.61), channel_id=1, source_target_pairs={{0,4},{4,0},{8,12},{12,8},{16,20},{20,16},{24,28},{28,24},{1,5},{5... | collective-permute-start | bytes 384008 | tf_op jit(solution)/shard_map/ppermute | solution.py:559

commit v6 on v5

--- a/solution.py
+++ b/solution.py
@@ -84,7 +84,7 @@
     return [jnp.where(keep, pltpu.roll(value, amount, axis), 0.0) for value in q]
 
 
-def volume_into(state_ref, scale, store):
+def volume_into(state_ref, scale, store, unroll=False):
     row = lax.broadcasted_iota(jnp.int32, (ROWS, LANES), 0)
     lane = lax.broadcasted_iota(jnp.int32, (ROWS, LANES), 1)
     cell = row % 4
@@ -136,20 +136,19 @@
             values.append(row)
         store(direction, nodes, values, q)
 
-    @pl.loop(0, 5)
-    def _(outer):
-        for inner in range(5):
-            line(0, [k * 25 + outer * 5 + inner for k in range(5)])
-
-    @pl.loop(0, 5)
-    def _(outer):
-        for inner in range(5):
-            line(1, [outer * 25 + k * 5 + inner for k in range(5)])
-
-    @pl.loop(0, 5)
-    def _(outer):
-        for inner in range(5):
-            line(2, [outer * 25 + inner * 5 + k for k in range(5)])
+    strides = ((25, 5, 1), (5, 25, 1), (1, 25, 5))
+    for direction, (step, outer_step, inner_step) in enumerate(strides):
+
+        def lines(outer):
+            for inner in range(5):
+                first = outer * outer_step + inner * inner_step
+                line(direction, [first + k * step for k in range(5)])
+
+        if unroll:
+            for outer in range(5):
+                lines(outer)
+        else:
+            pl.loop(0, 5)(lines)
 
 
 def volume_first_kernel(scale, state_ref, out_ref):
@@ -209,7 +208,7 @@
             for f, total in enumerate(original(totals)):
                 sum_ref[f * NODES + node] = total
 
-    volume_into(state_ref, scale, store)
+    volume_into(state_ref, scale, store, unroll=True)
 
 
 def on_parity(axis, even, odd):
@@ -373,13 +372,14 @@
     for part in inside:
         part.start()
     add_az(state_ref, az_far, az_near, weight, final=True)
-    add_far(state_ref, far, weight, final=True)
-    outside = [copy(3, far_plane, pl.ds(0, 25))]
-    outside += [copy(4 + k, k + 1, pl.ds(0, 5)) for k in range(3)]
-    outside += [copy(7 + k, k + 1, pl.ds(20, 5)) for k in range(3)]
+    outside = [copy(3 + k, k + 1, pl.ds(0, 5)) for k in range(3)]
+    outside += [copy(6 + k, k + 1, pl.ds(20, 5)) for k in range(3)]
     for part in outside:
         part.start()
-    for part in inside + outside:
+    add_far(state_ref, far, weight, final=True)
+    face = copy(9, far_plane, pl.ds(0, 25))
+    face.start()
+    for part in inside + outside + [face]:
         part.wait()
 
 

time: 59.4 us -> 59.7 us (level)
  no operation moved by 1% of the time
where the time goes in v6:
time: 59.7 us; the launch traced here: 59.4 us
  starting transfers between devices  29.4 us (49%)
  Pallas kernels  20.2 us (34%)
  waiting for transfers between devices  8.71 us (15%)
  between operations  1.05 us (2%)
    ppermute x4, starting transfers between devices, swap(): lax.ppermute(near, 'ax', pairs[0])  12.7 us
    all_to_all x1, starting transfers between devices, body(): lax.all_to_all(buffer, ('ax', 'az'), split_axis=0, concat_axis=0, tiled=T...  7.3 us
    all_to_all x1, waiting for transfers between devices, body(): lax.all_to_all(buffer, ('ax', 'az'), split_axis=0, concat_axis=0, tiled=T...  5.29 us
    pallas_call x1, Pallas kernels, body(): call(functools.partial(contribution_kernel, capacity, devices), pltpu.HBM...  3.63 us
    ppermute x4, starting transfers between devices, turn(): lax.ppermute(far, 'az', pairs[1])  3.53 us
    ppermute x4, waiting for transfers between devices, swap(): lax.ppermute(near, 'ax', pairs[0])  3.39 us
    ppermute x4, starting transfers between devices, turn(): lax.ppermute(near, 'az', pairs[0])  3.08 us
    pallas_call x1, Pallas kernels, body(): call(load_kernel, [vmem_state] + face_shapes, [IN_HBM], scratch=[pltpu.Se...  2.85 us
  transfers between devices with their start and end apart: 17, of which 4 were waited for; matrix products, arithmetic and copies ran while one was open for 0% of the time, Pallas kernels for 26%

profile of v6, /device:TPU:0, one launch (start us, length us, event | category | flops | bytes accessed | tf_op | source)
XLA Modules:
  0.0 59.4 jit_solution(10667646401325644883)
XLA Ops:
  0.6 3.6 %shard_map.80 = s16[768,384]{1,0:T(8,128)(2,1)} custom-call(bf16[3,256,512]{2,1,0:T(8,128)(2,1)} %bitcast.16, s32[1,256]{1,0:T(1,128)} %bitcast.18, s32[1,256]{1,0:T(1,128)} %bitcast.19, s32[1,256]{1,0:T(1,128)} %bitcast.20, bf16[125,2,512]{2,1,0:T(2,128)(2,1)} %bitcast.17), custom_call_target="tpu_custom_call" | custom-call | tf_op jit(solution)/shard_map/pallas_call | solution.py:583
  4.3 7.3 %all-to-all-start = ((s16[32,24,384]{2,1,0:T(8,128)(2,1)}), s16[32,24,384]{2,1,0:T(8,128)(2,1)S(1)}, u32[]{:S(2)}, u32[]{:S(2)}) async-start(s16[32,24,384]{2,1,0:T(8,128)(2,1)} %bitcast.15), calls=%async_computation | async-start | bytes 1179648 | tf_op jit(solution)/shard_map/all_to_all | solution.py:606
  11.6 2.8 %shard_map.77 = (f32[625,8,128]{2,1,0:T(8,128)S(1)}, bf16[125,4,128]{2,1,0:T(4,128)(2,1)}, bf16[125,4,128]{2,1,0:T(4,128)(2,1)S(1)}, bf16[125,2,128]{2,1,0:T(2,128)(2,1)S(1)}, bf16[125,2,128]{2,1,0:T(2,128)(2,1)S(1)}) custom-call(f32[625,8,128]{2,1,0:T(8,128)} %bitcast.13), custom_call_target="tpu_custom_call" | custom-call | tf_op jit(solution)/shard_map/pallas_call | solution.py:608
  14.4 0.0 copy-start
  14.5 0.7 %collective-permute-start.2 = (bf16[125,4,128]{2,1,0:T(4,128)(2,1)}, bf16[125,4,128]{2,1,0:T(4,128)(2,1)S(1)}, u32[]{:S(2)}, u32[]{:S(2)}) collective-permute-start(bf16[125,4,128]{2,1,0:T(4,128)(2,1)} %get-tuple-element.36), channel_id=1, source_target_pairs={{4,8},{8,4},{12,16},{16,12},{20,24},{24,20},{5,9},{9,5},{13,17},{1... | collective-permute-start | bytes 384008 | tf_op jit(solution)/shard_map/ppermute | solution.py:558
  15.1 1.6 %collective-permute-start = (bf16[125,2,128]{2,1,0:T(2,128)(2,1)S(1)}, bf16[125,2,128]{2,1,0:T(2,128)(2,1)S(1)}, u32[]{:S(2)}, u32[]{:S(2)}) collective-permute-start(bf16[125,2,128]{2,1,0:T(2,128)(2,1)S(1)} %get-tuple-element.34), channel_id=1, source_target_pairs={{1,2},{2,1},{3,0},{0,3},{5,6},{6,5},{7,4},{4,7},{9,10},{10,9},{11,... | collective-permute-start | bytes 192008 | tf_op jit(solution)/shard_map/ppermute | solution.py:568
  16.7 0.4 collective-permute-start.1
  17.1 4.2 %collective-permute-start.3 = (bf16[125,4,128]{2,1,0:T(4,128)(2,1)S(1)}, bf16[125,4,128]{2,1,0:T(4,128)(2,1)S(1)}, u32[]{:S(2)}, u32[]{:S(2)}) collective-permute-start(bf16[125,4,128]{2,1,0:T(4,128)(2,1)S(1)} %get-tuple-element.38), channel_id=1, source_target_pairs={{0,4},{4,0},{8,12},{12,8},{16,20},{20,16},{24,28},{28,24},{1,5},{5... | collective-permute-start | bytes 384008 | tf_op jit(solution)/shard_map/ppermute | solution.py:559
  21.2 1.6 %shard_map.78.state_in = f32[625,8,128]{2,1,0:T(8,128)S(1)} custom-call(f32[625,8,128]{2,1,0:T(8,128)S(1)} %get-tuple-element.33.state_ref.sum_in), custom_call_target="tpu_custom_call" | custom-call | tf_op jit(solution)/shard_map/pallas_call | solution.py:616
  22.8 0.0 collective-permute-done.az_far
  22.9 0.0 collective-permute-done.1.az_near
  22.9 0.3 shard_map.79.state_in
  23.2 5.3 %all-to-all-done = s16[32,24,384]{2,1,0:T(8,128)(2,1)S(1)} async-done(((s16[32,24,384]{2,1,0:T(8,128)(2,1)}), s16[32,24,384]{2,1,0:T(8,128)(2,1)S(1)}, u32[]{:S(2)}, u32[]{:S(2)}) %all-to-all-start) | async-done | bytes 589856 | tf_op jit(solution)/shard_map/all_to_all | solution.py:606
  28.5 1.7 %shard_map.81.source_ref = f32[3024,128]{1,0:T(8,128)S(1)} custom-call(s16[768,384]{1,0:T(8,128)(2,1)S(1)} %bitcast.12), custom_call_target="tpu_custom_call" | custom-call | tf_op jit(solution)/shard_map/pallas_call | solution.py:621
  30.2 0.0 collective-permute-done.2.far
  30.2 0.3 shard_map.82
  30.5 0.0 copy-start.1
  30.5 0.8 %collective-permute-start.4 = (bf16[125,4,128]{2,1,0:T(4,128)(2,1)S(1)}, bf16[125,4,128]{2,1,0:T(4,128)(2,1)S(1)}, u32[]{:S(2)}, u32[]{:S(2)}) collective-permute-start(bf16[125,4,128]{2,1,0:T(4,128)(2,1)S(1)} %get-tuple-element.41), channel_id=1, source_target_pairs={{4,8},{8,4},{12,16},{16,12},{20,24},{24,20},{5,9},{9,5},{13,17},{1... | collective-permute-start | bytes 384008 | tf_op jit(solution)/shard_map/ppermute | solution.py:558
  31.3 0.0 collective-permute-done.3.near
  31.3 0.5 shard_map.83
  31.8 1.0 %collective-permute-start.5 = (bf16[125,2,128]{2,1,0:T(2,128)(2,1)S(1)}, bf16[125,2,128]{2,1,0:T(2,128)(2,1)S(1)}, u32[]{:S(2)}, u32[]{:S(2)}) collective-permute-start(bf16[125,2,128]{2,1,0:T(2,128)(2,1)S(1)} %get-tuple-element.42), channel_id=1, source_target_pairs={{1,2},{2,1},{3,0},{0,3},{5,6},{6,5},{7,4},{4,7},{9,10},{10,9},{11,... | collective-permute-start | bytes 192008 | tf_op jit(solution)/shard_map/ppermute | solution.py:568
  32.8 0.6 %collective-permute-start.6 = (bf16[125,2,128]{2,1,0:T(2,128)(2,1)S(1)}, bf16[125,2,128]{2,1,0:T(2,128)(2,1)S(1)}, u32[]{:S(2)}, u32[]{:S(2)}) collective-permute-start(bf16[125,2,128]{2,1,0:T(2,128)(2,1)S(1)} %get-tuple-element.43), channel_id=1, source_target_pairs={{0,1},{1,0},{2,3},{3,2},{4,5},{5,4},{6,7},{7,6},{8,9},{9,8},{10,11... | collective-permute-start | bytes 192008 | tf_op jit(solution)/shard_map/ppermute | solution.py:568
  33.5 1.6 %shard_map.84 = (f32[625,8,128]{2,1,0:T(8,128)S(1)}, f32[625,8,128]{2,1,0:T(8,128)S(1)}, f32[3000,128]{1,0:T(8,128)}) custom-call(f32[625,8,128]{2,1,0:T(8,128)S(1)} %get-tuple-element.39.state_ref, f32[625,8,128]{2,1,0:T(8,128)S(1)} %copy-done.1, f32[3024,128]{1,0:T(8,128)S(1)} %shard_map.81.source_ref), custom_call_target="tpu_custom_call" | custom-call | tf_op jit(solution)/shard_map/pallas_call | solution.py:637
  35.1 3.1 %collective-permute-start.7 = (bf16[125,4,128]{2,1,0:T(4,128)(2,1)S(1)}, bf16[125,4,128]{2,1,0:T(4,128)(2,1)S(1)}, u32[]{:S(2)}, u32[]{:S(2)}) collective-permute-start(bf16[125,4,128]{2,1,0:T(4,128)(2,1)S(1)} %get-tuple-element.45), channel_id=1, source_target_pairs={{0,4},{4,0},{8,12},{12,8},{16,20},{20,16},{24,28},{28,24},{1,5},{5... | collective-permute-start | bytes 384008 | tf_op jit(solution)/shard_map/ppermute | solution.py:559
  38.3 0.0 collective-permute-done.5.az_far
  38.3 0.0 collective-permute-done.6.az_near
  38.3 0.4 shard_map.85
  38.7 0.7 %collective-permute-start.8 = (bf16[125,4,128]{2,1,0:T(4,128)(2,1)S(1)}, bf16[125,4,128]{2,1,0:T(4,128)(2,1)S(1)}, u32[]{:S(2)}, u32[]{:S(2)}) collective-permute-start(bf16[125,4,128]{2,1,0:T(4,128)(2,1)S(1)} %get-tuple-element.49), channel_id=1, source_target_pairs={{4,8},{8,4},{12,16},{16,12},{20,24},{24,20},{5,9},{9,5},{13,17},{1... | collective-permute-start | bytes 384008 | tf_op jit(solution)/shard_map/ppermute | solution.py:558
  39.4 2.5 %collective-permute-done.7.near = bf16[125,4,128]{2,1,0:T(4,128)(2,1)S(1)} collective-permute-done((bf16[125,4,128]{2,1,0:T(4,128)(2,1)S(1)}, bf16[125,4,128]{2,1,0:T(4,128)(2,1)S(1)}, u32[]{:S(2)}, u32[]{:S(2)}) %collective-permute-start.7) | collective-permute-done | bytes 128032 | tf_op jit(solution)/shard_map/ppermute | solution.py:559
  41.9 0.3 shard_map.86
  42.2 0.5 collective-permute-start.9
  42.8 1.0 %collective-permute-start.10 = (bf16[125,2,128]{2,1,0:T(2,128)(2,1)S(1)}, bf16[125,2,128]{2,1,0:T(2,128)(2,1)S(1)}, u32[]{:S(2)}, u32[]{:S(2)}) collective-permute-start(bf16[125,2,128]{2,1,0:T(2,128)(2,1)S(1)} %get-tuple-element.51), channel_id=1, source_target_pairs={{0,1},{1,0},{2,3},{3,2},{4,5},{5,4},{6,7},{7,6},{8,9},{9,8},{10,11... | collective-permute-start | bytes 192008 | tf_op jit(solution)/shard_map/ppermute | solution.py:568
  43.8 1.8 %collective-permute-start.11 = (bf16[125,4,128]{2,1,0:T(4,128)(2,1)S(1)}, bf16[125,4,128]{2,1,0:T(4,128)(2,1)S(1)}, u32[]{:S(2)}, u32[]{:S(2)}) collective-permute-start(bf16[125,4,128]{2,1,0:T(4,128)(2,1)S(1)} %get-tuple-element.53), channel_id=1, source_target_pairs={{0,4},{4,0},{8,12},{12,8},{16,20},{20,16},{24,28},{28,24},{1,5},{5... | collective-permute-start | bytes 384008 | tf_op jit(solution)/shard_map/ppermute | solution.py:559
  45.6 1.8 %shard_map.87 = (f32[625,8,128]{2,1,0:T(8,128)S(1)}, f32[625,8,128]{2,1,0:T(8,128)S(1)}) custom-call(f32[625,8,128]{2,1,0:T(8,128)S(1)} %get-tuple-element.46.state_ref, f32[625,8,128]{2,1,0:T(8,128)S(1)} %get-tuple-element.47.sum_in), custom_call_target="tpu_custom_call" | custom-call | tf_op jit(solution)/shard_map/pallas_call | solution.py:663
  47.4 0.0 collective-permute-done.10.az_near
  47.4 0.0 collective-permute-done.8.far
  47.4 0.5 shard_map.88
  47.9 0.7 %collective-permute-start.12 = (bf16[125,4,128]{2,1,0:T(4,128)(2,1)S(1)}, bf16[125,4,128]{2,1,0:T(4,128)(2,1)S(1)}, u32[]{:S(2)}, u32[]{:S(2)}) collective-permute-start(bf16[125,4,128]{2,1,0:T(4,128)(2,1)S(1)} %get-tuple-element.56), channel_id=1, source_target_pairs={{4,8},{8,4},{12,16},{16,12},{20,24},{24,20},{5,9},{9,5},{13,17},{1... | collective-permute-start | bytes 384008 | tf_op jit(solution)/shard_map/ppermute | solution.py:558
  48.6 0.7 %collective-permute-done.11.near = bf16[125,4,128]{2,1,0:T(4,128)(2,1)S(1)} collective-permute-done((bf16[125,4,128]{2,1,0:T(4,128)(2,1)S(1)}, bf16[125,4,128]{2,1,0:T(4,128)(2,1)S(1)}, u32[]{:S(2)}, u32[]{:S(2)}) %collective-permute-start.11) | collective-permute-done | bytes 128032 | tf_op jit(solution)/shard_map/ppermute | solution.py:559
  49.2 0.5 shard_map.89
  49.7 0.4 collective-permute-start.13
  50.2 1.0 %collective-permute-start.14 = (bf16[125,2,128]{2,1,0:T(2,128)(2,1)S(1)}, bf16[125,2,128]{2,1,0:T(2,128)(2,1)S(1)}, u32[]{:S(2)}, u32[]{:S(2)}) collective-permute-start(bf16[125,2,128]{2,1,0:T(2,128)(2,1)S(1)} %get-tuple-element.58), channel_id=1, source_target_pairs={{0,1},{1,0},{2,3},{3,2},{4,5},{5,4},{6,7},{7,6},{8,9},{9,8},{10,11... | collective-permute-start | bytes 192008 | tf_op jit(solution)/shard_map/ppermute | solution.py:568
  51.2 3.5 %collective-permute-start.15 = (bf16[125,4,128]{2,1,0:T(4,128)(2,1)S(1)}, bf16[125,4,128]{2,1,0:T(4,128)(2,1)S(1)}, u32[]{:S(2)}, u32[]{:S(2)}) collective-permute-start(bf16[125,4,128]{2,1,0:T(4,128)(2,1)S(1)} %get-tuple-element.61), channel_id=1, source_target_pairs={{0,4},{4,0},{8,12},{12,8},{16,20},{20,16},{24,28},{28,24},{1,5},{5... | collective-permute-start | bytes 384008 | tf_op jit(solution)/shard_map/ppermute | solution.py:559
  54.7 1.9 %shard_map.90 = f32[625,8,128]{2,1,0:T(8,128)S(1)} custom-call(f32[625,8,128]{2,1,0:T(8,128)S(1)} %get-tuple-element.54.state_ref, f32[625,8,128]{2,1,0:T(8,128)S(1)} %get-tuple-element.55.sum_in), custom_call_target="tpu_custom_call" | custom-call | tf_op jit(solution)/shard_map/pallas_call | solution.py:667
  56.6 0.0 collective-permute-done.14.az_near
  56.7 1.4 %shard_map.91 = (f32[5,5,25,8,128]{4,3,2,1,0:T(8,128)S(1)}, f32[5,5,25,8,128]{4,3,2,1,0:T(8,128)}) custom-call(f32[5,5,25,8,128]{4,3,2,1,0:T(8,128)S(1)} %bitcast.11, bf16[125,4,128]{2,1,0:T(4,128)(2,1)S(1)} %collective-permute-done.12.far, bf16[125,2,128]{2,1,0:T(2,128)(2,1)S(1)} %collective-permute-done.13.az_far, ...), custom_call_target="tpu_custom_call", output_to_operand_aliasing={{0}: (0, {})} | custom-call | flops 99999997952 | bytes 1000000000 | tf_op jit(solution)/shard_map/pallas_call | solution.py:675
  58.1 0.3 collective-permute-done.15.near
  58.3 0.9 %shard_map.92 = (f32[5,5,25,8,128]{4,3,2,1,0:T(8,128)S(1)}, f32[5,5,25,8,128]{4,3,2,1,0:T(8,128)}) custom-call(f32[5,5,25,8,128]{4,3,2,1,0:T(8,128)S(1)} %get-tuple-element.59.state_in, f32[5,5,25,8,128]{4,3,2,1,0:T(8,128)} %get-tuple-element.60.out_in, ...), custom_call_target="tpu_custom_call", output_to_operand_aliasing={{0}: (0, {}), {1}: (1, {})} | custom-call | tf_op jit(solution)/shard_map/pallas_call | solution.py:684
  (6 shorter events, 0.0 us)
Async XLA Ops:
  4.3 24.2 %all-to-all-start = ((s16[32,24,384]{2,1,0:T(8,128)(2,1)}), s16[32,24,384]{2,1,0:T(8,128)(2,1)S(1)}, u32[]{:S(2)}, u32[]{:S(2)}) async-start(s16[32,24,384]{2,1,0:T(8,128)(2,1)} %bitcast.15), calls=%async_computation | async-start | bytes 1179648 | tf_op jit(solution)/shard_map/all_to_all | solution.py:606
  14.4 8.4 %copy-start = (f32[625,8,128]{2,1,0:T(8,128)}, f32[625,8,128]{2,1,0:T(8,128)S(1)}, u32[]{:S(2)}) copy-start(f32[625,8,128]{2,1,0:T(8,128)S(1)} %get-tuple-element.33.state_ref.sum_in) | copy-start | bytes 7680004
  14.5 15.7 %collective-permute-start.2 = (bf16[125,4,128]{2,1,0:T(4,128)(2,1)}, bf16[125,4,128]{2,1,0:T(4,128)(2,1)S(1)}, u32[]{:S(2)}, u32[]{:S(2)}) collective-permute-start(bf16[125,4,128]{2,1,0:T(4,128)(2,1)} %get-tuple-element.36), channel_id=1, source_target_pairs={{4,8},{8,4},{12,16},{16,12},{20,24},{24,20},{5,9},{9,5},{13,17},{1... | collective-permute-start | bytes 384008 | tf_op jit(solution)/shard_map/ppermute | solution.py:558
  15.1 7.7 %collective-permute-start = (bf16[125,2,128]{2,1,0:T(2,128)(2,1)S(1)}, bf16[125,2,128]{2,1,0:T(2,128)(2,1)S(1)}, u32[]{:S(2)}, u32[]{:S(2)}) collective-permute-start(bf16[125,2,128]{2,1,0:T(2,128)(2,1)S(1)} %get-tuple-element.34), channel_id=1, source_target_pairs={{1,2},{2,1},{3,0},{0,3},{5,6},{6,5},{7,4},{4,7},{9,10},{10,9},{11,... | collective-permute-start | bytes 192008 | tf_op jit(solution)/shard_map/ppermute | solution.py:568
  16.7 6.1 %collective-permute-start.1 = (bf16[125,2,128]{2,1,0:T(2,128)(2,1)S(1)}, bf16[125,2,128]{2,1,0:T(2,128)(2,1)S(1)}, u32[]{:S(2)}, u32[]{:S(2)}) collective-permute-start(bf16[125,2,128]{2,1,0:T(2,128)(2,1)S(1)} %get-tuple-element.35), channel_id=1, source_target_pairs={{0,1},{1,0},{2,3},{3,2},{4,5},{5,4},{6,7},{7,6},{8,9},{9,8},{10,11... | collective-permute-start | bytes 192008 | tf_op jit(solution)/shard_map/ppermute | solution.py:568
  17.1 14.2 %collective-permute-start.3 = (bf16[125,4,128]{2,1,0:T(4,128)(2,1)S(1)}, bf16[125,4,128]{2,1,0:T(4,128)(2,1)S(1)}, u32[]{:S(2)}, u32[]{:S(2)}) collective-permute-start(bf16[125,4,128]{2,1,0:T(4,128)(2,1)S(1)} %get-tuple-element.38), channel_id=1, source_target_pairs={{0,4},{4,0},{8,12},{12,8},{16,20},{20,16},{24,28},{28,24},{1,5},{5... | collective-permute-start | bytes 384008 | tf_op jit(solution)/shard_map/ppermute | solution.py:559
  30.5 3.0 %copy-start.1 = (f32[625,8,128]{2,1,0:T(8,128)S(1)}, f32[625,8,128]{2,1,0:T(8,128)}, u32[]{:S(2)}) copy-start(f32[625,8,128]{2,1,0:T(8,128)} %copy-done) | copy-start | bytes 7680004
  30.5 7.8 %collective-permute-start.4 = (bf16[125,4,128]{2,1,0:T(4,128)(2,1)S(1)}, bf16[125,4,128]{2,1,0:T(4,128)(2,1)S(1)}, u32[]{:S(2)}, u32[]{:S(2)}) collective-permute-start(bf16[125,4,128]{2,1,0:T(4,128)(2,1)S(1)} %get-tuple-element.41), channel_id=1, source_target_pairs={{4,8},{8,4},{12,16},{16,12},{20,24},{24,20},{5,9},{9,5},{13,17},{1... | collective-permute-start | bytes 384008 | tf_op jit(solution)/shard_map/ppermute | solution.py:558
  31.8 6.4 %collective-permute-start.5 = (bf16[125,2,128]{2,1,0:T(2,128)(2,1)S(1)}, bf16[125,2,128]{2,1,0:T(2,128)(2,1)S(1)}, u32[]{:S(2)}, u32[]{:S(2)}) collective-permute-start(bf16[125,2,128]{2,1,0:T(2,128)(2,1)S(1)} %get-tuple-element.42), channel_id=1, source_target_pairs={{1,2},{2,1},{3,0},{0,3},{5,6},{6,5},{7,4},{4,7},{9,10},{10,9},{11,... | collective-permute-start | bytes 192008 | tf_op jit(solution)/shard_map/ppermute | solution.py:568
  32.8 5.4 %collective-permute-start.6 = (bf16[125,2,128]{2,1,0:T(2,128)(2,1)S(1)}, bf16[125,2,128]{2,1,0:T(2,128)(2,1)S(1)}, u32[]{:S(2)}, u32[]{:S(2)}) collective-permute-start(bf16[125,2,128]{2,1,0:T(2,128)(2,1)S(1)} %get-tuple-element.43), channel_id=1, source_target_pairs={{0,1},{1,0},{2,3},{3,2},{4,5},{5,4},{6,7},{7,6},{8,9},{9,8},{10,11... | collective-permute-start | bytes 192008 | tf_op jit(solution)/shard_map/ppermute | solution.py:568
  35.1 6.8 %collective-permute-start.7 = (bf16[125,4,128]{2,1,0:T(4,128)(2,1)S(1)}, bf16[125,4,128]{2,1,0:T(4,128)(2,1)S(1)}, u32[]{:S(2)}, u32[]{:S(2)}) collective-permute-start(bf16[125,4,128]{2,1,0:T(4,128)(2,1)S(1)} %get-tuple-element.45), channel_id=1, source_target_pairs={{0,4},{4,0},{8,12},{12,8},{16,20},{20,16},{24,28},{28,24},{1,5},{5... | collective-permute-start | bytes 384008 | tf_op jit(solution)/shard_map/ppermute | solution.py:559
  38.7 8.7 %collective-permute-start.8 = (bf16[125,4,128]{2,1,0:T(4,128)(2,1)S(1)}, bf16[125,4,128]{2,1,0:T(4,128)(2,1)S(1)}, u32[]{:S(2)}, u32[]{:S(2)}) collective-permute-start(bf16[125,4,128]{2,1,0:T(4,128)(2,1)S(1)} %get-tuple-element.49), channel_id=1, source_target_pairs={{4,8},{8,4},{12,16},{16,12},{20,24},{24,20},{5,9},{9,5},{13,17},{1... | collective-permute-start | bytes 384008 | tf_op jit(solution)/shard_map/ppermute | solution.py:558
  42.2 5.2 %collective-permute-start.9 = (bf16[125,2,128]{2,1,0:T(2,128)(2,1)S(1)}, bf16[125,2,128]{2,1,0:T(2,128)(2,1)S(1)}, u32[]{:S(2)}, u32[]{:S(2)}) collective-permute-start(bf16[125,2,128]{2,1,0:T(2,128)(2,1)S(1)} %get-tuple-element.50), channel_id=1, source_target_pairs={{1,2},{2,1},{3,0},{0,3},{5,6},{6,5},{7,4},{4,7},{9,10},{10,9},{11,... | collective-permute-start | bytes 192008 | tf_op jit(solution)/shard_map/ppermute | solution.py:568
  42.8 4.7 %collective-permute-start.10 = (bf16[125,2,128]{2,1,0:T(2,128)(2,1)S(1)}, bf16[125,2,128]{2,1,0:T(2,128)(2,1)S(1)}, u32[]{:S(2)}, u32[]{:S(2)}) collective-permute-start(bf16[125,2,128]{2,1,0:T(2,128)(2,1)S(1)} %get-tuple-element.51), channel_id=1, source_target_pairs={{0,1},{1,0},{2,3},{3,2},{4,5},{5,4},{6,7},{7,6},{8,9},{9,8},{10,11... | collective-permute-start | bytes 192008 | tf_op jit(solution)/shard_map/ppermute | solution.py:568
  43.8 5.4 %collective-permute-start.11 = (bf16[125,4,128]{2,1,0:T(4,128)(2,1)S(1)}, bf16[125,4,128]{2,1,0:T(4,128)(2,1)S(1)}, u32[]{:S(2)}, u32[]{:S(2)}) collective-permute-start(bf16[125,4,128]{2,1,0:T(4,128)(2,1)S(1)} %get-tuple-element.53), channel_id=1, source_target_pairs={{0,4},{4,0},{8,12},{12,8},{16,20},{20,16},{24,28},{28,24},{1,5},{5... | collective-permute-start | bytes 384008 | tf_op jit(solution)/shard_map/ppermute | solution.py:559
  47.9 8.8 %collective-permute-start.12 = (bf16[125,4,128]{2,1,0:T(4,128)(2,1)S(1)}, bf16[125,4,128]{2,1,0:T(4,128)(2,1)S(1)}, u32[]{:S(2)}, u32[]{:S(2)}) collective-permute-start(bf16[125,4,128]{2,1,0:T(4,128)(2,1)S(1)} %get-tuple-element.56), channel_id=1, source_target_pairs={{4,8},{8,4},{12,16},{16,12},{20,24},{24,20},{5,9},{9,5},{13,17},{1... | collective-permute-start | bytes 384008 | tf_op jit(solution)/shard_map/ppermute | solution.py:558
  49.7 6.9 %collective-permute-start.13 = (bf16[125,2,128]{2,1,0:T(2,128)(2,1)S(1)}, bf16[125,2,128]{2,1,0:T(2,128)(2,1)S(1)}, u32[]{:S(2)}, u32[]{:S(2)}) collective-permute-start(bf16[125,2,128]{2,1,0:T(2,128)(2,1)S(1)} %get-tuple-element.57), channel_id=1, source_target_pairs={{1,2},{2,1},{3,0},{0,3},{5,6},{6,5},{7,4},{4,7},{9,10},{10,9},{11,... | collective-permute-start | bytes 192008 | tf_op jit(solution)/shard_map/ppermute | solution.py:568
  50.2 6.5 %collective-permute-start.14 = (bf16[125,2,128]{2,1,0:T(2,128)(2,1)S(1)}, bf16[125,2,128]{2,1,0:T(2,128)(2,1)S(1)}, u32[]{:S(2)}, u32[]{:S(2)}) collective-permute-start(bf16[125,2,128]{2,1,0:T(2,128)(2,1)S(1)} %get-tuple-element.58), channel_id=1, source_target_pairs={{0,1},{1,0},{2,3},{3,2},{4,5},{5,4},{6,7},{7,6},{8,9},{9,8},{10,11... | collective-permute-start | bytes 192008 | tf_op jit(solution)/shard_map/ppermute | solution.py:568
  51.2 7.1 %collective-permute-start.15 = (bf16[125,4,128]{2,1,0:T(4,128)(2,1)S(1)}, bf16[125,4,128]{2,1,0:T(4,128)(2,1)S(1)}, u32[]{:S(2)}, u32[]{:S(2)}) collective-permute-start(bf16[125,4,128]{2,1,0:T(4,128)(2,1)S(1)} %get-tuple-element.61), channel_id=1, source_target_pairs={{0,4},{4,0},{8,12},{12,8},{16,20},{20,16},{24,28},{28,24},{1,5},{5... | collective-permute-start | bytes 384008 | tf_op jit(solution)/shard_map/ppermute | solution.py:559

commit v7 on v5

--- a/solution.py
+++ b/solution.py
@@ -184,11 +184,12 @@
 
 
 def volume_and_source_kernel(
-    scale, state_ref, sum_in, source_ref, out_ref, sum_ref, out_hbm, sem
+    scale, state_in, sum_in, source_ref, state_ref, out_ref, sum_ref, out_hbm, sem
 ):
     rows = pl.ds(0, out_hbm.shape[0])
     copy = pltpu.make_async_copy(source_ref.at[rows], out_hbm, sem.at[0])
     copy.start()
+    add_source(state_ref, source_ref, STEP_SCALES[0], INNER)
     volume_kernel(scale, state_ref, sum_in, out_ref, sum_ref)
     copy.wait()
 
@@ -324,6 +325,9 @@
     pack_az(state_ref, az_far, az_near)
 
 
+INNER = [a * 25 + n for a in (1, 2, 3) for n in range(5, 20)]
+
+
 def add_source(state_ref, source_ref, scale, nodes):
     for node in nodes:
         for c in range(3):
@@ -345,7 +349,7 @@
 
 def first_near_kernel(scale, state_in, source_ref, near, state_ref, near_out, *az_out):
     add_near(state_ref, near, scale)
-    add_source(state_ref, source_ref, scale, range(25, 100))
+    add_source(state_ref, source_ref, scale, [n for n in range(25, 100) if n not in INNER])
     pack_near(state_ref, near_out)
     pack_az(state_ref, *az_out)
 
@@ -373,13 +377,14 @@
     for part in inside:
         part.start()
     add_az(state_ref, az_far, az_near, weight, final=True)
-    add_far(state_ref, far, weight, final=True)
-    outside = [copy(3, far_plane, pl.ds(0, 25))]
-    outside += [copy(4 + k, k + 1, pl.ds(0, 5)) for k in range(3)]
-    outside += [copy(7 + k, k + 1, pl.ds(20, 5)) for k in range(3)]
+    outside = [copy(3 + k, k + 1, pl.ds(0, 5)) for k in range(3)]
+    outside += [copy(6 + k, k + 1, pl.ds(20, 5)) for k in range(3)]
     for part in outside:
         part.start()
-    for part in inside + outside:
+    add_far(state_ref, far, weight, final=True)
+    face = copy(9, far_plane, pl.ds(0, 25))
+    face.start()
+    for part in inside + outside + [face]:
         part.wait()
 
 
@@ -634,11 +639,12 @@
     )(rate, source, near)
     _, near = swap(None, near)
     az_far, az_near = turn(az_far, az_near)
-    moved, total, source = call(
+    _, moved, total, source = call(
         functools.partial(volume_and_source_kernel, STEP_SCALES[1]),
-        [vmem_state, vmem_state, pltpu.HBM(source_shape, f32)],
+        [vmem_state, vmem_state, vmem_state, pltpu.HBM(source_shape, f32)],
         3,
-        [IN_VMEM, IN_VMEM, IN_HBM],
+        [IN_VMEM, IN_VMEM, IN_VMEM, IN_HBM],
+        aliases={0: 0},
         scratch=[pltpu.SemaphoreType.DMA((1,))],
     )(rate, state, source)
 

time: 59.4 us -> 58.9 us (level)
  waiting for transfers between devices: 8.62 us -> 7.04 us
  starting transfers between devices: 29.4 us -> 30.5 us
    ppermute x4, waiting for transfers between devices: 3.3 us -> 1.73 us  [swap(): lax.ppermute(near, 'ax', pairs[0])]
    ppermute x4, starting transfers between devices: 12.7 us -> 13.9 us  [swap(): lax.ppermute(near, 'ax', pairs[0])]
  transfers between devices with their start and end apart: 17 -> 17, of which waited for: 4 -> 4; matrix products, arithmetic and copies ran while one was open for 0% -> 0% of each run, Pallas kernels for 26% -> 27%
where the time goes in v7:
time: 58.9 us; the launch traced here: 58.6 us
  starting transfers between devices  30.5 us (52%)
  Pallas kernels  20.1 us (34%)
  waiting for transfers between devices  7.04 us (12%)
  between operations  0.91 us (2%)
    ppermute x4, starting transfers between devices, swap(): lax.ppermute(near, 'ax', pairs[0])  13.9 us
    all_to_all x1, starting transfers between devices, body(): lax.all_to_all(buffer, ('ax', 'az'), split_axis=0, concat_axis=0, tiled=T...  7.3 us
    all_to_all x1, waiting for transfers between devices, body(): lax.all_to_all(buffer, ('ax', 'az'), split_axis=0, concat_axis=0, tiled=T...  5.29 us
    pallas_call x1, Pallas kernels, body(): call(functools.partial(contribution_kernel, capacity, devices), pltpu.HBM...  3.64 us
    ppermute x4, starting transfers between devices, turn(): lax.ppermute(far, 'az', pairs[1])  3.63 us
    ppermute x4, starting transfers between devices, turn(): lax.ppermute(near, 'az', pairs[0])  2.86 us
    pallas_call x1, Pallas kernels, body(): call(load_kernel, [vmem_state] + face_shapes, [IN_HBM], scratch=[pltpu.Se...  2.85 us
    ppermute x4, starting transfers between devices, swap(): lax.ppermute(far, 'ax', pairs[1])  2.81 us
  transfers between devices with their start and end apart: 17, of which 4 were waited for; matrix products, arithmetic and copies ran while one was open for 0% of the time, Pallas kernels for 27%

profile of v7, /device:TPU:0, one launch (start us, length us, event | category | flops | bytes accessed | tf_op | source)
XLA Modules:
  0.0 58.6 jit_solution(9777129359773765962)
XLA Ops:
  0.6 3.6 %shard_map.80 = s16[768,384]{1,0:T(8,128)(2,1)} custom-call(bf16[3,256,512]{2,1,0:T(8,128)(2,1)} %bitcast.16, s32[1,256]{1,0:T(1,128)} %bitcast.18, s32[1,256]{1,0:T(1,128)} %bitcast.19, s32[1,256]{1,0:T(1,128)} %bitcast.20, bf16[125,2,512]{2,1,0:T(2,128)(2,1)} %bitcast.17), custom_call_target="tpu_custom_call" | custom-call | tf_op jit(solution)/shard_map/pallas_call | solution.py:588
  4.3 7.3 %all-to-all-start = ((s16[32,24,384]{2,1,0:T(8,128)(2,1)}), s16[32,24,384]{2,1,0:T(8,128)(2,1)S(1)}, u32[]{:S(2)}, u32[]{:S(2)}) async-start(s16[32,24,384]{2,1,0:T(8,128)(2,1)} %bitcast.15), calls=%async_computation | async-start | bytes 1179648 | tf_op jit(solution)/shard_map/all_to_all | solution.py:611
  11.6 2.8 %shard_map.77 = (f32[625,8,128]{2,1,0:T(8,128)S(1)}, bf16[125,4,128]{2,1,0:T(4,128)(2,1)}, bf16[125,4,128]{2,1,0:T(4,128)(2,1)S(1)}, bf16[125,2,128]{2,1,0:T(2,128)(2,1)S(1)}, bf16[125,2,128]{2,1,0:T(2,128)(2,1)S(1)}) custom-call(f32[625,8,128]{2,1,0:T(8,128)} %bitcast.13), custom_call_target="tpu_custom_call" | custom-call | tf_op jit(solution)/shard_map/pallas_call | solution.py:613
  14.4 0.0 copy-start
  14.5 0.7 %collective-permute-start.2 = (bf16[125,4,128]{2,1,0:T(4,128)(2,1)}, bf16[125,4,128]{2,1,0:T(4,128)(2,1)S(1)}, u32[]{:S(2)}, u32[]{:S(2)}) collective-permute-start(bf16[125,4,128]{2,1,0:T(4,128)(2,1)} %get-tuple-element.36), channel_id=1, source_target_pairs={{4,8},{8,4},{12,16},{16,12},{20,24},{24,20},{5,9},{9,5},{13,17},{1... | collective-permute-start | bytes 384008 | tf_op jit(solution)/shard_map/ppermute | solution.py:563
  15.1 1.6 %collective-permute-start = (bf16[125,2,128]{2,1,0:T(2,128)(2,1)S(1)}, bf16[125,2,128]{2,1,0:T(2,128)(2,1)S(1)}, u32[]{:S(2)}, u32[]{:S(2)}) collective-permute-start(bf16[125,2,128]{2,1,0:T(2,128)(2,1)S(1)} %get-tuple-element.34), channel_id=1, source_target_pairs={{1,2},{2,1},{3,0},{0,3},{5,6},{6,5},{7,4},{4,7},{9,10},{10,9},{11,... | collective-permute-start | bytes 192008 | tf_op jit(solution)/shard_map/ppermute | solution.py:573
  16.7 0.4 collective-permute-start.1
  17.1 4.2 %collective-permute-start.3 = (bf16[125,4,128]{2,1,0:T(4,128)(2,1)S(1)}, bf16[125,4,128]{2,1,0:T(4,128)(2,1)S(1)}, u32[]{:S(2)}, u32[]{:S(2)}) collective-permute-start(bf16[125,4,128]{2,1,0:T(4,128)(2,1)S(1)} %get-tuple-element.38), channel_id=1, source_target_pairs={{0,4},{4,0},{8,12},{12,8},{16,20},{20,16},{24,28},{28,24},{1,5},{5... | collective-permute-start | bytes 384008 | tf_op jit(solution)/shard_map/ppermute | solution.py:564
  21.2 1.6 %shard_map.78.state_in = f32[625,8,128]{2,1,0:T(8,128)S(1)} custom-call(f32[625,8,128]{2,1,0:T(8,128)S(1)} %get-tuple-element.33.state_ref.sum_in), custom_call_target="tpu_custom_call" | custom-call | tf_op jit(solution)/shard_map/pallas_call | solution.py:621
  22.9 0.0 collective-permute-done.az_far
  22.9 0.0 collective-permute-done.1.az_near
  22.9 0.3 shard_map.79.state_in
  23.2 5.3 %all-to-all-done = s16[32,24,384]{2,1,0:T(8,128)(2,1)S(1)} async-done(((s16[32,24,384]{2,1,0:T(8,128)(2,1)}), s16[32,24,384]{2,1,0:T(8,128)(2,1)S(1)}, u32[]{:S(2)}, u32[]{:S(2)}) %all-to-all-start) | async-done | bytes 589856 | tf_op jit(solution)/shard_map/all_to_all | solution.py:611
  28.5 1.7 %shard_map.81.source_ref = f32[3024,128]{1,0:T(8,128)S(1)} custom-call(s16[768,384]{1,0:T(8,128)(2,1)S(1)} %bitcast.12), custom_call_target="tpu_custom_call" | custom-call | tf_op jit(solution)/shard_map/pallas_call | solution.py:626
  30.2 0.0 collective-permute-done.2.far
  30.2 0.3 shard_map.82
  30.5 0.0 copy-start.1
  30.5 0.8 %collective-permute-start.4 = (bf16[125,4,128]{2,1,0:T(4,128)(2,1)S(1)}, bf16[125,4,128]{2,1,0:T(4,128)(2,1)S(1)}, u32[]{:S(2)}, u32[]{:S(2)}) collective-permute-start(bf16[125,4,128]{2,1,0:T(4,128)(2,1)S(1)} %get-tuple-element.41), channel_id=1, source_target_pairs={{4,8},{8,4},{12,16},{16,12},{20,24},{24,20},{5,9},{9,5},{13,17},{1... | collective-permute-start | bytes 384008 | tf_op jit(solution)/shard_map/ppermute | solution.py:563
  31.3 0.4 shard_map.83
  31.8 1.0 %collective-permute-start.5 = (bf16[125,2,128]{2,1,0:T(2,128)(2,1)S(1)}, bf16[125,2,128]{2,1,0:T(2,128)(2,1)S(1)}, u32[]{:S(2)}, u32[]{:S(2)}) collective-permute-start(bf16[125,2,128]{2,1,0:T(2,128)(2,1)S(1)} %get-tuple-element.42), channel_id=1, source_target_pairs={{1,2},{2,1},{3,0},{0,3},{5,6},{6,5},{7,4},{4,7},{9,10},{10,9},{11,... | collective-permute-start | bytes 192008 | tf_op jit(solution)/shard_map/ppermute | solution.py:573
  32.8 0.6 %collective-permute-start.6 = (bf16[125,2,128]{2,1,0:T(2,128)(2,1)S(1)}, bf16[125,2,128]{2,1,0:T(2,128)(2,1)S(1)}, u32[]{:S(2)}, u32[]{:S(2)}) collective-permute-start(bf16[125,2,128]{2,1,0:T(2,128)(2,1)S(1)} %get-tuple-element.43), channel_id=1, source_target_pairs={{0,1},{1,0},{2,3},{3,2},{4,5},{5,4},{6,7},{7,6},{8,9},{9,8},{10,11... | collective-permute-start | bytes 192008 | tf_op jit(solution)/shard_map/ppermute | solution.py:573
  33.4 3.1 %collective-permute-start.7 = (bf16[125,4,128]{2,1,0:T(4,128)(2,1)S(1)}, bf16[125,4,128]{2,1,0:T(4,128)(2,1)S(1)}, u32[]{:S(2)}, u32[]{:S(2)}) collective-permute-start(bf16[125,4,128]{2,1,0:T(4,128)(2,1)S(1)} %get-tuple-element.45), channel_id=1, source_target_pairs={{0,4},{4,0},{8,12},{12,8},{16,20},{20,16},{24,28},{28,24},{1,5},{5... | collective-permute-start | bytes 384008 | tf_op jit(solution)/shard_map/ppermute | solution.py:564
  36.5 1.8 %shard_map.84 = (f32[625,8,128]{2,1,0:T(8,128)S(1)}, f32[625,8,128]{2,1,0:T(8,128)S(1)}, f32[625,8,128]{2,1,0:T(8,128)S(1)}, f32[3000,128]{1,0:T(8,128)}) custom-call(f32[625,8,128]{2,1,0:T(8,128)S(1)} %get-tuple-element.39.state_in, f32[625,8,128]{2,1,0:T(8,128)S(1)} %copy-done.1, f32[3024,128]{1,0:T(8,128)S(1)} %shard_map.81.source_ref), custom_call_target="tpu_custom_call", output_to_operand_aliasing={{0}: (0, {})} | custom-call | tf_op jit(solution)/shard_map/pallas_call | solution.py:642
  38.3 0.0 collective-permute-done.5.az_far
  38.3 0.0 collective-permute-done.6.az_near
  38.3 0.5 shard_map.85
  38.8 0.7 %collective-permute-start.8 = (bf16[125,4,128]{2,1,0:T(4,128)(2,1)S(1)}, bf16[125,4,128]{2,1,0:T(4,128)(2,1)S(1)}, u32[]{:S(2)}, u32[]{:S(2)}) collective-permute-start(bf16[125,4,128]{2,1,0:T(4,128)(2,1)S(1)} %get-tuple-element.49), channel_id=1, source_target_pairs={{4,8},{8,4},{12,16},{16,12},{20,24},{24,20},{5,9},{9,5},{13,17},{1... | collective-permute-start | bytes 384008 | tf_op jit(solution)/shard_map/ppermute | solution.py:563
  39.5 0.7 %collective-permute-done.7.near = bf16[125,4,128]{2,1,0:T(4,128)(2,1)S(1)} collective-permute-done((bf16[125,4,128]{2,1,0:T(4,128)(2,1)S(1)}, bf16[125,4,128]{2,1,0:T(4,128)(2,1)S(1)}, u32[]{:S(2)}, u32[]{:S(2)}) %collective-permute-start.7) | collective-permute-done | bytes 128032 | tf_op jit(solution)/shard_map/ppermute | solution.py:564
  40.2 0.3 shard_map.86
  40.6 0.6 %collective-permute-start.9 = (bf16[125,2,128]{2,1,0:T(2,128)(2,1)S(1)}, bf16[125,2,128]{2,1,0:T(2,128)(2,1)S(1)}, u32[]{:S(2)}, u32[]{:S(2)}) collective-permute-start(bf16[125,2,128]{2,1,0:T(2,128)(2,1)S(1)} %get-tuple-element.50), channel_id=1, source_target_pairs={{1,2},{2,1},{3,0},{0,3},{5,6},{6,5},{7,4},{4,7},{9,10},{10,9},{11,... | collective-permute-start | bytes 192008 | tf_op jit(solution)/shard_map/ppermute | solution.py:573
  41.2 0.8 %collective-permute-start.10 = (bf16[125,2,128]{2,1,0:T(2,128)(2,1)S(1)}, bf16[125,2,128]{2,1,0:T(2,128)(2,1)S(1)}, u32[]{:S(2)}, u32[]{:S(2)}) collective-permute-start(bf16[125,2,128]{2,1,0:T(2,128)(2,1)S(1)} %get-tuple-element.51), channel_id=1, source_target_pairs={{0,1},{1,0},{2,3},{3,2},{4,5},{5,4},{6,7},{7,6},{8,9},{9,8},{10,11... | collective-permute-start | bytes 192008 | tf_op jit(solution)/shard_map/ppermute | solution.py:573
  42.0 3.7 %collective-permute-start.11 = (bf16[125,4,128]{2,1,0:T(4,128)(2,1)S(1)}, bf16[125,4,128]{2,1,0:T(4,128)(2,1)S(1)}, u32[]{:S(2)}, u32[]{:S(2)}) collective-permute-start(bf16[125,4,128]{2,1,0:T(4,128)(2,1)S(1)} %get-tuple-element.53), channel_id=1, source_target_pairs={{0,4},{4,0},{8,12},{12,8},{16,20},{20,16},{24,28},{28,24},{1,5},{5... | collective-permute-start | bytes 384008 | tf_op jit(solution)/shard_map/ppermute | solution.py:564
  45.7 1.7 %shard_map.87 = (f32[625,8,128]{2,1,0:T(8,128)S(1)}, f32[625,8,128]{2,1,0:T(8,128)S(1)}) custom-call(f32[625,8,128]{2,1,0:T(8,128)S(1)} %get-tuple-element.46.state_ref, f32[625,8,128]{2,1,0:T(8,128)S(1)} %get-tuple-element.47.sum_in), custom_call_target="tpu_custom_call" | custom-call | tf_op jit(solution)/shard_map/pallas_call | solution.py:669
  47.4 0.0 collective-permute-done.9.az_far
  47.5 0.0 collective-permute-done.10.az_near
  47.5 0.5 shard_map.88
  47.9 0.7 %collective-permute-start.12 = (bf16[125,4,128]{2,1,0:T(4,128)(2,1)S(1)}, bf16[125,4,128]{2,1,0:T(4,128)(2,1)S(1)}, u32[]{:S(2)}, u32[]{:S(2)}) collective-permute-start(bf16[125,4,128]{2,1,0:T(4,128)(2,1)S(1)} %get-tuple-element.56), channel_id=1, source_target_pairs={{4,8},{8,4},{12,16},{16,12},{20,24},{24,20},{5,9},{9,5},{13,17},{1... | collective-permute-start | bytes 384008 | tf_op jit(solution)/shard_map/ppermute | solution.py:563
  48.6 0.7 %collective-permute-done.11.near = bf16[125,4,128]{2,1,0:T(4,128)(2,1)S(1)} collective-permute-done((bf16[125,4,128]{2,1,0:T(4,128)(2,1)S(1)}, bf16[125,4,128]{2,1,0:T(4,128)(2,1)S(1)}, u32[]{:S(2)}, u32[]{:S(2)}) %collective-permute-start.11) | collective-permute-done | bytes 128032 | tf_op jit(solution)/shard_map/ppermute | solution.py:564
  49.3 0.3 shard_map.89
  49.6 0.4 collective-permute-start.13
  50.0 1.0 %collective-permute-start.14 = (bf16[125,2,128]{2,1,0:T(2,128)(2,1)S(1)}, bf16[125,2,128]{2,1,0:T(2,128)(2,1)S(1)}, u32[]{:S(2)}, u32[]{:S(2)}) collective-permute-start(bf16[125,2,128]{2,1,0:T(2,128)(2,1)S(1)} %get-tuple-element.58), channel_id=1, source_target_pairs={{0,1},{1,0},{2,3},{3,2},{4,5},{5,4},{6,7},{7,6},{8,9},{9,8},{10,11... | collective-permute-start | bytes 192008 | tf_op jit(solution)/shard_map/ppermute | solution.py:573
  51.1 3.0 %collective-permute-start.15 = (bf16[125,4,128]{2,1,0:T(4,128)(2,1)S(1)}, bf16[125,4,128]{2,1,0:T(4,128)(2,1)S(1)}, u32[]{:S(2)}, u32[]{:S(2)}) collective-permute-start(bf16[125,4,128]{2,1,0:T(4,128)(2,1)S(1)} %get-tuple-element.61), channel_id=1, source_target_pairs={{0,4},{4,0},{8,12},{12,8},{16,20},{20,16},{24,28},{28,24},{1,5},{5... | collective-permute-start | bytes 384008 | tf_op jit(solution)/shard_map/ppermute | solution.py:564
  54.1 1.8 %shard_map.90 = f32[625,8,128]{2,1,0:T(8,128)S(1)} custom-call(f32[625,8,128]{2,1,0:T(8,128)S(1)} %get-tuple-element.54.state_ref, f32[625,8,128]{2,1,0:T(8,128)S(1)} %get-tuple-element.55.sum_in), custom_call_target="tpu_custom_call" | custom-call | tf_op jit(solution)/shard_map/pallas_call | solution.py:673
  55.9 0.0 collective-permute-done.13.az_far
  55.9 0.0 collective-permute-done.14.az_near
  55.9 1.4 %shard_map.91 = (f32[5,5,25,8,128]{4,3,2,1,0:T(8,128)S(1)}, f32[5,5,25,8,128]{4,3,2,1,0:T(8,128)}) custom-call(f32[5,5,25,8,128]{4,3,2,1,0:T(8,128)S(1)} %bitcast.11, bf16[125,4,128]{2,1,0:T(4,128)(2,1)S(1)} %collective-permute-done.12.far, bf16[125,2,128]{2,1,0:T(2,128)(2,1)S(1)} %collective-permute-done.13.az_far, ...), custom_call_target="tpu_custom_call", output_to_operand_aliasing={{0}: (0, {})} | custom-call | flops 99999997952 | bytes 1000000000 | tf_op jit(solution)/shard_map/pallas_call | solution.py:681
  57.3 0.3 collective-permute-done.15.near
  57.7 0.9 %shard_map.92 = (f32[5,5,25,8,128]{4,3,2,1,0:T(8,128)S(1)}, f32[5,5,25,8,128]{4,3,2,1,0:T(8,128)}) custom-call(f32[5,5,25,8,128]{4,3,2,1,0:T(8,128)S(1)} %get-tuple-element.59.state_in, f32[5,5,25,8,128]{4,3,2,1,0:T(8,128)} %get-tuple-element.60.out_in, ...), custom_call_target="tpu_custom_call", output_to_operand_aliasing={{0}: (0, {}), {1}: (1, {})} | custom-call | tf_op jit(solution)/shard_map/pallas_call | solution.py:690
  (6 shorter events, 0.0 us)
Async XLA Ops:
  4.3 24.2 %all-to-all-start = ((s16[32,24,384]{2,1,0:T(8,128)(2,1)}), s16[32,24,384]{2,1,0:T(8,128)(2,1)S(1)}, u32[]{:S(2)}, u32[]{:S(2)}) async-start(s16[32,24,384]{2,1,0:T(8,128)(2,1)} %bitcast.15), calls=%async_computation | async-start | bytes 1179648 | tf_op jit(solution)/shard_map/all_to_all | solution.py:611
  14.4 8.4 %copy-start = (f32[625,8,128]{2,1,0:T(8,128)}, f32[625,8,128]{2,1,0:T(8,128)S(1)}, u32[]{:S(2)}) copy-start(f32[625,8,128]{2,1,0:T(8,128)S(1)} %get-tuple-element.33.state_ref.sum_in) | copy-start | bytes 7680004
  14.5 15.7 %collective-permute-start.2 = (bf16[125,4,128]{2,1,0:T(4,128)(2,1)}, bf16[125,4,128]{2,1,0:T(4,128)(2,1)S(1)}, u32[]{:S(2)}, u32[]{:S(2)}) collective-permute-start(bf16[125,4,128]{2,1,0:T(4,128)(2,1)} %get-tuple-element.36), channel_id=1, source_target_pairs={{4,8},{8,4},{12,16},{16,12},{20,24},{24,20},{5,9},{9,5},{13,17},{1... | collective-permute-start | bytes 384008 | tf_op jit(solution)/shard_map/ppermute | solution.py:563
  15.1 7.7 %collective-permute-start = (bf16[125,2,128]{2,1,0:T(2,128)(2,1)S(1)}, bf16[125,2,128]{2,1,0:T(2,128)(2,1)S(1)}, u32[]{:S(2)}, u32[]{:S(2)}) collective-permute-start(bf16[125,2,128]{2,1,0:T(2,128)(2,1)S(1)} %get-tuple-element.34), channel_id=1, source_target_pairs={{1,2},{2,1},{3,0},{0,3},{5,6},{6,5},{7,4},{4,7},{9,10},{10,9},{11,... | collective-permute-start | bytes 192008 | tf_op jit(solution)/shard_map/ppermute | solution.py:573
  16.7 6.1 %collective-permute-start.1 = (bf16[125,2,128]{2,1,0:T(2,128)(2,1)S(1)}, bf16[125,2,128]{2,1,0:T(2,128)(2,1)S(1)}, u32[]{:S(2)}, u32[]{:S(2)}) collective-permute-start(bf16[125,2,128]{2,1,0:T(2,128)(2,1)S(1)} %get-tuple-element.35), channel_id=1, source_target_pairs={{0,1},{1,0},{2,3},{3,2},{4,5},{5,4},{6,7},{7,6},{8,9},{9,8},{10,11... | collective-permute-start | bytes 192008 | tf_op jit(solution)/shard_map/ppermute | solution.py:573
  17.1 14.2 %collective-permute-start.3 = (bf16[125,4,128]{2,1,0:T(4,128)(2,1)S(1)}, bf16[125,4,128]{2,1,0:T(4,128)(2,1)S(1)}, u32[]{:S(2)}, u32[]{:S(2)}) collective-permute-start(bf16[125,4,128]{2,1,0:T(4,128)(2,1)S(1)} %get-tuple-element.38), channel_id=1, source_target_pairs={{0,4},{4,0},{8,12},{12,8},{16,20},{20,16},{24,28},{28,24},{1,5},{5... | collective-permute-start | bytes 384008 | tf_op jit(solution)/shard_map/ppermute | solution.py:564
  30.5 6.0 %copy-start.1 = (f32[625,8,128]{2,1,0:T(8,128)S(1)}, f32[625,8,128]{2,1,0:T(8,128)}, u32[]{:S(2)}) copy-start(f32[625,8,128]{2,1,0:T(8,128)} %copy-done) | copy-start | bytes 7680004
  30.5 7.8 %collective-permute-start.4 = (bf16[125,4,128]{2,1,0:T(4,128)(2,1)S(1)}, bf16[125,4,128]{2,1,0:T(4,128)(2,1)S(1)}, u32[]{:S(2)}, u32[]{:S(2)}) collective-permute-start(bf16[125,4,128]{2,1,0:T(4,128)(2,1)S(1)} %get-tuple-element.41), channel_id=1, source_target_pairs={{4,8},{8,4},{12,16},{16,12},{20,24},{24,20},{5,9},{9,5},{13,17},{1... | collective-permute-start | bytes 384008 | tf_op jit(solution)/shard_map/ppermute | solution.py:563
  31.8 6.6 %collective-permute-start.5 = (bf16[125,2,128]{2,1,0:T(2,128)(2,1)S(1)}, bf16[125,2,128]{2,1,0:T(2,128)(2,1)S(1)}, u32[]{:S(2)}, u32[]{:S(2)}) collective-permute-start(bf16[125,2,128]{2,1,0:T(2,128)(2,1)S(1)} %get-tuple-element.42), channel_id=1, source_target_pairs={{1,2},{2,1},{3,0},{0,3},{5,6},{6,5},{7,4},{4,7},{9,10},{10,9},{11,... | collective-permute-start | bytes 192008 | tf_op jit(solution)/shard_map/ppermute | solution.py:573
  32.8 5.5 %collective-permute-start.6 = (bf16[125,2,128]{2,1,0:T(2,128)(2,1)S(1)}, bf16[125,2,128]{2,1,0:T(2,128)(2,1)S(1)}, u32[]{:S(2)}, u32[]{:S(2)}) collective-permute-start(bf16[125,2,128]{2,1,0:T(2,128)(2,1)S(1)} %get-tuple-element.43), channel_id=1, source_target_pairs={{0,1},{1,0},{2,3},{3,2},{4,5},{5,4},{6,7},{7,6},{8,9},{9,8},{10,11... | collective-permute-start | bytes 192008 | tf_op jit(solution)/shard_map/ppermute | solution.py:573
  33.4 6.8 %collective-permute-start.7 = (bf16[125,4,128]{2,1,0:T(4,128)(2,1)S(1)}, bf16[125,4,128]{2,1,0:T(4,128)(2,1)S(1)}, u32[]{:S(2)}, u32[]{:S(2)}) collective-permute-start(bf16[125,4,128]{2,1,0:T(4,128)(2,1)S(1)} %get-tuple-element.45), channel_id=1, source_target_pairs={{0,4},{4,0},{8,12},{12,8},{16,20},{20,16},{24,28},{28,24},{1,5},{5... | collective-permute-start | bytes 384008 | tf_op jit(solution)/shard_map/ppermute | solution.py:564
  38.8 8.7 %collective-permute-start.8 = (bf16[125,4,128]{2,1,0:T(4,128)(2,1)S(1)}, bf16[125,4,128]{2,1,0:T(4,128)(2,1)S(1)}, u32[]{:S(2)}, u32[]{:S(2)}) collective-permute-start(bf16[125,4,128]{2,1,0:T(4,128)(2,1)S(1)} %get-tuple-element.49), channel_id=1, source_target_pairs={{4,8},{8,4},{12,16},{16,12},{20,24},{24,20},{5,9},{9,5},{13,17},{1... | collective-permute-start | bytes 384008 | tf_op jit(solution)/shard_map/ppermute | solution.py:563
  40.6 6.9 %collective-permute-start.9 = (bf16[125,2,128]{2,1,0:T(2,128)(2,1)S(1)}, bf16[125,2,128]{2,1,0:T(2,128)(2,1)S(1)}, u32[]{:S(2)}, u32[]{:S(2)}) collective-permute-start(bf16[125,2,128]{2,1,0:T(2,128)(2,1)S(1)} %get-tuple-element.50), channel_id=1, source_target_pairs={{1,2},{2,1},{3,0},{0,3},{5,6},{6,5},{7,4},{4,7},{9,10},{10,9},{11,... | collective-permute-start | bytes 192008 | tf_op jit(solution)/shard_map/ppermute | solution.py:573
  41.2 6.3 %collective-permute-start.10 = (bf16[125,2,128]{2,1,0:T(2,128)(2,1)S(1)}, bf16[125,2,128]{2,1,0:T(2,128)(2,1)S(1)}, u32[]{:S(2)}, u32[]{:S(2)}) collective-permute-start(bf16[125,2,128]{2,1,0:T(2,128)(2,1)S(1)} %get-tuple-element.51), channel_id=1, source_target_pairs={{0,1},{1,0},{2,3},{3,2},{4,5},{5,4},{6,7},{7,6},{8,9},{9,8},{10,11... | collective-permute-start | bytes 192008 | tf_op jit(solution)/shard_map/ppermute | solution.py:573
  42.0 7.3 %collective-permute-start.11 = (bf16[125,4,128]{2,1,0:T(4,128)(2,1)S(1)}, bf16[125,4,128]{2,1,0:T(4,128)(2,1)S(1)}, u32[]{:S(2)}, u32[]{:S(2)}) collective-permute-start(bf16[125,4,128]{2,1,0:T(4,128)(2,1)S(1)} %get-tuple-element.53), channel_id=1, source_target_pairs={{0,4},{4,0},{8,12},{12,8},{16,20},{20,16},{24,28},{28,24},{1,5},{5... | collective-permute-start | bytes 384008 | tf_op jit(solution)/shard_map/ppermute | solution.py:564
  47.9 8.0 %collective-permute-start.12 = (bf16[125,4,128]{2,1,0:T(4,128)(2,1)S(1)}, bf16[125,4,128]{2,1,0:T(4,128)(2,1)S(1)}, u32[]{:S(2)}, u32[]{:S(2)}) collective-permute-start(bf16[125,4,128]{2,1,0:T(4,128)(2,1)S(1)} %get-tuple-element.56), channel_id=1, source_target_pairs={{4,8},{8,4},{12,16},{16,12},{20,24},{24,20},{5,9},{9,5},{13,17},{1... | collective-permute-start | bytes 384008 | tf_op jit(solution)/shard_map/ppermute | solution.py:563
  49.6 6.3 %collective-permute-start.13 = (bf16[125,2,128]{2,1,0:T(2,128)(2,1)S(1)}, bf16[125,2,128]{2,1,0:T(2,128)(2,1)S(1)}, u32[]{:S(2)}, u32[]{:S(2)}) collective-permute-start(bf16[125,2,128]{2,1,0:T(2,128)(2,1)S(1)} %get-tuple-element.57), channel_id=1, source_target_pairs={{1,2},{2,1},{3,0},{0,3},{5,6},{6,5},{7,4},{4,7},{9,10},{10,9},{11,... | collective-permute-start | bytes 192008 | tf_op jit(solution)/shard_map/ppermute | solution.py:573
  50.0 5.9 %collective-permute-start.14 = (bf16[125,2,128]{2,1,0:T(2,128)(2,1)S(1)}, bf16[125,2,128]{2,1,0:T(2,128)(2,1)S(1)}, u32[]{:S(2)}, u32[]{:S(2)}) collective-permute-start(bf16[125,2,128]{2,1,0:T(2,128)(2,1)S(1)} %get-tuple-element.58), channel_id=1, source_target_pairs={{0,1},{1,0},{2,3},{3,2},{4,5},{5,4},{6,7},{7,6},{8,9},{9,8},{10,11... | collective-permute-start | bytes 192008 | tf_op jit(solution)/shard_map/ppermute | solution.py:573
  51.1 6.6 %collective-permute-start.15 = (bf16[125,4,128]{2,1,0:T(4,128)(2,1)S(1)}, bf16[125,4,128]{2,1,0:T(4,128)(2,1)S(1)}, u32[]{:S(2)}, u32[]{:S(2)}) collective-permute-start(bf16[125,4,128]{2,1,0:T(4,128)(2,1)S(1)} %get-tuple-element.61), channel_id=1, source_target_pairs={{0,4},{4,0},{8,12},{12,8},{16,20},{20,16},{24,28},{28,24},{1,5},{5... | collective-permute-start | bytes 384008 | tf_op jit(solution)/shard_map/ppermute | solution.py:564
